TPU v7x, 32 devices: a whole 2x2x4 slice. The times are simulated.
32 devices in a mesh: expert: 8 (over z, x), tensor: 4 (over y, core).
Axes of the slice: x: 2, y: 2, z: 4, core: 2. Of those that a mesh axis runs over, the one named last changes fastest.
Arguments:
- tokens: bfloat16 [4096, 768], P('expert'), may hold values from -6 to 6
- cotangent: bfloat16 [4096, 768], P('expert', 'tensor'), may hold values from -6 to 6
- norm1_gain: float32 [768], replicated, may hold values from 0.5 to 1.5
- w_query: bfloat16 [768, 768], P(None, 'tensor'), may hold values from -0.21875 to 0.21875
- w_key: bfloat16 [768, 768], P(None, 'tensor'), may hold values from -0.21875 to 0.21875
- w_value: bfloat16 [768, 768], P(None, 'tensor'), may hold values from -0.21875 to 0.21875
- w_attn_out: bfloat16 [768, 768], P('tensor'), may hold values from -2.5 to 2.5
- bias_table: float32 [32, 12], P(None, 'tensor'), may hold values from -3 to 3
- norm2_gain: float32 [768], P('tensor'), may hold values from 0.5 to 1.5
- w_router: bfloat16 [768, 8], P('tensor'), may hold values from -0.15625 to 0.15625
- expert_in: bfloat16 [8, 768, 3072], P('expert', None, 'tensor'), may hold values from -0.21875 to 0.21875
- expert_out: bfloat16 [8, 3072, 768], P('expert', 'tensor'), may hold values from -1.25 to 1.25
- route: int32 [4096], P('expert'), may hold values from 0 to 7, as said below
- slot: int32 [4096], P('expert'), may hold values from 0 to 127, as said below
- segment: int32 [4096], P('expert'), may hold values from 0 to 15, never falling along the last dimension, each value on 1 to 512 neighbouring positions
- rel_bucket: int32 [1023], replicated, may hold values from 0 to 31, as said below
Outputs:
- block_out: bfloat16 [4096, 768], P('expert', 'tensor')
- input_grad: float32 [4096, 768], P('expert', 'tensor')
- norm1_gain_grad: float32 [768], replicated
- query_grad: float32 [768, 768], P(None, 'tensor')
- key_grad: float32 [768, 768], P(None, 'tensor')
- value_grad: float32 [768, 768], P(None, 'tensor')
- attn_out_grad: float32 [768, 768], P('tensor')
- table_grad: float32 [32, 12], P(None, 'tensor')
- norm2_gain_grad: float32 [768], P('tensor')
- router_grad: float32 [768, 8], P('tensor')
- expert_in_grad: float32 [8, 768, 3072], P('expert', None, 'tensor')
- expert_out_grad: float32 [8, 3072, 768], P('expert', 'tensor')
Inputs may be any that keep to these rules, and one draw needn't show every extreme that they name: `route`: in each aligned block of 512 rows no expert is named more than 128 times, and one expert, the same in every block, is named exactly 128 times in every block. Within each aligned block of 512 rows no two tokens share both route and slot. `segment`: never falls along the tokens; a document holds 1 to 512 tokens. `rel_bucket`: entry 511 + r belongs to a key r positions after its query; it grows with the distance on each side, offsets after the query take buckets above 16 and offset 0 takes bucket 0.
All inputs are finite; a program needn't handle non-finite values.
Results may differ from a plain program's by a relative error of at most 0.015.
Values may be sent and summed in bfloat16 or wider, within the bound.
No kernel may reach another device: no remote copies, remote signals or barrier semaphores. Data moves between devices by JAX's collectives and lax.ppermute only.
A program may use at most 128 MiB of HBM per device.

v0:
```python
import jax
import jax.numpy as jnp
from jax import lax
from jax.sharding import PartitionSpec as P

D = 768
HDIM = 64
EXP_DEV = 1
SEQ = 512


EPSILON = 1e-06
PRECISE = lax.Precision.HIGHEST
MASKED_SCORE = -1e30
SCORE_SCALE = 0.125


def exact_dot(left, right):
    return jnp.dot(left, right, precision=PRECISE, preferred_element_type=jnp.float32)


def bias_offsets(rel_bucket, bias_table):
    bucket_marks = (
        rel_bucket[:, None] == jnp.arange(bias_table.shape[0], dtype=jnp.int32)[None, :]
    ).astype(jnp.float32)
    return (bucket_marks, exact_dot(bucket_marks, bias_table))


def bias_band(offsets):
    head_count = offsets.shape[1]
    width = offsets.shape[0]
    length = (width + 1) // 2
    padded = jnp.pad(offsets.T, ((0, 0), (0, 1)))
    tiled = jnp.tile(padded, (1, length))
    skewed = tiled[:, length - 1 : length - 1 + length * width]
    return skewed.reshape(head_count, length, width)[:, :, :length]


def split_heads(matrix, seq_count):
    return matrix.reshape(seq_count, SEQ, -1, HDIM)


def block_scores(queries, keys_all, seg_query, seg_keys, bias_rows):
    raw_scores = (
        jnp.einsum("qhd,khd->hqk", queries, keys_all, preferred_element_type=jnp.float32)
        * SCORE_SCALE
    )
    same_doc = (seg_query[:, None] == seg_keys[None, :])[None]
    return jnp.where(same_doc, raw_scores + bias_rows, MASKED_SCORE)


def attend(query_rows, key_rows, value_rows, segment, offsets):
    seq_count = query_rows.shape[0] // SEQ
    band = bias_band(offsets)

    def one_sequence(inputs):
        queries, keys_all, values, seg_ids = inputs
        outputs, levels = ([], [])
        scores = block_scores(queries, keys_all, seg_ids, seg_ids, band)
        row_peak = jnp.max(scores, axis=2, keepdims=True)
        weights = jnp.exp(scores - row_peak)
        totals = jnp.sum(weights, axis=2, keepdims=True)
        weights_low = (weights / totals).astype(jnp.bfloat16)
        mixed_block = jnp.einsum(
            "hqk,khd->qhd", weights_low, values, preferred_element_type=jnp.float32
        )
        outputs.append(mixed_block.astype(jnp.bfloat16))
        levels.append(row_peak[:, :, 0] + jnp.log(totals[:, :, 0]))
        return (jnp.concatenate(outputs, 0), jnp.concatenate(levels, 1))

    mixed_all, log_totals = lax.map(
        one_sequence,
        (
            split_heads(query_rows, seq_count),
            split_heads(key_rows, seq_count),
            split_heads(value_rows, seq_count),
            segment.reshape(seq_count, SEQ),
        ),
    )
    return (mixed_all.reshape(query_rows.shape[0], -1), log_totals)


def diagonal_sums(score_grid):
    head_count, height, key_count = score_grid.shape
    flipped = score_grid[:, ::-1, :]
    padded = jnp.pad(flipped, ((0, 0), (0, 0), (0, height)))
    stretch = key_count + height
    flat_rows = padded.reshape(head_count, height * stretch)[:, : height * (stretch - 1)]
    return jnp.sum(flat_rows.reshape(head_count, height, stretch - 1), axis=1)


def attend_back(query_rows, key_rows, value_rows, segment, offsets, log_totals, d_mixed):
    token_count = query_rows.shape[0]
    seq_count = token_count // SEQ
    block_rows = min(512, SEQ)
    head_count = query_rows.shape[1] // HDIM
    band = bias_band(offsets)

    def one_sequence(inputs):
        queries, keys_all, values, seg_ids, levels, grads_out = inputs
        d_keys = jnp.zeros(keys_all.shape, jnp.float32)
        d_values = jnp.zeros(values.shape, jnp.float32)
        d_offsets = jnp.zeros((head_count, 2 * SEQ - 1), jnp.float32)
        scores = block_scores(queries, keys_all, seg_ids, seg_ids, band)
        weights = jnp.exp(scores - levels[:, 0:block_rows, None])
        d_weights = jnp.einsum(
            "qhd,khd->hqk", grads_out, values, preferred_element_type=jnp.float32
        )
        row_inner = jnp.sum(d_weights * weights, axis=2, keepdims=True)
        d_scores = weights * (d_weights - row_inner)
        lower_edge = SEQ - block_rows
        d_offsets = d_offsets.at[:, lower_edge : lower_edge + SEQ + block_rows - 1].add(
            diagonal_sums(d_scores)
        )
        d_low = d_scores.astype(jnp.bfloat16)
        d_queries = [
            (
                jnp.einsum("hqk,khd->qhd", d_low, keys_all, preferred_element_type=jnp.float32)
                * SCORE_SCALE
            ).astype(jnp.bfloat16)
        ]
        d_keys = d_keys + jnp.einsum(
            "hqk,qhd->khd", d_low, queries, preferred_element_type=jnp.float32
        )
        d_values = d_values + jnp.einsum(
            "hqk,qhd->khd",
            weights.astype(jnp.bfloat16),
            grads_out,
            preferred_element_type=jnp.float32,
        )
        return (
            jnp.concatenate(d_queries, 0),
            (d_keys * SCORE_SCALE).astype(jnp.bfloat16),
            d_values.astype(jnp.bfloat16),
            d_offsets,
        )

    d_query, d_key, d_value, d_offsets = lax.map(
        one_sequence,
        (
            split_heads(query_rows, seq_count),
            split_heads(key_rows, seq_count),
            split_heads(value_rows, seq_count),
            segment.reshape(seq_count, SEQ),
            log_totals,
            split_heads(d_mixed, seq_count),
        ),
    )
    return (
        d_query.reshape(token_count, -1),
        d_key.reshape(token_count, -1),
        d_value.reshape(token_count, -1),
        jnp.sum(d_offsets, axis=0),
    )


def row_totals(first_term, second_term):
    return lax.psum((first_term, second_term), "tensor")


def to_experts(rows_low, route, slot):
    expert_count = lax.axis_size("expert") * EXP_DEV
    capacity = 2 * rows_low.shape[0] // expert_count
    whole_rows = lax.all_gather(rows_low, "tensor", axis=1, tiled=True)
    buffer = (
        jnp.zeros((expert_count, capacity, whole_rows.shape[1]), jnp.bfloat16)
        .at[route, slot]
        .set(whole_rows)
    )
    arrived = lax.all_to_all(buffer, "expert", split_axis=0, concat_axis=0, tiled=True)
    sources = arrived.shape[0] // EXP_DEV
    arrived = arrived.reshape(sources, EXP_DEV, capacity, -1)
    return jnp.transpose(arrived, (1, 0, 2, 3)).reshape(EXP_DEV, sources * capacity, -1)


def from_experts(partial_rows, route, slot):
    sources = lax.axis_size("expert")
    capacity = partial_rows.shape[1] // sources
    sectioned = partial_rows.reshape(EXP_DEV, sources, capacity, -1)
    came_back = lax.all_to_all(
        jnp.transpose(sectioned, (1, 0, 2, 3)).reshape(sources * EXP_DEV, capacity, -1),
        "expert",
        split_axis=0,
        concat_axis=0,
        tiled=True,
    )
    picked = came_back[route, slot]
    return lax.psum_scatter(picked, "tensor", scatter_dimension=1, tiled=True).astype(jnp.bfloat16)


def on_device(
    tokens,
    cotangent,
    norm1_gain,
    w_query,
    w_key,
    w_value,
    w_attn_out,
    bias_table,
    norm2_gain,
    w_router,
    expert_in,
    expert_out,
    route,
    slot,
    segment,
    rel_bucket,
):
    col_count = cotangent.shape[1]
    col_start = lax.axis_index("tensor") * col_count
    inputs32 = tokens.astype(jnp.float32)
    input_cols = lax.dynamic_slice_in_dim(inputs32, col_start, col_count, 1)
    scale_one = lax.rsqrt(jnp.mean(inputs32 * inputs32, axis=1, keepdims=True) + EPSILON)
    normed_one = (inputs32 * scale_one * norm1_gain).astype(jnp.bfloat16)
    query_rows = jnp.dot(normed_one, w_query, preferred_element_type=jnp.float32).astype(
        jnp.bfloat16
    )
    key_rows = jnp.dot(normed_one, w_key, preferred_element_type=jnp.float32).astype(jnp.bfloat16)
    value_rows = jnp.dot(normed_one, w_value, preferred_element_type=jnp.float32).astype(
        jnp.bfloat16
    )
    bucket_marks, offsets = bias_offsets(rel_bucket, bias_table)
    mixed, log_totals = attend(query_rows, key_rows, value_rows, segment, offsets)
    attn_part = jnp.dot(mixed, w_attn_out, preferred_element_type=jnp.float32)
    residual = input_cols + lax.psum_scatter(attn_part, "tensor", scatter_dimension=1, tiled=True)
    gained = residual * norm2_gain
    router_w32 = w_router.astype(jnp.float32)
    square_sum, logit_base = row_totals(
        jnp.sum(residual * residual, axis=1), exact_dot(gained, router_w32)
    )
    scale_two = lax.rsqrt(square_sum / D + EPSILON)[:, None]
    normed_two = residual * scale_two * norm2_gain
    logits = scale_two * logit_base
    shifted = jnp.exp(logits - jnp.max(logits, axis=1, keepdims=True))
    router_probs = shifted / jnp.sum(shifted, axis=1, keepdims=True)
    route_marks = (route[:, None] == jnp.arange(logits.shape[1], dtype=jnp.int32)[None, :]).astype(
        jnp.float32
    )
    gate_value = jnp.sum(router_probs * route_marks, axis=1)
    expert_rows = to_experts(normed_two.astype(jnp.bfloat16), route, slot)
    hidden = jnp.einsum("erd,edf->erf", expert_rows, expert_in, preferred_element_type=jnp.float32)
    act_low = jax.nn.gelu(hidden).astype(jnp.bfloat16)
    expert_part = jnp.einsum(
        "erf,efd->erd", act_low, expert_out, preferred_element_type=jnp.float32
    )
    returned = from_experts(expert_part, route, slot).astype(jnp.float32)
    block_out = (residual + gate_value[:, None] * returned).astype(jnp.bfloat16)
    grad_cols = cotangent.astype(jnp.float32)
    gate_part = jnp.sum(grad_cols * returned, axis=1)
    grad_rows = to_experts((gate_value[:, None] * grad_cols).astype(jnp.bfloat16), route, slot)
    d_act = jnp.einsum("erd,efd->erf", grad_rows, expert_out, preferred_element_type=jnp.float32)
    expert_out_grad = jnp.einsum(
        "erf,erd->efd", act_low, grad_rows, preferred_element_type=jnp.float32
    )
    gelu_pull = jax.vjp(jax.nn.gelu, hidden)[1]
    d_hidden = gelu_pull(d_act)[0].astype(jnp.bfloat16)
    expert_in_grad = jnp.einsum(
        "erd,erf->edf", expert_rows, d_hidden, preferred_element_type=jnp.float32
    )
    d_part = jnp.einsum("erf,edf->erd", d_hidden, expert_in, preferred_element_type=jnp.float32)
    d_routed = from_experts(d_part, route, slot).astype(jnp.float32)
    d_gate, cross_part = row_totals(gate_part, jnp.sum(gained * d_routed, axis=1))
    d_logits = d_gate[:, None] * router_probs * (route_marks - gate_value[:, None])
    router_grad = exact_dot(normed_two.T, d_logits)
    d_normed_two = d_routed + exact_dot(d_logits, router_w32.T)
    cross_two = cross_part + jnp.sum(d_logits * logit_base, axis=1)
    norm2_gain_grad = jnp.sum(d_normed_two * residual * scale_two, axis=0)
    d_residual = (
        grad_cols
        + scale_two * norm2_gain * d_normed_two
        - residual * scale_two**3 * cross_two[:, None] / D
    )
    attn_full = lax.all_gather(d_residual.astype(jnp.bfloat16), "tensor", axis=1, tiled=True)
    attn_out_grad = jnp.einsum("tc,td->cd", mixed, attn_full, preferred_element_type=jnp.float32)
    d_mixed = jnp.einsum(
        "td,cd->tc", attn_full, w_attn_out, preferred_element_type=jnp.float32
    ).astype(jnp.bfloat16)
    d_query, d_key, d_value, d_offsets = attend_back(
        query_rows, key_rows, value_rows, segment, offsets, log_totals, d_mixed
    )
    table_grad = exact_dot(bucket_marks.T, d_offsets.T)
    query_grad = jnp.einsum("td,tc->dc", normed_one, d_query, preferred_element_type=jnp.float32)
    key_grad = jnp.einsum("td,tc->dc", normed_one, d_key, preferred_element_type=jnp.float32)
    value_grad = jnp.einsum("td,tc->dc", normed_one, d_value, preferred_element_type=jnp.float32)
    d_normed_part = jnp.einsum("tc,dc->td", d_query, w_query, preferred_element_type=jnp.float32)
    d_normed_part = d_normed_part + jnp.einsum(
        "tc,dc->td", d_key, w_key, preferred_element_type=jnp.float32
    )
    d_normed_part = d_normed_part + jnp.einsum(
        "tc,dc->td", d_value, w_value, preferred_element_type=jnp.float32
    )
    d_normed_one = lax.psum(d_normed_part, "tensor")
    cross_one = jnp.sum(norm1_gain * inputs32 * d_normed_one, axis=1, keepdims=True)
    d_inputs = scale_one * norm1_gain * d_normed_one - inputs32 * scale_one**3 * cross_one / D
    input_grad = d_residual + lax.dynamic_slice_in_dim(d_inputs, col_start, col_count, 1)
    gain_piece = jnp.sum(d_normed_one * inputs32 * scale_one, axis=0)
    summed = lax.psum(
        (
            query_grad,
            key_grad,
            value_grad,
            attn_out_grad,
            table_grad,
            router_grad,
            gain_piece,
            norm2_gain_grad,
        ),
        "expert",
    )
    norm1_gain_grad = summed[6]
    return (
        block_out,
        input_grad,
        norm1_gain_grad,
        summed[0],
        summed[1],
        summed[2],
        summed[3],
        summed[4],
        summed[7],
        summed[5],
        expert_in_grad,
        expert_out_grad,
    )


def solution(mesh):
    return jax.shard_map(
        on_device,
        mesh=mesh,
        in_specs=(
            P("expert", None),
            P("expert", "tensor"),
            P(),
            P(None, "tensor"),
            P(None, "tensor"),
            P(None, "tensor"),
            P("tensor", None),
            P(None, "tensor"),
            P("tensor"),
            P("tensor", None),
            P("expert", None, "tensor"),
            P("expert", "tensor", None),
            P("expert"),
            P("expert"),
            P("expert"),
            P(),
        ),
        out_specs=(
            P("expert", "tensor"),
            P("expert", "tensor"),
            P(),
            P(None, "tensor"),
            P(None, "tensor"),
            P(None, "tensor"),
            P("tensor", None),
            P(None, "tensor"),
            P("tensor"),
            P("tensor", None),
            P("expert", None, "tensor"),
            P("expert", "tensor", None),
        ),
        check_vma=False,
    )
```

profile of v0, /device:TPU:0, one launch (start us, length us, event | category | flops | bytes accessed | tf_op | source)
XLA Modules:
  0.0 733.3 jit_solution(6065779419443352207)
XLA Ops:
  7.3 1.0 broadcast_compare_fusion
  8.3 1.4 copy.38
  10.0 1.1 convolution_convert_fusion.2
  11.1 1.1 convolution_convert_fusion.3
  12.2 1.1 convolution_convert_fusion.1
  13.7 3.4 broadcast_bitcast_fusion
  17.2 7.1 copy.61
  24.3 6.3 slice.37
  30.6 13.2 %reshape.225 = f32[3,512,1023]{2,1,0:T(8,128)} reshape(f32[3,523776]{1,0:T(4,128)} %slice.37) | data formatting | bytes 12570624 | tf_op jit(solution)/shard_map/reshape | solution.py:36
  43.8 3.8 slice.38
  47.7 3.6 copy.59
  51.3 2.8 fusion.64
  54.5 1.2 copy-done.2
  57.0 1.6 fusion.65
  58.7 1.4 convert_element_type.104
  60.2 29.5 %reduce-scatter.4.cloned.1.call-done = f32[512,192]{0,1:T(8,128)} async-done(((f32[512,768]{0,1:T(8,128)}), f32[512,192]{0,1:T(8,128)}) %reduce-scatter.4.cloned.1.call-update) | async-done | bytes 393232 | tf_op jit(solution)/shard_map/reduce_scatter | solution.py:225
  89.7 1.2 multiply_reduce_fusion.5
  90.9 5.8 psum.91
  96.7 8.8 %all_gather.9 = bf16[512,768]{0,1:T(8,128)(2,1)S(1)} all-gather(bf16[512,192]{0,1:T(8,128)(2,1)S(1)} %fusion.43), channel_id=1, replica_groups=mesh['expert'=8,'tensor'=4] {'tensor'}, dimensions={1}, use_global_device_ids=true | all-gather | bytes 983040 | tf_op jit(solution)/shard_map/all_gather | solution.py:164
  105.5 1.2 copy.41
  106.8 46.5 %scatter_fusion = bf16[8,128,768]{2,1,0:T(8,128)(2,1)S(1)} fusion(bf16[8,128,768]{2,1,0:T(8,128)(2,1)S(1)} %broadcast.136.clone, s32[512]{0:T(512)S(1)} %bitcast.94, bf16[512,768]{1,0:T(8,128)(2,1)} %copy.41), kind=kCustom, calls=%fused_computation.2 | custom fusion | bytes 2363392 | tf_op jit(solution)/shard_map/scatter | solution.py:168
  153.3 42.8 %all_to_all.20 = bf16[8,128,768]{2,1,0:T(8,128)(2,1)S(1)} all-to-all(bf16[8,128,768]{2,1,0:T(8,128)(2,1)S(1)} %scatter_fusion), channel_id=1, replica_groups=mesh['expert'=8,'tensor'=4] {'expert'}, dimensions={0} | all-to-all | bytes 3145728 | tf_op jit(solution)/shard_map/all_to_all | solution.py:170
  196.1 3.4 multiply_convert_fusion
  199.5 1.4 fusion.15
  200.9 74.3 %all_to_all.21 = f32[8,128,768]{2,1,0:T(8,128)} all-to-all(f32[8,128,768]{2,1,0:T(8,128)S(1)} %fusion.15), channel_id=1, replica_groups=mesh['expert'=8,'tensor'=4] {'expert'}, dimensions={0} | all-to-all | bytes 6291456 | tf_op jit(solution)/shard_map/all_to_all | solution.py:180
  275.2 7.1 gather_fusion
  282.3 1.6 copy.42
  284.9 25.5 %reduce-scatter.6.cloned.1.call-done = f32[512,192]{0,1:T(8,128)} async-done(((f32[512,768]{0,1:T(8,128)}), f32[512,192]{0,1:T(8,128)}) %reduce-scatter.6.cloned.1.call-update) | async-done | bytes 393232 | tf_op jit(solution)/shard_map/reduce_scatter | solution.py:188
  310.4 1.1 fusion.36
  311.5 10.2 %all-reduce.4 = (f32[512,8]{0,1:T(8,128)S(1)}, f32[512]{0:T(512)S(1)}) all-reduce(f32[512,8]{0,1:T(8,128)S(1)} %fusion.40, f32[512]{0:T(512)S(1)} %fusion.36), channel_id=1, replica_groups=mesh['expert'=8,'tensor'=4] {'tensor'}, use_global_device_ids=true, to_apply=%region_6.7 | all-reduce | flops 4608 | bytes 36864 | tf_op jit(solution)/shard_map/psum | solution.py:158
  321.8 8.8 %all_gather.10 = bf16[512,768]{0,1:T(8,128)(2,1)S(1)} all-gather(bf16[512,192]{0,1:T(8,128)(2,1)S(1)} %fusion.35), channel_id=1, replica_groups=mesh['expert'=8,'tensor'=4] {'tensor'}, dimensions={1}, use_global_device_ids=true | all-gather | bytes 983040 | tf_op jit(solution)/shard_map/all_gather | solution.py:164
  330.6 1.2 copy.43
  331.8 46.5 %scatter_fusion.1 = bf16[8,128,768]{2,1,0:T(8,128)(2,1)S(1)} fusion(bf16[8,128,768]{2,1,0:T(8,128)(2,1)S(1)} %broadcast.136, s32[512]{0:T(512)S(1)} %bitcast.95, bf16[512,768]{1,0:T(8,128)(2,1)} %copy.43), kind=kCustom, calls=%fused_computation.3 | custom fusion | bytes 2363392 | tf_op jit(solution)/shard_map/scatter | solution.py:168
  378.4 42.9 %all_to_all.22 = bf16[8,128,768]{2,1,0:T(8,128)(2,1)S(1)} all-to-all(bf16[8,128,768]{2,1,0:T(8,128)(2,1)S(1)} %scatter_fusion.1), channel_id=1, replica_groups=mesh['expert'=8,'tensor'=4] {'expert'}, dimensions={0} | all-to-all | bytes 3145728 | tf_op jit(solution)/shard_map/all_to_all | solution.py:170
  421.3 5.4 fusion.6
  426.7 1.4 fusion.13
  428.2 74.3 %all_to_all.23 = f32[8,128,768]{2,1,0:T(8,128)} all-to-all(f32[8,128,768]{2,1,0:T(8,128)S(1)} %fusion.13), channel_id=1, replica_groups=mesh['expert'=8,'tensor'=4] {'expert'}, dimensions={0} | all-to-all | bytes 6291456 | tf_op jit(solution)/shard_map/all_to_all | solution.py:180
  502.5 7.1 gather_fusion.1
  509.6 1.6 copy.44
  511.4 26.3 %reduce-scatter.8.cloned.1.call-done = f32[512,192]{0,1:T(8,128)} async-done(((f32[512,768]{0,1:T(8,128)}), f32[512,192]{0,1:T(8,128)}) %reduce-scatter.8.cloned.1.call-update) | async-done | bytes 393232 | tf_op jit(solution)/shard_map/reduce_scatter | solution.py:188
  537.7 1.5 multiply_reduce_fusion.4
  539.2 5.9 psum.94
  545.3 8.9 %all_gather.11 = bf16[512,768]{0,1:T(8,128)(2,1)S(1)} all-gather(bf16[512,192]{0,1:T(8,128)(2,1)S(1)} %fusion.60), channel_id=1, replica_groups=mesh['expert'=8,'tensor'=4] {'tensor'}, dimensions={1}, use_global_device_ids=true | all-gather | bytes 983040 | tf_op jit(solution)/shard_map/all_gather | solution.py:273
  557.8 1.0 copy-done.4
  560.0 1.3 fusion.61
  562.2 1.6 add_add_fusion
  564.8 1.2 fusion.68
  566.0 1.3 fusion.63
  567.3 1.3 fusion.62
  569.2 1.0 copy-done.16
  570.2 4.4 convolution_bitcast_fusion
  574.6 2.8 convolution_bitcast_fusion.1
  577.5 26.1 %rev.4 = f32[3,512,512]{1,2,0:T(8,128)} reverse(f32[3,512,512]{1,2,0:T(8,128)} %copy-done.4), dimensions={1} | reverse | bytes 6291456 | tf_op jit(solution)/shard_map/while/body/eval_jaxpr/rev | solution.py:85
  603.6 3.6 copy.60
  607.1 5.4 pad_bitcast_fusion
  612.5 7.1 copy.62
  619.6 4.2 slice.39
  623.8 13.3 %reshape.235 = f32[3,512,1023]{2,1,0:T(8,128)} reshape(f32[3,523776]{1,0:T(4,128)} %slice.39) | data formatting | bytes 12570624 | tf_op jit(solution)/shard_map/while/body/eval_jaxpr/reshape | solution.py:89
  637.1 3.2 reduce_sum.135
  640.8 2.0 multiply_reduce_fusion.1
  642.8 38.0 %all-reduce.2 = (f32[768]{0:T(1024)}, f32[32,3]{0,1:T(4,128)}, f32[192]{0:T(256)}, f32[192,8]{0,1:T(8,128)}) all-reduce(f32[768]{0:T(1024)S(1)} %get-tuple-element.97, f32[32,3]{0,1:T(4,128)S(1)} %fusion.31, f32[192]{0:T(256)S(1)} %get-tuple-element.99, f32[192,8]{0,1:T(8,128)S(1)} %fusion.42), channel_id=1, replica_groups=mesh['expert'=8,'tensor'=4] {'expert'}, use_global_device_ids=true, to_apply=%region_23.24 | all-reduce | flops 2592 | bytes 20736 | tf_op jit(solution)/shard_map/psum | solution.py:297
  680.8 2.2 fusion.39
  683.0 39.0 %all-reduce.10.cloned.1.call-done = (f32[768,192]{0,1:T(8,128)}, f32[768,192]{0,1:T(8,128)}, f32[768,192]{0,1:T(8,128)}, f32[192,768]{1,0:T(8,128)}) async-done(((f32[768,192]{0,1:T(8,128)}, f32[768,192]{0,1:T(8,128)}, f32[768,192]{0,1:T(8,128)}, f32[192,768]{1,0:T(8,128)}), (f32[768,192]{0,1:T(8,128)}, f32[768,192]{0,1:T(8,128)}, f32[768,192]{0,1:T(8,128)}, ...) | async-done | bytes 2359312 | tf_op jit(solution)/shard_map/psum | solution.py:297
  722.0 2.1 copy.70
  (142 shorter events, 14.3 us)
Async XLA Ops:
  7.2 188.9 %copy-start = (bf16[1,768,768]{2,1,0:T(8,128)(2,1)S(1)}, bf16[1,768,768]{2,1,0:T(8,128)(2,1)}, u32[]{:S(2)}) copy-start(bf16[1,768,768]{2,1,0:T(8,128)(2,1)} %param.30) | copy-start | bytes 3538948
  7.2 2.8 copy-start.40
  7.2 2.7 copy-start.33
  7.2 82.4 %reduce-scatter.4.cloned.1.call-start = ((), (), s32[]{:S(2)}) async-start(), calls=%async_computation.7 | async-start | bytes 1966080 | tf_op jit(solution)/shard_map/reduce_scatter | solution.py:225
  9.7 2.5 copy-start.7
  9.7 1.4 copy-start.29
  10.0 2.2 copy-start.31
  11.1 2.2 copy-start.44
  11.1 2.2 copy-start.45
  47.7 3.6 copy-start.20
  47.7 3.6 copy-start.22
  54.0 1.7 copy-start.2
  54.0 1.6 copy-start.35
  55.7 1.4 copy-start.18
  56.4 0.7 copy-start.24
  57.0 1.7 copy-start.8
  58.6 1.5 copy-start.41
  58.6 1.5 copy-start.37
  58.7 251.7 %reduce-scatter.6.cloned.1.call-start = ((), (), s32[]{:S(2)}) async-start(), calls=%async_computation.8 | async-start | bytes 1966080 | tf_op jit(solution)/shard_map/reduce_scatter | solution.py:188
  58.7 37.9 %copy-start.38 = (f32[192]{0:T(256)S(1)}, f32[192]{0:T(256)}, u32[]{:S(2)}) copy-start(f32[192]{0:T(256)} %param.28) | copy-start | bytes 2308
  90.9 477.9 %copy-start.5 = (f32[512,192]{0,1:T(8,128)}, f32[512,192]{0,1:T(8,128)S(1)}, u32[]{:S(2)}) copy-start(f32[512,192]{0,1:T(8,128)S(1)} %get-tuple-element.112) | copy-start | bytes 1179652
  196.1 3.4 copy-start.13
  196.1 3.4 copy-start.42
  199.5 1.4 copy-start.46
  283.9 0.7 copy-start.39
  283.9 26.5 %copy-start.12 = (bf16[512,192]{0,1:T(8,128)(2,1)S(1)}, bf16[512,192]{0,1:T(8,128)(2,1)}, u32[]{:S(2)}) copy-start(bf16[512,192]{0,1:T(8,128)(2,1)} %param.21) | copy-start | bytes 589828
  283.9 253.8 %reduce-scatter.8.cloned.1.call-start = ((), (), s32[]{:S(2)}) async-start(), calls=%async_computation.9 | async-start | bytes 1966080 | tf_op jit(solution)/shard_map/reduce_scatter | solution.py:188
  378.4 42.9 %copy-start.43 = (bf16[1,768,768]{2,1,0:T(8,128)(2,1)S(1)}, bf16[1,768,768]{2,1,0:T(8,128)(2,1)}, u32[]{:S(2)}) copy-start(bf16[1,768,768]{2,1,0:T(8,128)(2,1)} %param.31) | copy-start | bytes 3538948
  421.3 5.4 copy-start.15
  426.7 1.4 copy-start.47
  511.3 129.5 %all-reduce.8.cloned.1.call-start = ((), (), s32[]{:S(2)}) async-start(), calls=%async_computation.10 | async-start | bytes 3145728 | tf_op jit(solution)/shard_map/psum | solution.py:292
  511.4 42.9 %copy-start.19 = (bf16[192,768]{1,0:T(8,128)(2,1)S(1)}, bf16[192,768]{1,0:T(8,128)(2,1)}, u32[]{:S(2)}) copy-start(bf16[192,768]{1,0:T(8,128)(2,1)} %param.26) | copy-start | bytes 884740
  539.2 15.3 %copy-start.10 = (f32[512,192]{0,1:T(8,128)}, f32[512,192]{0,1:T(8,128)S(1)}, u32[]{:S(2)}) copy-start(f32[512,192]{0,1:T(8,128)S(1)} %get-tuple-element.125) | copy-start | bytes 1179652
  545.2 9.4 %copy-start.3 = (f32[3,512,512]{1,2,0:T(8,128)S(1)}, f32[3,512,512]{1,2,0:T(8,128)}, u32[]{:S(2)}) copy-start(f32[3,512,512]{1,2,0:T(8,128)} %copy-done.2) | copy-start | bytes 9437188
  554.6 0.9 copy-start.36
  556.2 0.9 copy-start.21
  557.2 1.7 copy-start.4
  557.2 1.7 copy-start.23
  558.8 1.1 copy-start.9
  559.2 2.1 copy-start.32
  559.9 1.7 copy-start.34
  561.3 1.0 copy-start.30
  563.8 0.9 copy-start.25
  563.9 158.1 %all-reduce.10.cloned.1.call-start = ((), (), s32[]{:S(2)}) async-start(), calls=%async_computation.11 | async-start | bytes 4718592 | tf_op jit(solution)/shard_map/psum | solution.py:297
  568.6 1.6 copy-start.16
  570.2 4.4 copy-start.14
  570.2 4.4 copy-start.48
  640.3 40.4 %copy-start.6 = (f32[512,192]{0,1:T(8,128)S(1)}, f32[512,192]{0,1:T(8,128)}, u32[]{:S(2)}) copy-start(f32[512,192]{0,1:T(8,128)} %copy-done.5) | copy-start | bytes 1179652
  640.4 40.4 %copy-start.11 = (f32[512,192]{0,1:T(8,128)S(1)}, f32[512,192]{0,1:T(8,128)}, u32[]{:S(2)}) copy-start(f32[512,192]{0,1:T(8,128)} %copy-done.10) | copy-start | bytes 1179652
  640.4 40.4 %copy-start.17 = (f32[512,192]{0,1:T(8,128)S(1)}, f32[512,192]{0,1:T(8,128)}, u32[]{:S(2)}) copy-start(f32[512,192]{0,1:T(8,128)} %reduce-scatter.6.cloned.1.call-done) | copy-start | bytes 1179652
  722.0 2.1 copy-start.28
  722.0 2.9 copy-start.27
  722.0 3.7 copy-start.26
  722.0 4.5 copy-start.1
Sparse Core Ops, SparseCore 0:
  58.8 30.8 reduce-scatter.3
  284.1 26.2 reduce-scatter.5
  511.4 26.2 reduce-scatter.7
  564.0 42.8 all-reduce.7
  611.8 110.1 all-reduce.9
where the time goes:
time: 746 us; the launch traced here: 733 us
  blocking collectives  321 us (43%)
  local copies, waits for them, and re-layouts  223 us (30%)
  waiting for transfers between devices  120 us (16%)
  matrix products  40.6 us (5%)
  between operations  14.5 us (2%)
  other arithmetic  14 us (2%)
    all_to_all x2, blocking collectives, from_experts(): lax.all_to_all(jnp.transpose(sectioned, (1, 0, 2, 3)).reshape(sources * E...  149 us
    scatter x2, local copies, waits for them, and re-layouts, to_experts(): buffer = jnp.zeros((expert_count, capacity, whole_rows.shape[1]), jnp.bfl...  93 us
    all_to_all x2, blocking collectives, to_experts(): lax.all_to_all(buffer, 'expert', split_axis=0, concat_axis=0, tiled=True)  85.7 us
    reduce_scatter x2, waiting for transfers between devices, from_experts(): lax.psum_scatter(picked, 'tensor', scatter_dimension=1, tiled=True)  51.8 us
    unnamed x109, local copies, waits for them, and re-layouts  42.9 us
    psum x1, waiting for transfers between devices, on_device(): lax.psum((query_grad, key_grad, value_grad, attn_out_grad, table_grad, ro...  39 us
    psum x1, blocking collectives, on_device(): lax.psum((query_grad, key_grad, value_grad, attn_out_grad, table_grad, ro...  38 us
    reduce_scatter x1, waiting for transfers between devices, on_device(): lax.psum_scatter(attn_part, 'tensor', scatter_dimension=1, tiled=True)  29.5 us
  transfers between devices with their start and end apart: 5, of which 4 were waited for; matrix products, arithmetic and copies ran while one was open for 11% of the time, Pallas kernels for 0%

commit v1 on v0

v1 whole, which is shorter than its diff:
```python
import functools

import jax
import jax.numpy as jnp
from jax import lax
from jax.experimental import pallas as pl
from jax.experimental.pallas import tpu as pltpu
from jax.sharding import PartitionSpec as P

HDIM = 64
EPSILON = 1e-06
MASKED_SCORE = -1e30
SCORE_SCALE = 0.125
PRECISE = lax.Precision.HIGHEST
F32 = jnp.float32
BF16 = jnp.bfloat16
GELU_C = 0.7978845608028654
GELU_A = 0.044715
CHUNK = 128


def dot_nn(a, b, precision=None):
    return lax.dot_general(
        a, b, (((1,), (0,)), ((), ())), precision=precision, preferred_element_type=F32
    )


def dot_nt(a, b, precision=None):
    return lax.dot_general(
        a, b, (((1,), (1,)), ((), ())), precision=precision, preferred_element_type=F32
    )


def dot_tn(a, b, precision=None):
    return lax.dot_general(
        a, b, (((0,), (0,)), ((), ())), precision=precision, preferred_element_type=F32
    )


def row_scale(rows):
    return lax.rsqrt(jnp.mean(rows * rows, axis=1, keepdims=True) + EPSILON)


def bucket_marks(bucket_ref, count):
    width = bucket_ref.shape[1]
    return lax.broadcasted_iota(jnp.int32, (count, width), 0) == bucket_ref[...]


def in_order(blocks, place):
    stack = place
    for j, (block, where) in enumerate(blocks):
        stack[where] = block[...]
    return jnp.concatenate([stack[r] for r in range(len(blocks))], axis=1)


def attend_kernel(
    tokens, gain, w_query, w_key, w_value, seg_col, seg_row, bucket, table,
    normed_out, query_out, key_out, value_out, probs_out, mixed_out, band,
):
    length = tokens.shape[0]
    width = 2 * length
    heads = query_out.shape[1] // HDIM
    rows = tokens[...].astype(F32)
    normed = (rows * row_scale(rows) * gain[...]).astype(BF16)
    normed_out[...] = normed
    query = dot_nn(normed, w_query[...]).astype(BF16)
    key = dot_nn(normed, w_key[...]).astype(BF16)
    value = dot_nn(normed, w_value[...]).astype(BF16)
    query_out[...] = query
    key_out[...] = key
    value_out[...] = value
    marks = bucket_marks(bucket, table.shape[0])
    for h in range(heads):
        cols = slice(h * HDIM, (h + 1) * HDIM)
        offsets = jnp.sum(
            jnp.where(marks, table[:, h : h + 1], 0.0), axis=0, keepdims=True
        )
        base = jnp.concatenate(
            [offsets] + [pltpu.roll(offsets, r, 1) for r in range(1, 8)], axis=0
        )
        for b in range(length // 8):
            turned = pltpu.roll(base, (length + 1 + 8 * b) % width, 1)
            band[8 * b : 8 * b + 8, :] = turned[:, :length]
        for c in range(0, length, CHUNK):
            span = slice(c, c + CHUNK)
            scores = dot_nt(query[span, cols], key[:, cols]) * SCORE_SCALE + band[span, :]
            scores = jnp.where(seg_col[span, :] == seg_row[...], scores, MASKED_SCORE)
            weights = jnp.exp(scores - jnp.max(scores, axis=1, keepdims=True))
            probs = weights / jnp.sum(weights, axis=1, keepdims=True)
            probs_out[h, span, :] = probs
            mixed_out[span, cols] = dot_nn(probs.astype(BF16), value[:, cols]).astype(BF16)


def cotangent_kernel(meta, code, c0, c1, c2, c3, *rest):
    outs, place = rest[:-1], rest[-1]
    rank = meta[0]
    full = in_order([(c, rank ^ j) for j, c in enumerate((c0, c1, c2, c3))], place)
    outs[0][...] = full
    dispatch(code, full, outs[1:])


def dispatch(code, rows, outs):
    share = outs[0].shape[0]
    for k, out in enumerate(outs):
        ids = lax.broadcasted_iota(jnp.int32, (share, code.shape[1]), 0) + k * share
        marks = jnp.where(ids == code[...], 1.0, 0.0).astype(BF16)
        out[...] = dot_nn(marks, rows).astype(BF16)


def residual_kernel(
    meta, code, route_col, m0, m1, m2, m3, w0, w1, w2, w3, p0, p1, p2, p3, tokens,
    residual_out, gate_out, probs_out, params_out, *rest,
):
    outs, place = rest[:-1], rest[-1]
    rank = meta[0]
    experts = probs_out.shape[1]
    params = in_order([(p, rank ^ j) for j, p in enumerate((p0, p1, p2, p3))], place)
    params_out[...] = params
    router = params[:experts]
    gain = params[experts : experts + 1]
    residual = tokens[...].astype(F32)
    for m, w in ((m0, w0), (m1, w1), (m2, w2), (m3, w3)):
        residual = residual + dot_nn(m[...], w[...])
    residual_out[...] = residual
    normed = residual * row_scale(residual) * gain
    logits = dot_nt(normed, router, PRECISE)
    shifted = jnp.exp(logits - jnp.max(logits, axis=1, keepdims=True))
    probs = shifted / jnp.sum(shifted, axis=1, keepdims=True)
    probs_out[...] = probs
    lanes = lax.broadcasted_iota(jnp.int32, probs.shape, 1)
    gate_out[...] = jnp.sum(jnp.where(lanes == route_col[...], probs, 0.0), axis=1, keepdims=True)
    dispatch(code, normed.astype(BF16), outs)


def expert_kernel(
    meta, x0, x1, x2, x3, c0, c1, c2, c3, w_in, w_out, router,
    rows_out, act_out, cots_out, d_hidden_out, keep_out, send_out,
    x_all, c_all, part_all, *, direct,
):
    rank, expert = meta[0], meta[1]
    ranks = 4
    total = rows_out.shape[0]
    feats = rows_out.shape[1]
    cols = feats // ranks
    if direct:
        sources, _, share, _ = x_all.shape
        for j, (x, c) in enumerate(((x0, c0), (x1, c1), (x2, c2), (x3, c3))):
            for s in range(sources):
                x_all[s, rank ^ j] = x[s * share : (s + 1) * share, :]
                c_all[s, rank ^ j] = c[s * share : (s + 1) * share, :]
        step = 256 // (ranks * share)
    else:
        step = 0

    def chunk(i, carry):
        span = pl.ds(pl.multiple_of(i * 256, 256), 256)
        if direct:
            rows = x_all[pl.ds(i * step, step)].reshape(256, feats)
            cots = c_all[pl.ds(i * step, step)].reshape(256, feats)
        else:
            rows = x0[span, :]
            cots = c0[span, :]
        rows_out[span, :] = rows
        logits = dot_nt(rows, router[...].astype(BF16))
        shifted = jnp.exp(logits - jnp.max(logits, axis=1, keepdims=True))
        lanes = lax.broadcasted_iota(jnp.int32, logits.shape, 1)
        gate = jnp.sum(jnp.where(lanes == expert, shifted, 0.0), axis=1, keepdims=True) / jnp.sum(
            shifted, axis=1, keepdims=True
        )
        cots = (gate * cots.astype(F32)).astype(BF16)
        cots_out[span, :] = cots
        hidden = dot_nn(rows, w_in[...])
        bent = jnp.tanh(GELU_C * (hidden + GELU_A * hidden * hidden * hidden))
        act = (0.5 * hidden * (1.0 + bent)).astype(BF16)
        act_out[span, :] = act
        slope = 0.5 * (1.0 + bent) + 0.5 * hidden * (1.0 - bent * bent) * (
            GELU_C * (1.0 + 3.0 * GELU_A * hidden * hidden)
        )
        d_hidden = (dot_nt(cots, w_out[...]) * slope).astype(BF16)
        d_hidden_out[span, :] = d_hidden
        part = dot_nn(act, w_out[...]).astype(BF16)
        d_part = dot_nt(d_hidden, w_in[...]).astype(BF16)
        for r in range(ranks):
            j = rank ^ r
            place = (j % 2) * 2 + j // 2
            own = slice(r * cols, (r + 1) * cols)
            part_all[place] = jnp.concatenate([part[:, own], d_part[:, own]], axis=1)
        keep_out[:, span, :] = part_all[0:2]
        send_out[:, span, :] = part_all[2:4]
        return carry

    lax.fori_loop(0, total // 256, chunk, 0)


def combine_kernel(meta, code_col, residual, gate, cotangent, *rest):
    *blocks, block_out, packed_out, came, place = rest
    rank = meta[0]
    cap = blocks[0].shape[0]
    cols = cotangent.shape[1]
    for k, block in enumerate(blocks):
        came[k * cap : (k + 1) * cap, :] = block[...]
    ids = lax.broadcasted_iota(jnp.int32, (code_col.shape[0], came.shape[0]), 1)
    marks = jnp.where(ids == code_col[...], 1.0, 0.0).astype(BF16)
    both = dot_nn(marks, came[...])
    returned = both[:, :cols]
    for r in range(4):
        place[r] = residual[:, r * cols : (r + 1) * cols]
    block_out[...] = (place[rank] + gate[...] * returned).astype(BF16)
    total = jnp.sum(cotangent[...].astype(F32) * returned, axis=1, keepdims=True)
    high = total.astype(BF16).astype(F32)
    low = total - high
    tail = packed_out.shape[1] - cols
    lanes = lax.broadcasted_iota(jnp.int32, (total.shape[0], tail), 1)
    extra = jnp.where(lanes == 0, high, jnp.where(lanes == 1, low, 0.0))
    packed_out[...] = jnp.concatenate([both[:, cols:], extra], axis=1).astype(BF16)


def residual_back_kernel(
    meta, r0, r1, r2, r3, residual, gate, probs, route_col, params, cotangent, mixed, w_attn_out,
    d_attn_cols_out, attn_grad_out, d_mixed_out, router_grad_out, gain_grad_out,
    place, place_f32,
):
    rank = meta[0]
    experts = probs.shape[1]
    feats = residual.shape[1]
    cols = feats // 4
    router = params[:experts, :]
    gain = params[experts : experts + 1, :]
    d_gate = 0.0
    for j, r in enumerate((r0, r1, r2, r3)):
        place[rank ^ j] = r[:, :cols]
        d_gate = d_gate + r[:, cols : cols + 1].astype(F32) + r[:, cols + 1 : cols + 2].astype(F32)
    d_routed = jnp.concatenate([place[r] for r in range(4)], axis=1).astype(F32)
    res = residual[...]
    scale = row_scale(res)
    lanes = lax.broadcasted_iota(jnp.int32, probs.shape, 1)
    onehot = jnp.where(lanes == route_col[...], 1.0, 0.0)
    d_logits = d_gate * probs[...] * (onehot - gate[...])
    d_normed = d_routed + dot_nn(d_logits, router, PRECISE)
    normed = res * scale * gain
    router_grad = dot_tn(d_logits, normed, PRECISE)
    gain_grad = jnp.sum(d_normed * res * scale, axis=0, keepdims=True)
    cross = jnp.sum(gain * res * d_normed, axis=1, keepdims=True)
    d_residual = (
        cotangent[...].astype(F32)
        + scale * gain * d_normed
        - res * (scale * scale * scale * cross * (1.0 / feats))
    )
    for r in range(4):
        own = slice(r * cols, (r + 1) * cols)
        place_f32[r] = d_residual[:, own]

        @pl.when(rank == r)
        def _():
            router_grad_out[...] = router_grad[:, own]
            gain_grad_out[...] = gain_grad[:, own]

    d_attn_cols_out[...] = place_f32[rank]
    d_attn = d_residual.astype(BF16)
    attn_grad_out[...] = dot_tn(mixed[...], d_attn).astype(BF16)
    d_mixed_out[...] = dot_nt(d_attn, w_attn_out[...]).astype(BF16)


def attend_back_kernel(
    meta, tokens, gain, normed, query, key, value, probs, d_mixed, bucket,
    w_query, w_key, w_value,
    query_grad_out, key_grad_out, value_grad_out, table_grad_out, gain_grad_out,
    keep_out, send_out, d_query, d_key, d_value, place,
    *, buckets,
):
    rank = meta[0]
    length = tokens.shape[0]
    width = 2 * length
    heads = query.shape[1] // HDIM
    marks = bucket_marks(bucket, buckets)
    zeros = jnp.zeros((8, width - length), F32)
    table_cols = []
    for h in range(heads):
        cols = slice(h * HDIM, (h + 1) * HDIM)
        dk = jnp.zeros((length, HDIM), F32)
        dv = jnp.zeros((length, HDIM), F32)
        diagonals = jnp.zeros((8, width), F32)
        for c in range(0, length, CHUNK):
            span = slice(c, c + CHUNK)
            weights = probs[h, span, :]
            d_probs = dot_nt(d_mixed[span, cols], value[:, cols])
            inner = jnp.sum(d_probs * weights, axis=1, keepdims=True)
            d_scores = weights * (d_probs - inner)
            for b in range(CHUNK // 8):
                piece = jnp.concatenate([d_scores[8 * b : 8 * b + 8, :], zeros], axis=1)
                diagonals = diagonals + pltpu.roll(piece, (length - 1 - c - 8 * b) % width, 1)
            low = d_scores.astype(BF16)
            d_query[span, cols] = (dot_nn(low, key[:, cols]) * SCORE_SCALE).astype(BF16)
            dk = dk + dot_tn(low, query[span, cols])
            dv = dv + dot_tn(weights.astype(BF16), d_mixed[span, cols])
        d_key[:, cols] = (dk * SCORE_SCALE).astype(BF16)
        d_value[:, cols] = dv.astype(BF16)
        line = diagonals[0:1]
        for r in range(1, 8):
            line = line + pltpu.roll(diagonals[r : r + 1], width - r, 1)
        table_cols.append(jnp.sum(jnp.where(marks, line, 0.0), axis=1, keepdims=True))
    table_grad_out[...] = jnp.concatenate(table_cols, axis=1)
    normed_rows = normed[...]
    query_grad_out[...] = dot_tn(normed_rows, d_query[...]).astype(BF16)
    key_grad_out[...] = dot_tn(normed_rows, d_key[...]).astype(BF16)
    value_grad_out[...] = dot_tn(normed_rows, d_value[...]).astype(BF16)
    d_normed = (
        dot_nt(d_query[...], w_query[...])
        + dot_nt(d_key[...], w_key[...])
        + dot_nt(d_value[...], w_value[...])
    )
    rows = tokens[...].astype(F32)
    scale = row_scale(rows)
    product = d_normed * rows
    gain_grad_out[...] = jnp.sum(product * scale, axis=0, keepdims=True)
    cross = jnp.sum(product * gain[...], axis=1, keepdims=True)
    high = cross.astype(BF16).astype(F32)
    low = cross - high
    cols = rows.shape[1] // 4
    tail = place.shape[2] - cols
    lanes = lax.broadcasted_iota(jnp.int32, (length, tail), 1)
    extra = jnp.where(lanes == 0, high, jnp.where(lanes == 1, low, 0.0)).astype(BF16)
    for r in range(4):
        j = rank ^ r
        own = d_normed[:, r * cols : (r + 1) * cols].astype(BF16)
        place[(j % 2) * 2 + j // 2] = jnp.concatenate([own, extra], axis=1)
    keep_out[...] = place[0:2]
    send_out[...] = place[2:4]


def input_kernel(meta, tokens, gain, d_attn_cols, first, second, out, place, gain_place):
    rank = meta[0]
    feats = tokens.shape[1]
    cols = feats // 4
    rows = tokens[...].astype(F32)
    scale = row_scale(rows)
    both = first[...].astype(F32) + second[...].astype(F32)
    cross = both[:, cols : cols + 1] + both[:, cols + 1 : cols + 2]
    for r in range(4):
        place[r] = rows[:, r * cols : (r + 1) * cols]
        gain_place[r] = gain[:, r * cols : (r + 1) * cols]
    out[...] = (
        d_attn_cols[...]
        + scale * gain_place[rank] * both[:, :cols]
        - place[rank] * (scale * scale * scale * cross * (1.0 / feats))
    )


def call(kernel, outs, scratch, *operands, flops=0, moved=0, smem=1):
    specs = [
        pl.BlockSpec(memory_space=pltpu.SMEM if i < smem else pltpu.VMEM)
        for i in range(len(operands))
    ]
    return pl.pallas_call(
        kernel,
        out_shape=[jax.ShapeDtypeStruct(shape, kind) for shape, kind in outs],
        in_specs=specs,
        out_specs=[pl.BlockSpec(memory_space=pltpu.VMEM)] * len(outs),
        scratch_shapes=[pltpu.VMEM(shape, kind) for shape, kind in scratch],
        compiler_params=pltpu.CompilerParams(vmem_limit_bytes=48 * 1024 * 1024),
        cost_estimate=pl.CostEstimate(flops=flops, bytes_accessed=moved, transcendentals=0),
    )(*operands)


def swap(array, axis, bit):
    size = lax.axis_size(axis)
    return lax.ppermute(array, axis, [(i, i ^ bit) for i in range(size)])


def gather_four(array):
    across = swap(array, "tensor", 2)
    beside = swap(array, "tensor", 1)
    return [array, beside, across, swap(across, "tensor", 1)]


def exchange(blocks):
    return [blocks[0]] + [swap(b, "expert", k) for k, b in enumerate(blocks) if k]


def on_device(
    tokens, cotangent, norm1_gain, w_query, w_key, w_value, w_attn_out, bias_table, norm2_gain,
    w_router, expert_in, expert_out, route, slot, segment, rel_bucket,
):
    length, feats = tokens.shape
    cols = cotangent.shape[1]
    heads = cols // HDIM
    experts = lax.axis_size("expert")
    cap = 2 * length // experts
    share = cap // 4
    rank = lax.axis_index("tensor").astype(jnp.int32)
    expert = lax.axis_index("expert").astype(jnp.int32)
    meta = jnp.stack([rank, expert])
    total = experts * cap
    direct = share % 16 == 0

    relative = route ^ expert
    code_col = (relative * cap + slot)[:, None]
    part_slot = slot - rank * share
    inside = (part_slot >= 0) & (part_slot < share)
    code_row = jnp.where(inside, relative * share + part_slot, -1)[None, :]
    route_col = route[:, None]

    cot_parts = gather_four(cotangent)
    cot_outs = call(
        cotangent_kernel,
        [((length, feats), BF16)] + [((share, feats), BF16)] * experts,
        [((4, length, cols), BF16)],
        meta, code_row, *cot_parts,
        flops=2 * total // 4 * length * feats, moved=4 * length * feats,
    )
    cot_full = cot_outs[0]
    cot_rows = gather_four(jnp.concatenate(exchange(cot_outs[1:]), axis=0))

    attn_weights = gather_four(w_attn_out)
    pad_rows = -(experts + 1) % 8
    packed_params = jnp.concatenate(
        [w_router.astype(F32).T, norm2_gain[None, :], jnp.zeros((pad_rows, cols), F32)], axis=0
    )
    param_rows = packed_params.shape[0]
    params_parts = gather_four(packed_params)

    gain_row = norm1_gain[None, :]
    bucket_row = jnp.concatenate([rel_bucket, jnp.full((1,), -1, jnp.int32)])[None, :]
    normed, query, key, value, probs, mixed = call(
        attend_kernel,
        [((length, feats), BF16)]
        + [((length, cols), BF16)] * 3
        + [((heads, length, length), F32), ((length, cols), BF16)],
        [((length, length), F32)],
        tokens, gain_row, w_query, w_key, w_value, segment[:, None], segment[None, :],
        bucket_row, bias_table,
        flops=8 * length * feats * cols, moved=8 * length * feats, smem=0,
    )

    mixed_parts = gather_four(mixed)
    res_outs = call(
        residual_kernel,
        [
            ((length, feats), F32),
            ((length, 1), F32),
            ((length, experts), F32),
            ((param_rows, feats), F32),
        ]
        + [((share, feats), BF16)] * experts,
        [((4, param_rows, cols), F32)],
        meta, code_row, route_col, *mixed_parts, *attn_weights, *params_parts, tokens,
        flops=4 * length * feats * feats, moved=8 * length * feats,
    )
    residual, gate, router_probs, params = res_outs[:4]
    rows = gather_four(jnp.concatenate(exchange(res_outs[4:]), axis=0))

    if not direct:
        def assemble(parts):
            stacked = jnp.stack(parts).reshape(4, experts, share, feats)
            stacked = stacked[rank ^ jnp.arange(4, dtype=jnp.int32)]
            return [jnp.transpose(stacked, (1, 0, 2, 3)).reshape(total, feats)]

        one = jnp.zeros((16, 128), BF16)
        rows = assemble(rows) + [one] * 3
        cot_rows = assemble(cot_rows) + [one] * 3
    w_in, w_out = expert_in[0], expert_out[0]
    hidden_count = w_in.shape[1]
    all_shape = (experts, 4, share, feats) if direct else (1, 1, 16, 128)
    rows_all, act, cots, d_hidden, keep, send = call(
        functools.partial(expert_kernel, direct=direct),
        [((total, feats), BF16), ((total, hidden_count), BF16), ((total, feats), BF16),
         ((total, hidden_count), BF16), ((2, total, 2 * cols), BF16), ((2, total, 2 * cols), BF16)],
        [(all_shape, BF16), (all_shape, BF16), ((4, 256, 2 * cols), BF16)],
        meta, *rows, *cot_rows, w_in, w_out, params[:experts],
        flops=8 * total * feats * hidden_count, moved=20 * total * feats,
    )
    expert_out_grad = dot_tn(act, cots)[None]
    expert_in_grad = dot_tn(rows_all, d_hidden)[None]

    met = (keep.astype(F32) + swap(send, "tensor", 1).astype(F32)).astype(BF16)
    whole = (met[0].astype(F32) + swap(met[1], "tensor", 2).astype(F32)).astype(BF16)
    came = exchange([whole[k * cap : (k + 1) * cap] for k in range(experts)])

    packed_width = -(-(cols + 2) // 128) * 128
    block_out, packed = call(
        combine_kernel,
        [((length, cols), BF16), ((length, packed_width), BF16)],
        [((total, 2 * cols), BF16), ((4, length, cols), F32)],
        meta, code_col, residual, gate, cotangent, *came,
        flops=2 * length * total * 2 * cols, moved=8 * length * feats,
    )
    packed_parts = gather_four(packed)
    d_attn_cols, attn_grad, d_mixed, router_grad, gain2_grad = call(
        residual_back_kernel,
        [((length, cols), F32), ((cols, feats), BF16), ((length, cols), BF16),
         ((experts, cols), F32), ((1, cols), F32)],
        [((4, length, cols), BF16), ((4, length, cols), F32)],
        meta, *packed_parts, residual, gate, router_probs, route_col, params, cot_full, mixed,
        w_attn_out,
        flops=4 * length * feats * cols, moved=8 * length * feats,
    )
    query_grad, key_grad, value_grad, table_grad, gain1_grad, keep_in, send_in = call(
        functools.partial(attend_back_kernel, buckets=bias_table.shape[0]),
        [((feats, cols), BF16)] * 3
        + [(bias_table.shape, F32), ((1, feats), F32)]
        + [((2, length, packed_width), BF16)] * 2,
        [((length, cols), BF16)] * 3 + [((4, length, packed_width), BF16)],
        meta, tokens, gain_row, normed, query, key, value, probs, d_mixed, bucket_row,
        w_query, w_key, w_value,
        flops=16 * length * feats * cols, moved=12 * length * feats,
    )
    met_in = (keep_in.astype(F32) + swap(send_in, "tensor", 1).astype(F32)).astype(BF16)
    far = swap(met_in[1], "tensor", 2)
    (input_grad,) = call(
        input_kernel,
        [((length, cols), F32)],
        [((4, length, cols), F32), ((4, 1, cols), F32)],
        meta, tokens, gain_row, d_attn_cols, met_in[0], far,
        flops=length * feats, moved=4 * length * feats,
    )

    attn_grad = lax.psum(attn_grad, "expert")
    query_grad, key_grad, value_grad = lax.psum((query_grad, key_grad, value_grad), "expert")
    table_grad, router_grad, gain2_grad = lax.psum((table_grad, router_grad, gain2_grad), "expert")
    gain1_grad = lax.psum(gain1_grad, ("expert", "tensor"))
    return (
        block_out,
        input_grad,
        gain1_grad[0],
        query_grad.astype(F32),
        key_grad.astype(F32),
        value_grad.astype(F32),
        attn_grad.astype(F32),
        table_grad,
        gain2_grad[0],
        router_grad.T,
        expert_in_grad,
        expert_out_grad,
    )


def solution(mesh):
    return jax.shard_map(
        on_device,
        mesh=mesh,
        in_specs=(
            P("expert", None),
            P("expert", "tensor"),
            P(),
            P(None, "tensor"),
            P(None, "tensor"),
            P(None, "tensor"),
            P("tensor", None),
            P(None, "tensor"),
            P("tensor"),
            P("tensor", None),
            P("expert", None, "tensor"),
            P("expert", "tensor", None),
            P("expert"),
            P("expert"),
            P("expert"),
            P(),
        ),
        out_specs=(
            P("expert", "tensor"),
            P("expert", "tensor"),
            P(),
            P(None, "tensor"),
            P(None, "tensor"),
            P(None, "tensor"),
            P("tensor", None),
            P(None, "tensor"),
            P("tensor"),
            P("tensor", None),
            P("expert", None, "tensor"),
            P("expert", "tensor", None),
        ),
        check_vma=False,
    )
```

time: 746 us -> 308 us (0.41); the launches traced: 733 us -> 307 us
  blocking collectives: 321 us -> 73.9 us
  local copies, waits for them, and re-layouts: 223 us -> 26.6 us
  starting transfers between devices: 0.21 us -> 60.1 us
  waiting for transfers between devices: 120 us -> 70 us
  Pallas kernels: 0 us -> 47.8 us
  matrix products: 40.6 us -> 7.71 us
  other arithmetic: 14 us -> 6.37 us
    all_to_all x4 -> x0, blocking collectives: 234 us -> none  [the longest x2 149 us: from_experts(): lax.all_to_all(jnp.transpose(sectioned, (1, 0, 2, 3)).reshape(sources * E...]
    scatter x2 -> x0, local copies, waits for them, and re-layouts: 93 us -> none  [to_experts(): buffer = jnp.zeros((expert_count, capacity, whole_rows.shape[1]), jnp.bfl...]
    reduce_scatter x3 -> x0, waiting for transfers between devices: 81.3 us -> none  [the longest x2 51.8 us: from_experts(): lax.psum_scatter(picked, 'tensor', scatter_dimension=1, tiled=True)]
    ppermute x0 -> x46, waiting for transfers between devices: none -> 66.9 us  [swap(): return lax.ppermute(array, axis, [(i, i ^ bit) for i in range(size)])]
    ppermute x0 -> x46, starting transfers between devices: none -> 60 us  [swap(): return lax.ppermute(array, axis, [(i, i ^ bit) for i in range(size)])]
    pallas_call x0 -> x8, Pallas kernels: none -> 47.8 us  [call(): pl.pallas_call(kernel, out_shape=[jax.ShapeDtypeStruct(shape, kind) for s...]
    psum x2 -> x1, waiting for transfers between devices: 39 us -> 3.09 us  [on_device(): lax.psum((query_grad, key_grad, value_grad), 'expert')]
    dot_general x29 -> x2, matrix products: 40.6 us -> 7.71 us  [dot_tn(): lax.dot_general(a, b, (((0,), (0,)), ((), ())), precision=precision, pref...]
  transfers between devices with their start and end apart: 5 -> 47, of which waited for: 4 -> 20; matrix products, arithmetic and copies ran while one was open for 11% -> 6% of each run, Pallas kernels for 0% -> 5%
where the time goes in v1:
time: 308 us; the launch traced here: 307 us
  blocking collectives  73.9 us (24%)
  waiting for transfers between devices  70 us (23%)
  starting transfers between devices  60.1 us (20%)
  Pallas kernels  47.8 us (16%)
  local copies, waits for them, and re-layouts  26.6 us (9%)
  between operations  14.6 us (5%)
  matrix products  7.71 us (3%)
  other arithmetic  6.37 us (2%)
    ppermute x46, waiting for transfers between devices, swap(): return lax.ppermute(array, axis, [(i, i ^ bit) for i in range(size)])  66.9 us
    ppermute x46, starting transfers between devices, swap(): return lax.ppermute(array, axis, [(i, i ^ bit) for i in range(size)])  60 us
    pallas_call x8, Pallas kernels, call(): pl.pallas_call(kernel, out_shape=[jax.ShapeDtypeStruct(shape, kind) for s...  47.8 us
    psum x1, blocking collectives, on_device(): gain1_grad = lax.psum(gain1_grad, ('expert', 'tensor'))  37.5 us
    psum x1, blocking collectives, on_device(): lax.psum((table_grad, router_grad, gain2_grad), 'expert')  36.4 us
    unnamed x133, local copies, waits for them, and re-layouts  23 us
    dot_general x2, matrix products, dot_tn(): lax.dot_general(a, b, (((0,), (0,)), ((), ())), precision=precision, pref...  7.71 us
  transfers between devices with their start and end apart: 47, of which 20 were waited for; matrix products, arithmetic and copies ran while one was open for 6% of the time, Pallas kernels for 5%

profile of v1, /device:TPU:0, one launch (start us, length us, event | category | flops | bytes accessed | tf_op | source)
XLA Modules:
  0.0 307.2 jit_solution(14968423917639542166)
XLA Ops:
  7.3 1.1 copy.55.c0.cotangent
  8.4 3.0 collective-permute-start.20
  15.0 1.1 copy.45.w_query
  16.1 1.1 copy.46.w_key
  17.8 7.2 %shard_map.247 = (bf16[512,768]{1,0:T(8,128)(2,1)S(1)}, bf16[512,192]{1,0:T(8,128)(2,1)S(1)}, bf16[512,192]{1,0:T(8,128)(2,1)S(1)}, bf16[512,192]{1,0:T(8,128)(2...) custom-call(bf16[512,768]{1,0:T(8,128)(2,1)S(1)} %copy-done, f32[1,768]{1,0:T(1,128)S(1)} %broadcast_in_dim.41.gain, ...), custom_call_target="tpu_custom_call" | custom-call | flops 603979776 | bytes 3145728 | tf_op jit(solution)/shard_map/pallas_call | solution.py:354
  26.5 1.7 collective-permute-start.1
  29.6 1.3 collective-permute-done.21.c3
  30.9 2.4 shard_map.249
  33.3 1.6 collective-permute-start.22
  34.8 2.6 collective-permute-done.22
  37.4 1.6 collective-permute-start.23
  39.0 2.5 collective-permute-done.23
  41.5 2.5 collective-permute-start.24
  44.0 2.5 collective-permute-done.24
  46.5 2.6 collective-permute-start.25
  49.1 2.4 collective-permute-done.25
  51.5 4.3 %collective-permute-start.26 = (bf16[32,768]{1,0:T(8,128)(2,1)S(1)}, bf16[32,768]{1,0:T(8,128)(2,1)S(1)}, u32[]{:S(2)}, u32[]{:S(2)}) collective-permute-start(bf16[32,768]{1,0:T(8,128)(2,1)S(1)} %get-tuple-element.75), channel_id=1, source_target_pairs={{0,20},{4,16},{8,28},{12,24},{16,4},{20,0},{24,12},{28,8},{1,21},{... | collective-permute-start | bytes 147464 | tf_op jit(solution)/shard_map/ppermute | solution.py:367
  56.4 1.5 collective-permute-done.26
  57.9 4.1 %collective-permute-start.27 = (bf16[32,768]{1,0:T(8,128)(2,1)S(1)}, bf16[32,768]{1,0:T(8,128)(2,1)S(1)}, u32[]{:S(2)}, u32[]{:S(2)}) collective-permute-start(bf16[32,768]{1,0:T(8,128)(2,1)S(1)} %get-tuple-element.76), channel_id=1, source_target_pairs={{0,24},{4,28},{8,16},{12,20},{16,8},{20,12},{24,0},{28,4},{1,25},{... | collective-permute-start | bytes 147464 | tf_op jit(solution)/shard_map/ppermute | solution.py:367
  62.6 1.5 collective-permute-done.27
  64.1 6.8 %collective-permute-start.28 = (bf16[32,768]{1,0:T(8,128)(2,1)S(1)}, bf16[32,768]{1,0:T(8,128)(2,1)S(1)}, u32[]{:S(2)}, u32[]{:S(2)}) collective-permute-start(bf16[32,768]{1,0:T(8,128)(2,1)S(1)} %get-tuple-element.77), channel_id=1, source_target_pairs={{0,28},{4,24},{8,20},{12,16},{16,12},{20,8},{24,4},{28,0},{1,29},{... | collective-permute-start | bytes 147464 | tf_op jit(solution)/shard_map/ppermute | solution.py:367
  70.9 2.1 collective-permute-done.28
  73.0 1.4 collective-permute-done.8.p3
  74.9 1.0 copy-done.17
  75.8 5.4 %shard_map.248 = (f32[512,768]{1,0:T(8,128)S(1)}, f32[512,1]{1,0:T(8,128)S(1)}, f32[512,8]{1,0:T(8,128)S(1)}, f32[16,768]{1,0:T(8,128)S(1)}, bf16[32,768]{1,0:T(...) custom-call(s32[2]{0:T(128)S(1)} %pad_add_fusion.1.meta, ...), custom_call_target="tpu_custom_call" | custom-call | flops 1207959552 | bytes 3145728 | tf_op jit(solution)/shard_map/pallas_call | solution.py:354
  82.7 1.0 collective-permute-start.9
  83.6 2.5 collective-permute-start.11
  86.1 2.4 collective-permute-start.12
  88.5 1.0 collective-permute-start.13
  89.5 4.4 %collective-permute-start.14 = (bf16[32,768]{1,0:T(8,128)(2,1)S(1)}, bf16[32,768]{1,0:T(8,128)(2,1)S(1)}, u32[]{:S(2)}, u32[]{:S(2)}) collective-permute-start(bf16[32,768]{1,0:T(8,128)(2,1)S(1)} %get-tuple-element.68), channel_id=1, source_target_pairs={{0,24},{4,28},{8,16},{12,20},{16,8},{20,12},{24,0},{28,4},{1,25},{... | collective-permute-start | bytes 147464 | tf_op jit(solution)/shard_map/ppermute | solution.py:367
  94.0 2.8 collective-permute-done.13
  96.8 3.9 %collective-permute-done.15 = bf16[32,768]{1,0:T(8,128)(2,1)S(1)} collective-permute-done((bf16[32,768]{1,0:T(8,128)(2,1)S(1)}, bf16[32,768]{1,0:T(8,128)(2,1)S(1)}, u32[]{:S(2)}, u32[]{:S(2)}) %collective-permute-start.15) | collective-permute-done | bytes 49184 | tf_op jit(solution)/shard_map/ppermute | solution.py:367
  100.7 1.6 collective-permute-start.17
  102.8 6.1 %collective-permute-done.17.x2 = bf16[256,768]{1,0:T(8,128)(2,1)S(1)} collective-permute-done((bf16[256,768]{1,0:T(8,128)(2,1)S(1)}, bf16[256,768]{1,0:T(8,128)(2,1)S(1)}, u32[]{:S(2)}, u32[]{:S(2)}) %collective-permute-start.17) | collective-permute-done | bytes 393248 | tf_op jit(solution)/shard_map/ppermute | solution.py:367
  109.0 1.7 collective-permute-done.18.x3
  110.6 11.7 %shard_map.250 = (bf16[1024,768]{1,0:T(8,128)(2,1)}, bf16[1024,768]{1,0:T(8,128)(2,1)}, bf16[1024,768]{1,0:T(8,128)(2,1)}, bf16[1024,768]{1,0:T(8,128)(2,1)}, bf...) custom-call(s32[2]{0:T(128)S(1)} %pad_add_fusion.1.meta, ...), custom_call_target="tpu_custom_call" | custom-call | flops 4831838208 | bytes 15728640 | tf_op jit(solution)/shard_map/pallas_call | solution.py:354
  122.5 3.5 %collective-permute-done.32 = bf16[2,1024,384]{2,1,0:T(8,128)(2,1)S(1)} collective-permute-done((bf16[2,1024,384]{2,1,0:T(8,128)(2,1)}, bf16[2,1024,384]{2,1,0:T(8,128)(2,1)S(1)}, u32[]{:S(2)}, u32[]{:S(2)}) %collective-permute-start.32) | collective-permute-done | bytes 1572896 | tf_op jit(solution)/shard_map/ppermute | solution.py:367
  126.0 1.8 add_convert_fusion
  127.9 1.7 collective-permute-start.33
  129.6 18.0 %collective-permute-done.33 = bf16[1024,384]{1,0:T(8,128)(2,1)S(1)} collective-permute-done((bf16[1024,384]{1,0:T(8,128)(2,1)S(1)}, bf16[1024,384]{1,0:T(8,128)(2,1)S(1)}, u32[]{:S(2)}, u32[]{:S(2)}) %collective-permute-start.33) | collective-permute-done | bytes 786464 | tf_op jit(solution)/shard_map/ppermute | solution.py:367
  149.0 3.1 collective-permute-start.36
  152.1 1.9 collective-permute-start.37
  155.5 1.5 collective-permute-start.39
  157.6 3.4 %collective-permute-start.40 = (bf16[128,384]{1,0:T(8,128)(2,1)}, bf16[128,384]{1,0:T(8,128)(2,1)}, u32[]{:S(2)}, u32[]{:S(2)}) collective-permute-start(bf16[128,384]{1,0:T(8,128)(2,1)} %get-tuple-element.137), channel_id=1, source_target_pairs={{0,28},{4,24},{8,20},{12,16},{16,12},{20,8},{24,4},{28,0},{1,29},{... | collective-permute-start | bytes 294920 | tf_op jit(solution)/shard_map/ppermute | solution.py:367
  161.9 4.7 %collective-permute-done.37.rest_4_ = bf16[128,384]{1,0:T(8,128)(2,1)} collective-permute-done((bf16[128,384]{1,0:T(8,128)(2,1)}, bf16[128,384]{1,0:T(8,128)(2,1)}, u32[]{:S(2)}, u32[]{:S(2)}) %collective-permute-start.37) | collective-permute-done | bytes 98336 | tf_op jit(solution)/shard_map/ppermute | solution.py:367
  166.6 2.0 collective-permute-done.38.rest_5_
  168.6 0.9 copy-done.2
  174.2 2.9 shard_map.251
  177.8 1.4 collective-permute-start.42
  179.2 5.0 %collective-permute-done.42.r2 = bf16[512,256]{1,0:T(8,128)(2,1)S(1)} collective-permute-done((bf16[512,256]{1,0:T(8,128)(2,1)S(1)}, bf16[512,256]{1,0:T(8,128)(2,1)S(1)}, u32[]{:S(2)}, u32[]{:S(2)}) %collective-permute-start.42) | collective-permute-done | bytes 262176 | tf_op jit(solution)/shard_map/ppermute | solution.py:367
  184.1 1.5 collective-permute-done.43.r3
  185.8 6.1 %shard_map.252 = (f32[512,192]{1,0:T(8,128)S(1)}, bf16[192,768]{1,0:T(8,128)(2,1)}, bf16[512,192]{1,0:T(8,128)(2,1)S(1)}, f32[8,192]{1,0:T(8,128)S(1)}, f32[1,192]{1,0:T(1,128)S(1)}) custom-call(s32[2]{0:T(128)S(1)} %pad_add_fusion.1.meta, bf16[512,256]{1,0:T(8,128)(2,1)S(1)} %get-tuple-element.82.r0, bf16[512,256]{1,0:T(8,128)(2,1)S(1)} %collective-permute-done.41.r1, ...), custom_call_target="tpu_custom_call" | custom-call | flops 301989888 | bytes 3145728 | tf_op jit(solution)/shard_map/pallas_call | solution.py:354
  192.7 11.1 %shard_map.253 = (bf16[768,192]{1,0:T(8,128)(2,1)}, bf16[768,192]{1,0:T(8,128)(2,1)}, bf16[768,192]{1,0:T(8,128)(2,1)}, f32[32,3]{1,0:T(8,128)S(1)}, f32[1,768]{...) custom-call(s32[2]{0:T(128)S(1)} %pad_add_fusion.1.meta, ...), custom_call_target="tpu_custom_call" | custom-call | flops 1207959552 | bytes 4718592 | tf_op jit(solution)/shard_map/pallas_call | solution.py:354
  204.6 4.8 %convolution_bitcast_fusion = f32[1,768,768]{2,1,0:T(8,128)} fusion(bf16[1024,768]{1,0:T(8,128)(2,1)} %get-tuple-element.104, bf16[1024,768]{1,0:T(8,128)(2,1)} %get-tuple-element.105), kind=kOutput, calls=%fused_computation.1 | convolution fusion | flops 1207959552 | bytes 5505024 | tf_op jit(solution)/shard_map/dot_general | solution.py:35
  209.6 1.4 collective-permute-start.45
  211.1 2.9 convolution_bitcast_fusion.1
  214.8 36.4 %all-reduce = (f32[32,3]{1,0:T(8,128)S(1)}, f32[192]{0:T(256)}, f32[192,8]{0,1:T(8,128)}) all-reduce(f32[32,3]{1,0:T(8,128)S(1)} %copy-done.38, f32[192]{0:T(256)S(1)} %bitcast.41, f32[192,8]{0,1:T(8,128)S(1)} %bitcast.38), channel_id=1, replica_groups=mesh['expert'=8,'tensor'=4] {'expert'}, use_global_device_ids=true, to_apply=%region_5.6 | all-reduce | flops 1824 | bytes 14592 | tf_op jit(solution)/shard_map/psum | solution.py:519
  251.9 37.5 %psum.56 = f32[768]{0:T(1024)} all-reduce(f32[768]{0:T(1024)S(1)} %reduce), channel_id=1, replica_groups=mesh['expert'=8,'tensor'=4] {'expert','tensor'}, use_global_device_ids=true, to_apply=%region_0.1 | all-reduce | flops 768 | bytes 6144 | tf_op jit(solution)/shard_map/psum | solution.py:520
  289.4 1.1 shard_map.254
  291.5 3.1 %all-reduce.4.cloned.1.call-done = (bf16[768,192]{1,0:T(8,128)(2,1)}, bf16[768,192]{1,0:T(8,128)(2,1)}, bf16[768,192]{1,0:T(8,128)(2,1)}, bf16[192,768]{1,0:T(8,128)(2,1)}) async-done(((bf16[768,192]{1,0:T(8,128)(2,1)}, bf16[768,192]{1,0:T(8,128)(2,1)}, bf16[768,192]{1,0:T(8,128)(2,1)}, bf16[192,768]{1,0:T(8,128)(2,1)}), (bf16[768,192]{1,0:T(8,128)(2,1)}, bf16[768,192]{1,0:T(8,128)(2,1)}, ...) | async-done | bytes 1179664 | tf_op jit(solution)/shard_map/psum | solution.py:518
  294.5 1.9 convert_element_type.56
  296.4 2.0 copy.62
  298.4 1.0 copy.63
  299.4 1.0 copy.64
  (198 shorter events, 25.0 us)
Async XLA Ops:
  7.2 287.3 %all-reduce.4.cloned.1.call-start = ((), (), s32[]{:S(2)}) async-start(), calls=%async_computation | async-start | bytes 2949120 | tf_op jit(solution)/shard_map/psum | solution.py:518
  8.4 22.5 %copy-start.1 = (bf16[512,192]{1,0:T(8,128)(2,1)}, bf16[512,192]{1,0:T(8,128)(2,1)S(1)}, u32[]{:S(2)}) copy-start(bf16[512,192]{1,0:T(8,128)(2,1)S(1)} %copy.55.c0.cotangent) | copy-start | bytes 589828
  8.4 20.7 %collective-permute-start.20 = (bf16[512,192]{1,0:T(8,128)(2,1)S(1)}, bf16[512,192]{1,0:T(8,128)(2,1)}, u32[]{:S(2)}, u32[]{:S(2)}) collective-permute-start(bf16[512,192]{1,0:T(8,128)(2,1)S(1)} %copy.55.c0.cotangent), channel_id=1, source_target_pairs={{0,2},{1,3},{2,0},{3,1},{4,6},{5,7},{6,4},{7,5},{8,10},{9,11},{10,... | collective-permute-start | bytes 589832 | tf_op jit(solution)/shard_map/ppermute | solution.py:367
  11.4 17.8 %collective-permute-start.19 = (bf16[512,192]{1,0:T(8,128)(2,1)S(1)}, bf16[512,192]{1,0:T(8,128)(2,1)}, u32[]{:S(2)}, u32[]{:S(2)}) collective-permute-start(bf16[512,192]{1,0:T(8,128)(2,1)S(1)} %copy.55.c0.cotangent), channel_id=1, source_target_pairs={{0,1},{1,0},{2,3},{3,2},{4,5},{5,4},{6,7},{7,6},{8,9},{9,8},{10,11... | collective-permute-start | bytes 589832 | tf_op jit(solution)/shard_map/ppermute | solution.py:367
  13.0 12.0 %copy-start.35 = (f32[16,192]{1,0:T(8,128)}, f32[16,192]{1,0:T(8,128)S(1)}, u32[]{:S(2)}) copy-start(f32[16,192]{1,0:T(8,128)S(1)} %maximum_maximum_fusion.p0) | copy-start | bytes 36868
  13.0 42.8 %collective-permute-start.7 = (f32[16,192]{1,0:T(8,128)S(1)}, f32[16,192]{1,0:T(8,128)}, u32[]{:S(2)}, u32[]{:S(2)}) collective-permute-start(f32[16,192]{1,0:T(8,128)S(1)} %maximum_maximum_fusion.p0), channel_id=1, source_target_pairs={{0,2},{1,3},{2,0},{3,1},{4,6},{5,7},{6,4},{7,5},{8,10},{9,11},{10,... | collective-permute-start | bytes 36872 | tf_op jit(solution)/shard_map/ppermute | solution.py:367
  13.1 48.9 %collective-permute-start.6 = (f32[16,192]{1,0:T(8,128)S(1)}, f32[16,192]{1,0:T(8,128)}, u32[]{:S(2)}, u32[]{:S(2)}) collective-permute-start(f32[16,192]{1,0:T(8,128)S(1)} %maximum_maximum_fusion.p0), channel_id=1, source_target_pairs={{0,1},{1,0},{2,3},{3,2},{4,5},{5,4},{6,7},{7,6},{8,9},{9,8},{10,11... | collective-permute-start | bytes 36872 | tf_op jit(solution)/shard_map/ppermute | solution.py:367
  17.5 11.7 %copy-start.51 = (s32[512]{0:T(512)S(1)}, s32[512]{0:T(512)}, u32[]{:S(2)}) copy-start(s32[512]{0:T(512)} %param.29) | copy-start | bytes 6148
  17.5 11.7 %copy-start.16 = (bf16[192,768]{1,0:T(8,128)(2,1)S(1)}, bf16[192,768]{1,0:T(8,128)(2,1)}, u32[]{:S(2)}) copy-start(bf16[192,768]{1,0:T(8,128)(2,1)} %w_attn_out.1) | copy-start | bytes 884740
  26.5 48.3 %copy-start.19 = (bf16[512,192]{1,0:T(8,128)(2,1)}, bf16[512,192]{1,0:T(8,128)(2,1)S(1)}, u32[]{:S(2)}) copy-start(bf16[512,192]{1,0:T(8,128)(2,1)S(1)} %get-tuple-element.87.query) | copy-start | bytes 589828
  26.5 48.3 %copy-start.21 = (bf16[512,192]{1,0:T(8,128)(2,1)}, bf16[512,192]{1,0:T(8,128)(2,1)S(1)}, u32[]{:S(2)}) copy-start(bf16[512,192]{1,0:T(8,128)(2,1)S(1)} %get-tuple-element.88.key) | copy-start | bytes 589828
  26.5 35.5 %collective-permute-start.1 = (bf16[512,192]{1,0:T(8,128)(2,1)}, bf16[512,192]{1,0:T(8,128)(2,1)}, u32[]{:S(2)}, u32[]{:S(2)}) collective-permute-start(bf16[512,192]{1,0:T(8,128)(2,1)} %get-tuple-element.59.m0.mixed), channel_id=1, source_target_pairs={{0,2},{1,3},{2,0},{3,1},{4,6},{5,7},{6,4},{7,5},{8,10},{9,11},{10,... | collective-permute-start | bytes 589832 | tf_op jit(solution)/shard_map/ppermute | solution.py:367
  29.1 45.8 %copy-start.3 = (s32[512,1]{1,0:T(8,128)S(1)}, s32[512,1]{1,0:T(8,128)}, u32[]{:S(2)}) copy-start(s32[512,1]{1,0:T(8,128)} %copy.50.route_col) | copy-start | bytes 6148
  29.1 45.8 %copy-start.36 = (f32[16,192]{1,0:T(8,128)S(1)}, f32[16,192]{1,0:T(8,128)}, u32[]{:S(2)}) copy-start(f32[16,192]{1,0:T(8,128)} %copy-done.35) | copy-start | bytes 36868
  29.2 1.8 collective-permute-start.21
  29.2 26.7 %collective-permute-start.4 = (bf16[192,768]{1,0:T(8,128)(2,1)S(1)}, bf16[192,768]{1,0:T(8,128)(2,1)S(1)}, u32[]{:S(2)}, u32[]{:S(2)}) collective-permute-start(bf16[192,768]{1,0:T(8,128)(2,1)S(1)} %copy-done.16), channel_id=1, source_target_pairs={{0,2},{1,3},{2,0},{3,1},{4,6},{5,7},{6,4},{7,5},{8,10},{9,11},{10,... | collective-permute-start | bytes 884744 | tf_op jit(solution)/shard_map/ppermute | solution.py:367
  33.3 41.5 %copy-start.11 = (bf16[512,768]{1,0:T(8,128)(2,1)}, bf16[512,768]{1,0:T(8,128)(2,1)S(1)}, u32[]{:S(2)}) copy-start(bf16[512,768]{1,0:T(8,128)(2,1)S(1)} %get-tuple-element.84.cotangent) | copy-start | bytes 2359300
  33.3 4.2 %collective-permute-start.22 = (bf16[32,768]{1,0:T(8,128)(2,1)S(1)}, bf16[32,768]{1,0:T(8,128)(2,1)S(1)}, u32[]{:S(2)}, u32[]{:S(2)}) collective-permute-start(bf16[32,768]{1,0:T(8,128)(2,1)S(1)} %get-tuple-element.71), channel_id=1, source_target_pairs={{0,4},{4,0},{8,12},{12,8},{16,20},{20,16},{24,28},{28,24},{1,5},{5... | collective-permute-start | bytes 147464 | tf_op jit(solution)/shard_map/ppermute | solution.py:367
  37.4 4.1 %collective-permute-start.23 = (bf16[32,768]{1,0:T(8,128)(2,1)S(1)}, bf16[32,768]{1,0:T(8,128)(2,1)S(1)}, u32[]{:S(2)}, u32[]{:S(2)}) collective-permute-start(bf16[32,768]{1,0:T(8,128)(2,1)S(1)} %get-tuple-element.72), channel_id=1, source_target_pairs={{0,8},{4,12},{8,0},{12,4},{16,24},{20,28},{24,16},{28,20},{1,9},{5... | collective-permute-start | bytes 147464 | tf_op jit(solution)/shard_map/ppermute | solution.py:367
  41.5 5.0 %collective-permute-start.24 = (bf16[32,768]{1,0:T(8,128)(2,1)S(1)}, bf16[32,768]{1,0:T(8,128)(2,1)S(1)}, u32[]{:S(2)}, u32[]{:S(2)}) collective-permute-start(bf16[32,768]{1,0:T(8,128)(2,1)S(1)} %get-tuple-element.73), channel_id=1, source_target_pairs={{0,12},{4,8},{8,4},{12,0},{16,28},{20,24},{24,20},{28,16},{1,13},{... | collective-permute-start | bytes 147464 | tf_op jit(solution)/shard_map/ppermute | solution.py:367
  46.5 5.0 %collective-permute-start.25 = (bf16[32,768]{1,0:T(8,128)(2,1)S(1)}, bf16[32,768]{1,0:T(8,128)(2,1)S(1)}, u32[]{:S(2)}, u32[]{:S(2)}) collective-permute-start(bf16[32,768]{1,0:T(8,128)(2,1)S(1)} %get-tuple-element.74), channel_id=1, source_target_pairs={{0,16},{4,20},{8,24},{12,28},{16,0},{20,4},{24,8},{28,12},{1,17},{... | collective-permute-start | bytes 147464 | tf_op jit(solution)/shard_map/ppermute | solution.py:367
  51.5 6.4 %collective-permute-start.26 = (bf16[32,768]{1,0:T(8,128)(2,1)S(1)}, bf16[32,768]{1,0:T(8,128)(2,1)S(1)}, u32[]{:S(2)}, u32[]{:S(2)}) collective-permute-start(bf16[32,768]{1,0:T(8,128)(2,1)S(1)} %get-tuple-element.75), channel_id=1, source_target_pairs={{0,20},{4,16},{8,28},{12,24},{16,4},{20,0},{24,12},{28,8},{1,21},{... | collective-permute-start | bytes 147464 | tf_op jit(solution)/shard_map/ppermute | solution.py:367
  55.8 19.0 %collective-permute-start.3 = (bf16[192,768]{1,0:T(8,128)(2,1)S(1)}, bf16[192,768]{1,0:T(8,128)(2,1)S(1)}, u32[]{:S(2)}, u32[]{:S(2)}) collective-permute-start(bf16[192,768]{1,0:T(8,128)(2,1)S(1)} %copy-done.16), channel_id=1, source_target_pairs={{0,1},{1,0},{2,3},{3,2},{4,5},{5,4},{6,7},{7,6},{8,9},{9,8},{10,11... | collective-permute-start | bytes 884744 | tf_op jit(solution)/shard_map/ppermute | solution.py:367
  55.9 18.9 %collective-permute-start.5 = (bf16[192,768]{1,0:T(8,128)(2,1)S(1)}, bf16[192,768]{1,0:T(8,128)(2,1)S(1)}, u32[]{:S(2)}, u32[]{:S(2)}) collective-permute-start(bf16[192,768]{1,0:T(8,128)(2,1)S(1)} %collective-permute-done.4.w2), channel_id=1, source_target_pairs={{0,1},{1,0},{2,3},{3,2},{4,5},{5,4},{6,7},{7,6},{8,9},{9,8},{10,11... | collective-permute-start | bytes 884744 | tf_op jit(solution)/shard_map/ppermute | solution.py:367
  57.9 6.2 %collective-permute-start.27 = (bf16[32,768]{1,0:T(8,128)(2,1)S(1)}, bf16[32,768]{1,0:T(8,128)(2,1)S(1)}, u32[]{:S(2)}, u32[]{:S(2)}) collective-permute-start(bf16[32,768]{1,0:T(8,128)(2,1)S(1)} %get-tuple-element.76), channel_id=1, source_target_pairs={{0,24},{4,28},{8,16},{12,20},{16,8},{20,12},{24,0},{28,4},{1,25},{... | collective-permute-start | bytes 147464 | tf_op jit(solution)/shard_map/ppermute | solution.py:367
  62.0 12.8 %collective-permute-start = (bf16[512,192]{1,0:T(8,128)(2,1)}, bf16[512,192]{1,0:T(8,128)(2,1)S(1)}, u32[]{:S(2)}, u32[]{:S(2)}) collective-permute-start(bf16[512,192]{1,0:T(8,128)(2,1)} %get-tuple-element.59.m0.mixed), channel_id=1, source_target_pairs={{0,1},{1,0},{2,3},{3,2},{4,5},{5,4},{6,7},{7,6},{8,9},{9,8},{10,11... | collective-permute-start | bytes 589832 | tf_op jit(solution)/shard_map/ppermute | solution.py:367
  62.1 12.7 %collective-permute-start.2 = (bf16[512,192]{1,0:T(8,128)(2,1)}, bf16[512,192]{1,0:T(8,128)(2,1)S(1)}, u32[]{:S(2)}, u32[]{:S(2)}) collective-permute-start(bf16[512,192]{1,0:T(8,128)(2,1)} %collective-permute-done.1.m2), channel_id=1, source_target_pairs={{0,1},{1,0},{2,3},{3,2},{4,5},{5,4},{6,7},{7,6},{8,9},{9,8},{10,11... | collective-permute-start | bytes 589832 | tf_op jit(solution)/shard_map/ppermute | solution.py:367
  64.1 8.9 %collective-permute-start.28 = (bf16[32,768]{1,0:T(8,128)(2,1)S(1)}, bf16[32,768]{1,0:T(8,128)(2,1)S(1)}, u32[]{:S(2)}, u32[]{:S(2)}) collective-permute-start(bf16[32,768]{1,0:T(8,128)(2,1)S(1)} %get-tuple-element.77), channel_id=1, source_target_pairs={{0,28},{4,24},{8,20},{12,16},{16,12},{20,8},{24,4},{28,0},{1,29},{... | collective-permute-start | bytes 147464 | tf_op jit(solution)/shard_map/ppermute | solution.py:367
  73.0 1.4 collective-permute-start.8
  74.4 28.5 %collective-permute-start.30 = (bf16[256,768]{1,0:T(8,128)(2,1)S(1)}, bf16[256,768]{1,0:T(8,128)(2,1)S(1)}, u32[]{:S(2)}, u32[]{:S(2)}) collective-permute-start(bf16[256,768]{1,0:T(8,128)(2,1)S(1)} %constant_dynamic-update-slice_fusion.8.c0), channel_id=1, source_target_pairs={{0,2},{1,3},{2,0},{3,1},{4,6},{5,7},{6,4},{7,5},{8,10},{9,11},{10,... | collective-permute-start | bytes 1179656 | tf_op jit(solution)/shard_map/ppermute | solution.py:367
  75.8 34.8 %copy-start.44 = (bf16[1,768,768]{2,1,0:T(8,128)(2,1)S(1)}, bf16[1,768,768]{2,1,0:T(8,128)(2,1)}, u32[]{:S(2)}) copy-start(bf16[1,768,768]{2,1,0:T(8,128)(2,1)} %param.26) | copy-start | bytes 3538948
  75.8 34.8 %copy-start.45 = (bf16[1,768,768]{2,1,0:T(8,128)(2,1)S(1)}, bf16[1,768,768]{2,1,0:T(8,128)(2,1)}, u32[]{:S(2)}) copy-start(bf16[1,768,768]{2,1,0:T(8,128)(2,1)} %param.27) | copy-start | bytes 3538948
  82.6 26.3 %copy-start.29 = (f32[16,768]{1,0:T(8,128)}, f32[16,768]{1,0:T(8,128)S(1)}, u32[]{:S(2)}) copy-start(f32[16,768]{1,0:T(8,128)S(1)} %get-tuple-element.78.params) | copy-start | bytes 147460
  82.7 5.9 %collective-permute-start.9 = (bf16[32,768]{1,0:T(8,128)(2,1)S(1)}, bf16[32,768]{1,0:T(8,128)(2,1)S(1)}, u32[]{:S(2)}, u32[]{:S(2)}) collective-permute-start(bf16[32,768]{1,0:T(8,128)(2,1)S(1)} %get-tuple-element.63), channel_id=1, source_target_pairs={{0,4},{4,0},{8,12},{12,8},{16,20},{20,16},{24,28},{28,24},{1,5},{5... | collective-permute-start | bytes 147464 | tf_op jit(solution)/shard_map/ppermute | solution.py:367
  83.6 5.9 %collective-permute-start.10 = (bf16[32,768]{1,0:T(8,128)(2,1)S(1)}, bf16[32,768]{1,0:T(8,128)(2,1)S(1)}, u32[]{:S(2)}, u32[]{:S(2)}) collective-permute-start(bf16[32,768]{1,0:T(8,128)(2,1)S(1)} %get-tuple-element.64), channel_id=1, source_target_pairs={{0,8},{4,12},{8,0},{12,4},{16,24},{20,28},{24,16},{28,20},{1,9},{5... | collective-permute-start | bytes 147464 | tf_op jit(solution)/shard_map/ppermute | solution.py:367
  83.6 10.3 %collective-permute-start.11 = (bf16[32,768]{1,0:T(8,128)(2,1)S(1)}, bf16[32,768]{1,0:T(8,128)(2,1)S(1)}, u32[]{:S(2)}, u32[]{:S(2)}) collective-permute-start(bf16[32,768]{1,0:T(8,128)(2,1)S(1)} %get-tuple-element.65), channel_id=1, source_target_pairs={{0,12},{4,8},{8,4},{12,0},{16,28},{20,24},{24,20},{28,16},{1,13},{... | collective-permute-start | bytes 147464 | tf_op jit(solution)/shard_map/ppermute | solution.py:367
  86.1 7.8 %collective-permute-start.12 = (bf16[32,768]{1,0:T(8,128)(2,1)S(1)}, bf16[32,768]{1,0:T(8,128)(2,1)S(1)}, u32[]{:S(2)}, u32[]{:S(2)}) collective-permute-start(bf16[32,768]{1,0:T(8,128)(2,1)S(1)} %get-tuple-element.66), channel_id=1, source_target_pairs={{0,16},{4,20},{8,24},{12,28},{16,0},{20,4},{24,8},{28,12},{1,17},{... | collective-permute-start | bytes 147464 | tf_op jit(solution)/shard_map/ppermute | solution.py:367
  88.5 8.3 %collective-permute-start.13 = (bf16[32,768]{1,0:T(8,128)(2,1)S(1)}, bf16[32,768]{1,0:T(8,128)(2,1)S(1)}, u32[]{:S(2)}, u32[]{:S(2)}) collective-permute-start(bf16[32,768]{1,0:T(8,128)(2,1)S(1)} %get-tuple-element.67), channel_id=1, source_target_pairs={{0,20},{4,16},{8,28},{12,24},{16,4},{20,0},{24,12},{28,8},{1,21},{... | collective-permute-start | bytes 147464 | tf_op jit(solution)/shard_map/ppermute | solution.py:367
  89.5 7.3 %collective-permute-start.14 = (bf16[32,768]{1,0:T(8,128)(2,1)S(1)}, bf16[32,768]{1,0:T(8,128)(2,1)S(1)}, u32[]{:S(2)}, u32[]{:S(2)}) collective-permute-start(bf16[32,768]{1,0:T(8,128)(2,1)S(1)} %get-tuple-element.68), channel_id=1, source_target_pairs={{0,24},{4,28},{8,16},{12,20},{16,8},{20,12},{24,0},{28,4},{1,25},{... | collective-permute-start | bytes 147464 | tf_op jit(solution)/shard_map/ppermute | solution.py:367
  93.9 6.8 %collective-permute-start.15 = (bf16[32,768]{1,0:T(8,128)(2,1)S(1)}, bf16[32,768]{1,0:T(8,128)(2,1)S(1)}, u32[]{:S(2)}, u32[]{:S(2)}) collective-permute-start(bf16[32,768]{1,0:T(8,128)(2,1)S(1)} %get-tuple-element.69), channel_id=1, source_target_pairs={{0,28},{4,24},{8,20},{12,16},{16,12},{20,8},{24,4},{28,0},{1,29},{... | collective-permute-start | bytes 147464 | tf_op jit(solution)/shard_map/ppermute | solution.py:367
  100.7 8.2 %collective-permute-start.17 = (bf16[256,768]{1,0:T(8,128)(2,1)S(1)}, bf16[256,768]{1,0:T(8,128)(2,1)S(1)}, u32[]{:S(2)}, u32[]{:S(2)}) collective-permute-start(bf16[256,768]{1,0:T(8,128)(2,1)S(1)} %constant_dynamic-update-slice_fusion.x0), channel_id=1, source_target_pairs={{0,2},{1,3},{2,0},{3,1},{4,6},{5,7},{6,4},{7,5},{8,10},{9,11},{10,... | collective-permute-start | bytes 1179656 | tf_op jit(solution)/shard_map/ppermute | solution.py:367
  102.3 6.6 %collective-permute-start.29 = (bf16[256,768]{1,0:T(8,128)(2,1)S(1)}, bf16[256,768]{1,0:T(8,128)(2,1)S(1)}, u32[]{:S(2)}, u32[]{:S(2)}) collective-permute-start(bf16[256,768]{1,0:T(8,128)(2,1)S(1)} %constant_dynamic-update-slice_fusion.8.c0), channel_id=1, source_target_pairs={{0,1},{1,0},{2,3},{3,2},{4,5},{5,4},{6,7},{7,6},{8,9},{9,8},{10,11... | collective-permute-start | bytes 1179656 | tf_op jit(solution)/shard_map/ppermute | solution.py:367
  102.3 6.6 %collective-permute-start.16 = (bf16[256,768]{1,0:T(8,128)(2,1)S(1)}, bf16[256,768]{1,0:T(8,128)(2,1)S(1)}, u32[]{:S(2)}, u32[]{:S(2)}) collective-permute-start(bf16[256,768]{1,0:T(8,128)(2,1)S(1)} %constant_dynamic-update-slice_fusion.x0), channel_id=1, source_target_pairs={{0,1},{1,0},{2,3},{3,2},{4,5},{5,4},{6,7},{7,6},{8,9},{9,8},{10,11... | collective-permute-start | bytes 1179656 | tf_op jit(solution)/shard_map/ppermute | solution.py:367
  102.8 6.1 %collective-permute-start.31 = (bf16[256,768]{1,0:T(8,128)(2,1)S(1)}, bf16[256,768]{1,0:T(8,128)(2,1)S(1)}, u32[]{:S(2)}, u32[]{:S(2)}) collective-permute-start(bf16[256,768]{1,0:T(8,128)(2,1)S(1)} %collective-permute-done.30.c2), channel_id=1, source_target_pairs={{0,1},{1,0},{2,3},{3,2},{4,5},{5,4},{6,7},{7,6},{8,9},{9,8},{10,11... | collective-permute-start | bytes 1179656 | tf_op jit(solution)/shard_map/ppermute | solution.py:367
  108.9 1.7 collective-permute-start.18
  122.4 3.6 %collective-permute-start.32 = (bf16[2,1024,384]{2,1,0:T(8,128)(2,1)}, bf16[2,1024,384]{2,1,0:T(8,128)(2,1)S(1)}, u32[]{:S(2)}, u32[]{:S(2)}) collective-permute-start(bf16[2,1024,384]{2,1,0:T(8,128)(2,1)} %get-tuple-element.80), channel_id=1, source_target_pairs={{0,1},{1,0},{2,3},{3,2},{4,5},{5,4},{6,7},{7,6},{8,9},{9,8},{10,11... | collective-permute-start | bytes 4718600 | tf_op jit(solution)/shard_map/ppermute | solution.py:367
  127.9 19.6 %collective-permute-start.33 = (bf16[1024,384]{1,0:T(8,128)(2,1)S(1)}, bf16[1024,384]{1,0:T(8,128)(2,1)S(1)}, u32[]{:S(2)}, u32[]{:S(2)}) collective-permute-start(bf16[1024,384]{1,0:T(8,128)(2,1)S(1)} %slice_bitcast_fusion), channel_id=1, source_target_pairs={{0,2},{1,3},{2,0},{3,1},{4,6},{5,7},{6,4},{7,5},{8,10},{9,11},{10,... | collective-permute-start | bytes 2359304 | tf_op jit(solution)/shard_map/ppermute | solution.py:367
  148.6 6.3 %collective-permute-start.34 = (bf16[128,384]{1,0:T(8,128)(2,1)S(1)}, bf16[128,384]{1,0:T(8,128)(2,1)S(1)}, u32[]{:S(2)}, u32[]{:S(2)}) collective-permute-start(bf16[128,384]{1,0:T(8,128)(2,1)S(1)} %get-tuple-element.143), channel_id=1, source_target_pairs={{0,4},{4,0},{8,12},{12,8},{16,20},{20,16},{24,28},{28,24},{1,5},{5... | collective-permute-start | bytes 294920 | tf_op jit(solution)/shard_map/ppermute | solution.py:367
  149.0 8.0 %collective-permute-start.35 = (bf16[128,384]{1,0:T(8,128)(2,1)S(1)}, bf16[128,384]{1,0:T(8,128)(2,1)S(1)}, u32[]{:S(2)}, u32[]{:S(2)}) collective-permute-start(bf16[128,384]{1,0:T(8,128)(2,1)S(1)} %get-tuple-element.142), channel_id=1, source_target_pairs={{0,8},{4,12},{8,0},{12,4},{16,24},{20,28},{24,16},{28,20},{1,9},{5... | collective-permute-start | bytes 294920 | tf_op jit(solution)/shard_map/ppermute | solution.py:367
  149.0 12.9 %collective-permute-start.36 = (bf16[128,384]{1,0:T(8,128)(2,1)}, bf16[128,384]{1,0:T(8,128)(2,1)}, u32[]{:S(2)}, u32[]{:S(2)}) collective-permute-start(bf16[128,384]{1,0:T(8,128)(2,1)} %get-tuple-element.141), channel_id=1, source_target_pairs={{0,12},{4,8},{8,4},{12,0},{16,28},{20,24},{24,20},{28,16},{1,13},{... | collective-permute-start | bytes 294920 | tf_op jit(solution)/shard_map/ppermute | solution.py:367
  152.1 14.5 %collective-permute-start.37 = (bf16[128,384]{1,0:T(8,128)(2,1)}, bf16[128,384]{1,0:T(8,128)(2,1)}, u32[]{:S(2)}, u32[]{:S(2)}) collective-permute-start(bf16[128,384]{1,0:T(8,128)(2,1)} %get-tuple-element.140), channel_id=1, source_target_pairs={{0,16},{4,20},{8,24},{12,28},{16,0},{20,4},{24,8},{28,12},{1,17},{... | collective-permute-start | bytes 294920 | tf_op jit(solution)/shard_map/ppermute | solution.py:367
  154.0 14.6 %collective-permute-start.38 = (bf16[128,384]{1,0:T(8,128)(2,1)}, bf16[128,384]{1,0:T(8,128)(2,1)}, u32[]{:S(2)}, u32[]{:S(2)}) collective-permute-start(bf16[128,384]{1,0:T(8,128)(2,1)} %get-tuple-element.139), channel_id=1, source_target_pairs={{0,20},{4,16},{8,28},{12,24},{16,4},{20,0},{24,12},{28,8},{1,21},{... | collective-permute-start | bytes 294920 | tf_op jit(solution)/shard_map/ppermute | solution.py:367
  155.5 13.1 %collective-permute-start.39 = (bf16[128,384]{1,0:T(8,128)(2,1)}, bf16[128,384]{1,0:T(8,128)(2,1)}, u32[]{:S(2)}, u32[]{:S(2)}) collective-permute-start(bf16[128,384]{1,0:T(8,128)(2,1)} %get-tuple-element.138), channel_id=1, source_target_pairs={{0,24},{4,28},{8,16},{12,20},{16,8},{20,12},{24,0},{28,4},{1,25},{... | collective-permute-start | bytes 294920 | tf_op jit(solution)/shard_map/ppermute | solution.py:367
  157.6 11.0 %collective-permute-start.40 = (bf16[128,384]{1,0:T(8,128)(2,1)}, bf16[128,384]{1,0:T(8,128)(2,1)}, u32[]{:S(2)}, u32[]{:S(2)}) collective-permute-start(bf16[128,384]{1,0:T(8,128)(2,1)} %get-tuple-element.137), channel_id=1, source_target_pairs={{0,28},{4,24},{8,20},{12,16},{16,12},{20,8},{24,4},{28,0},{1,29},{... | collective-permute-start | bytes 294920 | tf_op jit(solution)/shard_map/ppermute | solution.py:367
  174.1 11.6 %copy-start.12 = (bf16[512,768]{1,0:T(8,128)(2,1)S(1)}, bf16[512,768]{1,0:T(8,128)(2,1)}, u32[]{:S(2)}) copy-start(bf16[512,768]{1,0:T(8,128)(2,1)} %copy-done.11) | copy-start | bytes 2359300
  174.1 11.6 %copy-start.18 = (bf16[192,768]{1,0:T(8,128)(2,1)S(1)}, bf16[192,768]{1,0:T(8,128)(2,1)}, u32[]{:S(2)}) copy-start(bf16[192,768]{1,0:T(8,128)(2,1)} %w_attn_out.1) | copy-start | bytes 884740
  174.1 11.6 %copy-start.26 = (f32[512,8]{1,0:T(8,128)S(1)}, f32[512,8]{1,0:T(8,128)}, u32[]{:S(2)}) copy-start(f32[512,8]{1,0:T(8,128)} %copy-done.25) | copy-start | bytes 49156
  174.1 11.6 %copy-start.30 = (f32[16,768]{1,0:T(8,128)S(1)}, f32[16,768]{1,0:T(8,128)}, u32[]{:S(2)}) copy-start(f32[16,768]{1,0:T(8,128)} %copy-done.29) | copy-start | bytes 147460
  177.8 6.4 %collective-permute-start.42 = (bf16[512,256]{1,0:T(8,128)(2,1)S(1)}, bf16[512,256]{1,0:T(8,128)(2,1)S(1)}, u32[]{:S(2)}, u32[]{:S(2)}) collective-permute-start(bf16[512,256]{1,0:T(8,128)(2,1)S(1)} %get-tuple-element.82.r0), channel_id=1, source_target_pairs={{0,2},{1,3},{2,0},{3,1},{4,6},{5,7},{6,4},{7,5},{8,10},{9,11},{10,... | collective-permute-start | bytes 786440 | tf_op jit(solution)/shard_map/ppermute | solution.py:367
  179.2 5.0 %collective-permute-start.41 = (bf16[512,256]{1,0:T(8,128)(2,1)S(1)}, bf16[512,256]{1,0:T(8,128)(2,1)S(1)}, u32[]{:S(2)}, u32[]{:S(2)}) collective-permute-start(bf16[512,256]{1,0:T(8,128)(2,1)S(1)} %get-tuple-element.82.r0), channel_id=1, source_target_pairs={{0,1},{1,0},{2,3},{3,2},{4,5},{5,4},{6,7},{7,6},{8,9},{9,8},{10,11... | collective-permute-start | bytes 786440 | tf_op jit(solution)/shard_map/ppermute | solution.py:367
  184.1 1.5 collective-permute-start.43
  204.4 5.1 %collective-permute-start.44 = (bf16[2,512,256]{2,1,0:T(8,128)(2,1)S(1)}, bf16[2,512,256]{2,1,0:T(8,128)(2,1)S(1)}, u32[]{:S(2)}, u32[]{:S(2)}) collective-permute-start(bf16[2,512,256]{2,1,0:T(8,128)(2,1)S(1)} %get-tuple-element.93), channel_id=1, source_target_pairs={{0,1},{1,0},{2,3},{3,2},{4,5},{5,4},{6,7},{7,6},{8,9},{9,8},{10,11... | collective-permute-start | bytes 1572872 | tf_op jit(solution)/shard_map/ppermute | solution.py:367
  209.6 79.8 %collective-permute-start.45 = (bf16[512,256]{1,0:T(8,128)(2,1)S(1)}, bf16[512,256]{1,0:T(8,128)(2,1)S(1)}, u32[]{:S(2)}, u32[]{:S(2)}) collective-permute-start(bf16[512,256]{1,0:T(8,128)(2,1)S(1)} %get-tuple-element.145), channel_id=1, source_target_pairs={{0,2},{1,3},{2,0},{3,1},{4,6},{5,7},{6,4},{7,5},{8,10},{9,11},{10,... | collective-permute-start | bytes 786440 | tf_op jit(solution)/shard_map/ppermute | solution.py:367
  211.1 78.3 %copy-start.14 = (f32[512,192]{1,0:T(8,128)S(1)}, f32[512,192]{1,0:T(8,128)}, u32[]{:S(2)}) copy-start(f32[512,192]{1,0:T(8,128)} %copy-done.13) | copy-start | bytes 1179652
  (37 other events, 169.1 us)
Sparse Core Ops, SparseCore 0:
  204.7 89.8 all-reduce.3

commit v2 on v1

v2 whole, which is shorter than its diff:
```python
import functools

import jax
import jax.numpy as jnp
from jax import lax
from jax.experimental import pallas as pl
from jax.experimental.pallas import tpu as pltpu
from jax.sharding import PartitionSpec as P

HDIM = 64
EPSILON = 1e-06
MASKED_SCORE = -1e30
SCORE_SCALE = 0.125
PRECISE = lax.Precision.HIGHEST
F32 = jnp.float32
BF16 = jnp.bfloat16
GELU_C = 0.7978845608028654
GELU_A = 0.044715
CHUNK = 128


def dot_nn(a, b, precision=None):
    return lax.dot_general(
        a, b, (((1,), (0,)), ((), ())), precision=precision, preferred_element_type=F32
    )


def dot_nt(a, b, precision=None):
    return lax.dot_general(
        a, b, (((1,), (1,)), ((), ())), precision=precision, preferred_element_type=F32
    )


def dot_tn(a, b, precision=None):
    return lax.dot_general(
        a, b, (((0,), (0,)), ((), ())), precision=precision, preferred_element_type=F32
    )


def row_scale(rows):
    return lax.rsqrt(jnp.mean(rows * rows, axis=1, keepdims=True) + EPSILON)


def bucket_marks(bucket_ref, count):
    width = bucket_ref.shape[1]
    return lax.broadcasted_iota(jnp.int32, (count, width), 0) == bucket_ref[...]


def in_order(blocks, rank, place, axis):
    for j, block in enumerate(blocks):
        place[rank ^ j] = block[...]
    return jnp.concatenate([place[r] for r in range(len(blocks))], axis=axis)


def as_column(row):
    return jnp.broadcast_to(row, (128, row.shape[1])).T[:, 0:1]


def softmax_rows(logits):
    shifted = jnp.exp(logits - jnp.max(logits, axis=1, keepdims=True))
    return shifted / jnp.sum(shifted, axis=1, keepdims=True)


def attend_kernel(
    tokens, gain, w_query, w_key, w_value, seg_row, bucket, table,
    normed_out, query_out, key_out, value_out, probs_out, mixed_out, band,
):
    length = tokens.shape[0]
    width = 2 * length
    heads = query_out.shape[1] // HDIM
    rows = tokens[...].astype(F32)
    normed = (rows * row_scale(rows) * gain[...]).astype(BF16)
    normed_out[...] = normed
    query = dot_nt(normed, w_query[...]).astype(BF16)
    key = dot_nt(normed, w_key[...]).astype(BF16)
    value = dot_nt(normed, w_value[...]).astype(BF16)
    query_out[...] = query
    key_out[...] = key
    value_out[...] = value
    marks = bucket_marks(bucket, table.shape[0])
    seg_col = as_column(seg_row[...])
    for h in range(heads):
        cols = slice(h * HDIM, (h + 1) * HDIM)
        offsets = jnp.sum(
            jnp.where(marks, table[:, h : h + 1], 0.0), axis=0, keepdims=True
        )
        base = jnp.concatenate(
            [offsets] + [pltpu.roll(offsets, r, 1) for r in range(1, 8)], axis=0
        )
        for b in range(length // 8):
            turned = pltpu.roll(base, (length + 1 + 8 * b) % width, 1)
            band[8 * b : 8 * b + 8, :] = turned[:, :length]
        for c in range(0, length, CHUNK):
            span = slice(c, c + CHUNK)
            scores = dot_nt(query[span, cols], key[:, cols]) * SCORE_SCALE + band[span, :]
            scores = jnp.where(seg_col[span, :] == seg_row[...], scores, MASKED_SCORE)
            probs = softmax_rows(scores)
            probs_out[h, span, :] = probs
            mixed_out[span, cols] = dot_nn(probs.astype(BF16), value[:, cols]).astype(BF16)


def dispatch(code, rows, outs, transposed=False):
    share = outs[0].shape[0]
    for k, out in enumerate(outs):
        ids = lax.broadcasted_iota(jnp.int32, (share, code.shape[1]), 0) + k * share
        marks = jnp.where(ids == code[...], 1.0, 0.0).astype(BF16)
        product = dot_nt if transposed else dot_nn
        out[...] = product(marks, rows).astype(BF16)


def cotangent_kernel(meta, code, c0, c1, c2, c3, *rest):
    full_out, *outs, place = rest
    turned = in_order((c0, c1, c2, c3), meta[0], place, 0)
    full_out[...] = turned.astype(F32).T.astype(BF16)
    dispatch(code, turned, outs, transposed=True)


def residual_kernel(
    meta, code, route, m0, m1, m2, m3, w0, w1, w2, w3, p0, p1, p2, p3, tokens,
    residual_out, gate_out, probs_out, params_out, *rest,
):
    outs, place = rest[:-1], rest[-1]
    experts = probs_out.shape[1]
    params = in_order((p0, p1, p2, p3), meta[0], place, 1)
    params_out[...] = params
    router = params[:experts]
    gain = params[experts : experts + 1]
    residual = tokens[...].astype(F32)
    for m, w in ((m0, w0), (m1, w1), (m2, w2), (m3, w3)):
        residual = residual + dot_nn(m[...], w[...])
    residual_out[...] = residual
    normed = residual * row_scale(residual) * gain
    dispatch(code, normed.astype(BF16), outs)
    probs = softmax_rows(dot_nt(normed, router, PRECISE))
    probs_out[...] = probs
    lanes = lax.broadcasted_iota(jnp.int32, probs.shape, 1)
    marked = jnp.where(lanes == as_column(route[...]), probs, 0.0)
    gate_out[...] = jnp.sum(marked, axis=1, keepdims=True)


def expert_kernel(
    meta, x0, x1, x2, x3, c0, c1, c2, c3, w_in, w_out, router,
    rows_out, act_out, cots_out, d_hidden_out, keep_out, send_out,
    x_all, c_all, part_all, *, direct,
):
    rank, expert = meta[0], meta[1]
    ranks = 4
    total = rows_out.shape[0]
    feats = rows_out.shape[1]
    cols = feats // ranks
    if direct:
        sources, _, share, _ = x_all.shape
        for j, (x, c) in enumerate(((x0, c0), (x1, c1), (x2, c2), (x3, c3))):
            for s in range(sources):
                x_all[s, rank ^ j] = x[s * share : (s + 1) * share, :]
                c_all[s, rank ^ j] = c[s * share : (s + 1) * share, :]
        step = 256 // (ranks * share)
    else:
        step = 0

    def chunk(i, carry):
        span = pl.ds(pl.multiple_of(i * 256, 256), 256)
        if direct:
            rows = x_all[pl.ds(i * step, step)].reshape(256, feats)
            cots = c_all[pl.ds(i * step, step)].reshape(256, feats)
        else:
            rows = x0[span, :]
            cots = c0[span, :]
        rows_out[span, :] = rows
        probs = softmax_rows(dot_nt(rows, router[...].astype(BF16)))
        lanes = lax.broadcasted_iota(jnp.int32, probs.shape, 1)
        gate = jnp.sum(jnp.where(lanes == expert, probs, 0.0), axis=1, keepdims=True)
        cots_out[span, :] = (gate * cots.astype(F32)).astype(BF16)
        hidden = dot_nn(rows, w_in[...])
        pull = dot_nt(cots, w_out[...])
        bent = jnp.tanh(GELU_C * (hidden + GELU_A * hidden * hidden * hidden))
        act = (0.5 * hidden * (1.0 + bent)).astype(BF16)
        act_out[span, :] = act
        slope = 0.5 * (1.0 + bent) + 0.5 * hidden * (1.0 - bent * bent) * (
            GELU_C * (1.0 + 3.0 * GELU_A * hidden * hidden)
        )
        d_hidden = (gate * pull * slope).astype(BF16)
        d_hidden_out[span, :] = d_hidden
        d_gate = jnp.sum(pull * act.astype(F32), axis=1, keepdims=True)
        d_part = dot_nt(d_hidden, w_in[...]).astype(BF16)
        tail = jnp.broadcast_to(d_gate, (256, part_all.shape[2] - cols)).astype(BF16)
        for r in range(ranks):
            j = rank ^ r
            own = slice(r * cols, (r + 1) * cols)
            part_all[(j % 2) * 2 + j // 2] = jnp.concatenate([d_part[:, own], tail], axis=1)
        keep_out[:, span, :] = part_all[0:2]
        send_out[:, span, :] = part_all[2:4]
        return carry

    lax.fori_loop(0, total // 256, chunk, 0)


def expert_out_kernel(meta, act, w_out, keep_out, send_out, part_all):
    rank = meta[0]
    ranks = 4
    total = act.shape[0]
    feats = w_out.shape[1]
    cols = feats // ranks
    _, sources, half, _ = keep_out.shape
    step = 256 // (2 * half)

    def chunk(i, carry):
        span = pl.ds(pl.multiple_of(i * 256, 256), 256)
        part = dot_nn(act[span, :], w_out[...])
        for r in range(ranks):
            j = rank ^ r
            own = slice(r * cols, (r + 1) * cols)
            for s in range(step):
                low = part[2 * half * s : 2 * half * s + half, own]
                high = part[2 * half * s + half : 2 * half * (s + 1), own]
                part_all[(j % 2) * 2 + j // 2, s] = jnp.concatenate([low, high], axis=1).astype(
                    BF16
                )
        keep_out[:, pl.ds(i * step, step)] = part_all[0:2]
        send_out[:, pl.ds(i * step, step)] = part_all[2:4]
        return carry

    lax.fori_loop(0, total // 256, chunk, 0)


def combine_kernel(code, *rest):
    *blocks, out, came = rest
    cap = blocks[0].shape[0]
    for k, block in enumerate(blocks):
        came[k * cap : (k + 1) * cap, :] = block[...]
    ids = lax.broadcasted_iota(jnp.int32, (code.shape[1], came.shape[0]), 1)
    marks = jnp.where(ids == as_column(code[...]), 1.0, 0.0).astype(BF16)
    out[...] = dot_nn(marks, came[...]).astype(BF16)


def block_out_kernel(meta, code, came, residual, gate, block_out, place):
    rank = meta[0]
    cols = block_out.shape[1]
    count = came.shape[0]
    ids = lax.broadcasted_iota(jnp.int32, (code.shape[1], count), 1)
    where = as_column(code[...])
    low = jnp.where(ids == where, 1.0, 0.0).astype(BF16)
    high = jnp.where(ids + count == where, 1.0, 0.0).astype(BF16)
    returned = dot_nn(low, came[:, :cols]) + dot_nn(high, came[:, cols:])
    for r in range(4):
        place[r] = residual[:, r * cols : (r + 1) * cols]
    block_out[...] = (place[rank] + gate[...] * returned).astype(BF16)


def put_chunks(grads, out_keep, out_send, place, expert, order):
    count = len(order)
    size = grads.shape[0] // count
    for c in range(count):
        place[c ^ expert] = grads[c * size : (c + 1) * size, :]
    half = count // 2
    for i, k in enumerate(order):
        if i < half:
            out_keep[i] = place[k]
        else:
            out_send[i - half] = place[k]


def residual_back_kernel(
    meta, r0, r1, r2, r3, residual, gate, probs, route, params, cotangent, mixed, w_attn_out,
    attn_probs, normed_one, d_attn_cols_out, d_mixed_out, d_value_out, router_grad_out,
    gain_grad_out, *rest, chunked,
):
    *grads_out, place, place_f32, chunk_place = rest
    rank, expert = meta[0], meta[1]
    experts = probs.shape[1]
    feats = residual.shape[1]
    cols = feats // 4
    length = residual.shape[0]
    router = params[:experts, :]
    gain = params[experts : experts + 1, :]
    for j, r in enumerate((r0, r1, r2, r3)):
        place[rank ^ j] = r[:, :cols]
    d_gate = r0[:, cols : cols + 1].astype(F32)
    d_routed = jnp.concatenate([place[r] for r in range(4)], axis=1).astype(F32)
    res = residual[...]
    scale = row_scale(res)
    lanes = lax.broadcasted_iota(jnp.int32, probs.shape, 1)
    onehot = jnp.where(lanes == as_column(route[...]), 1.0, 0.0)
    d_logits = d_gate * probs[...] * (onehot - gate[...])
    d_normed = d_routed + dot_nn(d_logits, router, PRECISE)
    normed = res * scale * gain
    router_grad = dot_tn(d_logits, normed, PRECISE)
    gain_grad = jnp.sum(d_normed * res * scale, axis=0, keepdims=True)
    cross = jnp.sum(gain * res * d_normed, axis=1, keepdims=True)
    d_residual = (
        cotangent[...].astype(F32)
        + scale * gain * d_normed
        - res * (scale * scale * scale * cross * (1.0 / feats))
    )
    for r in range(4):
        own = slice(r * cols, (r + 1) * cols)
        place_f32[r] = d_residual[:, own]

        @pl.when(rank == r)
        def _():
            router_grad_out[...] = router_grad[:, own]
            gain_grad_out[...] = gain_grad[:, own]

    d_attn_cols_out[...] = place_f32[rank]
    d_attn = d_residual.astype(BF16)
    attn_grad = dot_tn(mixed[...], d_attn).astype(BF16)
    d_mixed = dot_nt(d_attn, w_attn_out[...]).astype(BF16)
    d_mixed_out[...] = d_mixed
    for h in range(cols // HDIM):
        own = slice(h * HDIM, (h + 1) * HDIM)
        total = jnp.zeros((length, HDIM), F32)
        for c in range(0, length, CHUNK):
            span = slice(c, c + CHUNK)
            total = total + dot_tn(attn_probs[h, span, :].astype(BF16), d_mixed[span, own])
        d_value_out[:, own] = total.astype(BF16)
    value_grad = dot_tn(d_value_out[...], normed_one[...]).astype(BF16)
    if chunked:
        both = jnp.concatenate([attn_grad, value_grad], axis=0)
        put_chunks(both, *grads_out, chunk_place, expert, chunked)
    else:
        grads_out[0][...] = attn_grad
        grads_out[1][...] = value_grad


def attend_back_kernel(
    meta, tokens, gain, normed, query, key, value, probs, d_mixed, d_value, bucket,
    w_query, w_key, w_value, router_grad, gain2_grad,
    small_out, keep_out, send_out, *rest, buckets, chunked,
):
    *grads_out, d_query, d_key, place, chunk_place = rest
    rank, expert = meta[0], meta[1]
    length = tokens.shape[0]
    width = 2 * length
    heads = query.shape[1] // HDIM
    feats = tokens.shape[1]
    cols = feats // 4
    marks = bucket_marks(bucket, buckets)
    zeros = jnp.zeros((8, width - length), F32)
    table_cols = []
    for h in range(heads):
        own = slice(h * HDIM, (h + 1) * HDIM)
        dk = jnp.zeros((length, HDIM), F32)
        diagonals = jnp.zeros((8, width), F32)
        for c in range(0, length, CHUNK):
            span = slice(c, c + CHUNK)
            weights = probs[h, span, :]
            d_probs = dot_nt(d_mixed[span, own], value[:, own])
            inner = jnp.sum(d_probs * weights, axis=1, keepdims=True)
            d_scores = weights * (d_probs - inner)
            for b in range(CHUNK // 8):
                piece = jnp.concatenate([d_scores[8 * b : 8 * b + 8, :], zeros], axis=1)
                diagonals = diagonals + pltpu.roll(piece, (length - 1 - c - 8 * b) % width, 1)
            low = d_scores.astype(BF16)
            d_query[span, own] = (dot_nn(low, key[:, own]) * SCORE_SCALE).astype(BF16)
            dk = dk + dot_tn(low, query[span, own])
        d_key[:, own] = (dk * SCORE_SCALE).astype(BF16)
        line = diagonals[0:1]
        for r in range(1, 8):
            line = line + pltpu.roll(diagonals[r : r + 1], width - r, 1)
        table_cols.append(jnp.sum(jnp.where(marks, line, 0.0), axis=1, keepdims=True))
    normed_rows = normed[...]
    query_grad = dot_tn(d_query[...], normed_rows).astype(BF16)
    key_grad = dot_tn(d_key[...], normed_rows).astype(BF16)
    if chunked:
        both = jnp.concatenate([query_grad, key_grad], axis=0)
        put_chunks(both, *grads_out, chunk_place, expert, chunked)
    else:
        grads_out[0][...] = query_grad
        grads_out[1][...] = key_grad
    d_normed = (
        dot_nn(d_query[...], w_query[...])
        + dot_nn(d_key[...], w_key[...])
        + dot_nn(d_value[...], w_value[...])
    )
    rows = tokens[...].astype(F32)
    scale = row_scale(rows)
    product = d_normed * rows
    gain1_grad = jnp.sum(product * scale, axis=0, keepdims=True)
    small_out[...] = jnp.zeros(small_out.shape, F32)
    for r in range(4):
        small_out[r : r + 1, :cols] = gain1_grad[:, r * cols : (r + 1) * cols]
    small_out[4:5, :cols] = gain2_grad[...]
    for h in range(heads):
        spread = jnp.broadcast_to(table_cols[h], (buckets, 128)).T
        small_out[8 + h : 9 + h, :buckets] = spread[0:1, :]
    small_out[16 : 16 + router_grad.shape[0], :cols] = router_grad[...]
    cross = jnp.sum(product * gain[...], axis=1, keepdims=True)
    high = cross.astype(BF16).astype(F32)
    low = cross - high
    tail = place.shape[2] - cols
    lanes = lax.broadcasted_iota(jnp.int32, (length, tail), 1)
    extra = jnp.where(lanes == 0, high, jnp.where(lanes == 1, low, 0.0)).astype(BF16)
    for r in range(4):
        j = rank ^ r
        own = d_normed[:, r * cols : (r + 1) * cols].astype(BF16)
        place[(j % 2) * 2 + j // 2] = jnp.concatenate([own, extra], axis=1)
    keep_out[...] = place[0:2]
    send_out[...] = place[2:4]


def input_kernel(meta, tokens, gain, d_attn_cols, first, second, out, place, gain_place):
    rank = meta[0]
    feats = tokens.shape[1]
    cols = feats // 4
    rows = tokens[...].astype(F32)
    scale = row_scale(rows)
    both = first[...].astype(F32) + second[...].astype(F32)
    cross = both[:, cols : cols + 1] + both[:, cols + 1 : cols + 2]
    for r in range(4):
        place[r] = rows[:, r * cols : (r + 1) * cols]
        gain_place[r] = gain[:, r * cols : (r + 1) * cols]
    out[...] = (
        d_attn_cols[...]
        + scale * gain_place[rank] * both[:, :cols]
        - place[rank] * (scale * scale * scale * cross * (1.0 / feats))
    )


def finish_kernel(meta, mine, other, first_out, second_out, place, *, order):
    expert = meta[1]
    count = len(order)
    size = mine.shape[1]
    half = count // 2
    for i, k in enumerate(order):
        place[k] = mine[i] if i < half else other[i - half]
    rows = first_out.shape[0]
    for c in range(count):
        chunk = place[c ^ expert].astype(F32)
        start = c * size
        if start < rows:
            first_out[start : start + size, :] = chunk
        else:
            second_out[start - rows : start - rows + size, :] = chunk


def call(kernel, outs, scratch, *operands, flops=0, moved=0, smem=1):
    specs = [
        pl.BlockSpec(memory_space=pltpu.SMEM if i < smem else pltpu.VMEM)
        for i in range(len(operands))
    ]
    return pl.pallas_call(
        kernel,
        out_shape=[jax.ShapeDtypeStruct(shape, kind) for shape, kind in outs],
        in_specs=specs,
        out_specs=[pl.BlockSpec(memory_space=pltpu.VMEM)] * len(outs),
        scratch_shapes=[pltpu.VMEM(shape, kind) for shape, kind in scratch],
        compiler_params=pltpu.CompilerParams(vmem_limit_bytes=48 * 1024 * 1024),
        cost_estimate=pl.CostEstimate(flops=flops, bytes_accessed=moved, transcendentals=0),
    )(*operands)


def swap(array, axis, bit):
    size = lax.axis_size(axis)
    return lax.ppermute(array, axis, [(i, i ^ bit) for i in range(size)])


def add_low(a, b):
    return (a.astype(F32) + b.astype(F32)).astype(BF16)


def gather_four(array):
    across = swap(array, "tensor", 2)
    beside = swap(array, "tensor", 1)
    return [array, beside, across, swap(across, "tensor", 1)]


def reduce_four(keep, send):
    got = swap(send, "tensor", 1)
    far = swap(add_low(keep[1], got[1]), "tensor", 2)
    return add_low(keep[0], got[0]), far


def exchange(blocks):
    if len(blocks) > 8:
        return hyper_exchange(blocks)
    return [blocks[0]] + [swap(b, "expert", k) for k, b in enumerate(blocks) if k]


def hyper_exchange(blocks):
    count = len(blocks)
    held = {k: [b] for k, b in enumerate(blocks)}
    bit = 1
    while bit < count:
        away = [k for k in sorted(held) if k & bit]
        sent = jnp.concatenate([b for k in away for b in held[k]], axis=0)
        got = swap(sent, "expert", bit)
        size = blocks[0].shape[0]
        at = 0
        fresh = {}
        for k in away:
            pieces = [got[at + i * size : at + (i + 1) * size] for i in range(len(held[k]))]
            at += len(held[k]) * size
            fresh[k ^ bit] = held[k ^ bit] + pieces
        held = fresh
        bit *= 2
    return held[0]


def reduce_chunks(keep, send, bits):
    got = swap(send, "expert", bits[0])
    for bit in bits[1:]:
        half = keep.shape[0] // 2
        sent = add_low(keep[half:], got[half:])
        keep = add_low(keep[:half], got[:half])
        got = swap(sent, "expert", bit)
    mine = add_low(keep, got)
    for bit in bits[:0:-1]:
        mine = jnp.concatenate([mine, swap(mine, "expert", bit)], axis=0)
    return mine, swap(mine, "expert", bits[0])


def chunk_order(bits):
    order = [0]
    for bit in reversed(bits):
        order = order + [k ^ bit for k in order]
    return order


def sum_over(array, axis):
    bit = 1
    while bit < lax.axis_size(axis):
        array = array + swap(array, axis, bit)
        bit *= 2
    return array


def on_device(
    tokens, cotangent, norm1_gain, w_query, w_key, w_value, w_attn_out, bias_table, norm2_gain,
    w_router, expert_in, expert_out, route, slot, segment, rel_bucket,
):
    length, feats = tokens.shape
    cols = cotangent.shape[1]
    heads = cols // HDIM
    experts = lax.axis_size("expert")
    cap = 2 * length // experts
    share = cap // 4
    half = cap // 2
    rank = lax.axis_index("tensor").astype(jnp.int32)
    expert = lax.axis_index("expert").astype(jnp.int32)
    meta = jnp.stack([rank, expert])
    total = experts * cap
    direct = share % 16 == 0
    buckets = bias_table.shape[0]
    first_bits, second_bits = (1, 2, 4), (2, 4, 1)
    chunked = experts == 8
    first_order = chunk_order(first_bits) if chunked else None
    second_order = chunk_order(second_bits) if chunked else None

    relative = route ^ expert
    code = (relative * cap + slot)[None, :]
    half_code = (relative * half + slot % half + (slot // half) * (total // 2))[None, :]
    part_slot = slot - rank * share
    inside = (part_slot >= 0) & (part_slot < share)
    share_code = jnp.where(inside, relative * share + part_slot, -1)[None, :]
    route_row = route[None, :]

    cot_parts = gather_four(cotangent.T)
    cot_full, *cot_blocks = call(
        cotangent_kernel,
        [((length, feats), BF16)] + [((share, feats), BF16)] * experts,
        [((4, cols, length), BF16)],
        meta, share_code, *cot_parts,
        flops=2 * total // 4 * length * feats, moved=4 * length * feats,
    )
    cot_rows = gather_four(jnp.concatenate(hyper_exchange(cot_blocks), axis=0))

    attn_weights = gather_four(w_attn_out)
    pad_rows = -(experts + 1) % 8
    packed_params = jnp.concatenate(
        [w_router.astype(F32).T, norm2_gain[None, :], jnp.zeros((pad_rows, cols), F32)], axis=0
    )
    param_rows = packed_params.shape[0]
    params_parts = gather_four(packed_params)

    gain_row = norm1_gain[None, :]
    bucket_row = jnp.concatenate([rel_bucket, jnp.full((1,), -1, jnp.int32)])[None, :]
    normed, query, key, value, probs, mixed = call(
        attend_kernel,
        [((length, feats), BF16)]
        + [((length, cols), BF16)] * 3
        + [((heads, length, length), F32), ((length, cols), BF16)],
        [((length, length), F32)],
        tokens, gain_row, w_query.T, w_key.T, w_value.T, segment[None, :], bucket_row, bias_table,
        flops=8 * length * feats * cols, moved=8 * length * feats, smem=0,
    )

    mixed_parts = gather_four(mixed)
    residual, gate, router_probs, params, *row_blocks = call(
        residual_kernel,
        [
            ((length, feats), F32),
            ((length, 1), F32),
            ((length, experts), F32),
            ((param_rows, feats), F32),
        ]
        + [((share, feats), BF16)] * experts,
        [((4, param_rows, cols), F32)],
        meta, share_code, route_row, *mixed_parts, *attn_weights, *params_parts, tokens,
        flops=4 * length * feats * feats, moved=8 * length * feats,
    )
    rows = gather_four(jnp.concatenate(exchange(row_blocks), axis=0))

    if not direct:
        def assemble(parts):
            stacked = jnp.stack(parts).reshape(4, experts, share, feats)
            stacked = stacked[rank ^ jnp.arange(4, dtype=jnp.int32)]
            return [jnp.transpose(stacked, (1, 0, 2, 3)).reshape(total, feats)]

        one = jnp.zeros((16, 128), BF16)
        rows = assemble(rows) + [one] * 3
        cot_rows = assemble(cot_rows) + [one] * 3
    w_in, w_out = expert_in[0], expert_out[0]
    hidden_count = w_in.shape[1]
    all_shape = (experts, 4, share, feats) if direct else (1, 1, 16, 128)
    wide = -(-(cols + 2) // 128) * 128
    rows_all, act, cots, d_hidden, keep, send = call(
        functools.partial(expert_kernel, direct=direct),
        [((total, feats), BF16), ((total, hidden_count), BF16), ((total, feats), BF16),
         ((total, hidden_count), BF16), ((2, total, wide), BF16), ((2, total, wide), BF16)],
        [(all_shape, BF16), (all_shape, BF16), ((4, 256, wide), BF16)],
        meta, *rows, *cot_rows, w_in, w_out, params[:experts],
        flops=6 * total * feats * hidden_count, moved=16 * total * feats,
    )
    near, far = reduce_four(keep, send)
    whole = add_low(near, far)
    came = exchange([whole[k * cap : (k + 1) * cap] for k in range(experts)])
    (d_routed,) = call(
        combine_kernel,
        [((length, wide), BF16)],
        [((total, wide), BF16)],
        code, *came,
        flops=2 * length * total * wide, moved=4 * length * feats, smem=0,
    )
    routed_parts = gather_four(d_routed)

    keep_fwd, send_fwd = call(
        expert_out_kernel,
        [((2, experts, half, 2 * cols), BF16)] * 2,
        [((4, 128 // half, half, 2 * cols), BF16)],
        meta, act, w_out,
        flops=2 * total * feats * hidden_count, moved=4 * total * feats,
    )
    near_fwd, far_fwd = reduce_four(keep_fwd, send_fwd)
    whole_fwd = add_low(near_fwd, far_fwd)
    came_fwd = jnp.concatenate(hyper_exchange([whole_fwd[k] for k in range(experts)]), axis=0)
    (block_out,) = call(
        block_out_kernel,
        [((length, cols), BF16)],
        [((4, length, cols), F32)],
        meta, half_code, came_fwd, residual, gate,
        flops=2 * length * total * cols, moved=8 * length * feats,
    )
    expert_out_grad = dot_tn(act, cots)[None]
    expert_in_grad = dot_tn(rows_all, d_hidden)[None]

    if chunked:
        size = 2 * cols // experts
        grad_outs = [((experts // 2, size, feats), BF16)] * 2
        chunk_scratch = ((experts, size, feats), BF16)
    else:
        grad_outs = [((cols, feats), BF16)] * 2
        chunk_scratch = ((16, 128), BF16)
    d_attn_cols, d_mixed, d_value, router_grad, gain2_grad, *first_grads = call(
        functools.partial(residual_back_kernel, chunked=first_order),
        [((length, cols), F32), ((length, cols), BF16), ((length, cols), BF16),
         ((experts, cols), F32), ((1, cols), F32)] + grad_outs,
        [((4, length, cols), BF16), ((4, length, cols), F32), chunk_scratch],
        meta, *routed_parts, residual, gate, router_probs, route_row, params, cot_full, mixed,
        w_attn_out, probs, normed,
        flops=6 * length * feats * cols, moved=12 * length * feats,
    )
    small_rows = 16 + -(-experts // 8) * 8
    small, keep_in, send_in, *second_grads = call(
        functools.partial(attend_back_kernel, buckets=buckets, chunked=second_order),
        [((small_rows, wide), F32)] + [((2, length, wide), BF16)] * 2 + grad_outs,
        [((length, cols), BF16)] * 2 + [((4, length, wide), BF16), chunk_scratch],
        meta, tokens, gain_row, normed, query, key, value, probs, d_mixed, d_value, bucket_row,
        w_query.T, w_key.T, w_value.T, router_grad, gain2_grad,
        flops=16 * length * feats * cols, moved=12 * length * feats,
    )
    near_in, far_in = reduce_four(keep_in, send_in)
    (input_grad,) = call(
        input_kernel,
        [((length, cols), F32)],
        [((4, length, cols), F32), ((4, 1, cols), F32)],
        meta, tokens, gain_row, d_attn_cols, near_in, far_in,
        flops=length * feats, moved=4 * length * feats,
    )

    small = sum_over(small, "expert")
    gain1_grad = sum_over(small[:8], "tensor")
    if chunked:
        grads = []
        for kept, bits, order in (
            (first_grads, first_bits, first_order),
            (second_grads, second_bits, second_order),
        ):
            mine, other = reduce_chunks(*kept, bits)
            grads += call(
                functools.partial(finish_kernel, order=order),
                [((cols, feats), F32)] * 2,
                [chunk_scratch],
                meta, mine, other,
                flops=0, moved=12 * cols * feats,
            )
        attn_grad, value_grad, query_grad, key_grad = grads
    else:
        attn_grad, value_grad, query_grad, key_grad = [
            g.astype(F32) for g in lax.psum((*first_grads, *second_grads), "expert")
        ]
    return (
        block_out,
        input_grad,
        gain1_grad[:4, :cols].reshape(feats),
        query_grad.T,
        key_grad.T,
        value_grad.T,
        attn_grad,
        small[8 : 8 + heads, :buckets].T,
        small[4, :cols],
        small[16 : 16 + experts, :cols].T,
        expert_in_grad,
        expert_out_grad,
    )


def solution(mesh):
    return jax.shard_map(
        on_device,
        mesh=mesh,
        in_specs=(
            P("expert", None),
            P("expert", "tensor"),
            P(),
            P(None, "tensor"),
            P(None, "tensor"),
            P(None, "tensor"),
            P("tensor", None),
            P(None, "tensor"),
            P("tensor"),
            P("tensor", None),
            P("expert", None, "tensor"),
            P("expert", "tensor", None),
            P("expert"),
            P("expert"),
            P("expert"),
            P(),
        ),
        out_specs=(
            P("expert", "tensor"),
            P("expert", "tensor"),
            P(),
            P(None, "tensor"),
            P(None, "tensor"),
            P(None, "tensor"),
            P("tensor", None),
            P(None, "tensor"),
            P("tensor"),
            P("tensor", None),
            P("expert", None, "tensor"),
            P("expert", "tensor", None),
        ),
        check_vma=False,
    )
```

time: 308 us -> 236 us (0.77)
  blocking collectives: 73.9 us -> 0 us
  waiting for transfers between devices: 70 us -> 101 us
  between operations: 14.6 us -> 1.31 us
  local copies, waits for them, and re-layouts: 26.6 us -> 16.3 us
  Pallas kernels: 47.8 us -> 53.2 us
  starting transfers between devices: 60.1 us -> 55.1 us
  other arithmetic: 6.37 us -> 2.23 us
    psum x2 -> x0, blocking collectives: 73.9 us -> none  [the longest x1 37.5 us: on_device(): gain1_grad = lax.psum(gain1_grad, ('expert', 'tensor'))]
    ppermute x46 -> x64, waiting for transfers between devices: 66.9 us -> 101 us  [swap(): return lax.ppermute(array, axis, [(i, i ^ bit) for i in range(size)])]
    unnamed x133 -> x76, local copies, waits for them, and re-layouts: 23 us -> 13 us
    pallas_call x8 -> x12, Pallas kernels: 47.8 us -> 53.2 us  [call(): pl.pallas_call(kernel, out_shape=[jax.ShapeDtypeStruct(shape, kind) for s...]
    ppermute x46 -> x64, starting transfers between devices: 60 us -> 55.1 us  [swap(): return lax.ppermute(array, axis, [(i, i ^ bit) for i in range(size)])]
    psum x1 -> x0, waiting for transfers between devices: 3.09 us -> none  [on_device(): lax.psum((query_grad, key_grad, value_grad), 'expert')]
  transfers between devices with their start and end apart: 47 -> 64, of which waited for: 20 -> 30; matrix products, arithmetic and copies ran while one was open for 6% -> 6% of each run, Pallas kernels for 5% -> 9%
where the time goes in v2:
time: 236 us; the launch traced here: 235 us
  waiting for transfers between devices  101 us (43%)
  starting transfers between devices  55.1 us (23%)
  Pallas kernels  53.2 us (23%)
  local copies, waits for them, and re-layouts  16.3 us (7%)
  matrix products  5.7 us (2%)
    ppermute x64, waiting for transfers between devices, swap(): return lax.ppermute(array, axis, [(i, i ^ bit) for i in range(size)])  101 us
    ppermute x64, starting transfers between devices, swap(): return lax.ppermute(array, axis, [(i, i ^ bit) for i in range(size)])  55.1 us
    pallas_call x12, Pallas kernels, call(): pl.pallas_call(kernel, out_shape=[jax.ShapeDtypeStruct(shape, kind) for s...  53.2 us
    unnamed x76, local copies, waits for them, and re-layouts  13 us
    dot_general x2, matrix products, dot_tn(): lax.dot_general(a, b, (((0,), (0,)), ((), ())), precision=precision, pref...  5.7 us
  transfers between devices with their start and end apart: 64, of which 30 were waited for; matrix products, arithmetic and copies ran while one was open for 6% of the time, Pallas kernels for 9%

profile of v2, /device:TPU:0, one launch (start us, length us, event | category | flops | bytes accessed | tf_op | source)
XLA Modules:
  0.0 235.1 jit_solution(6377679631087266024)
XLA Ops:
  0.7 3.0 %collective-permute-start.20 = (bf16[192,512]{1,0:T(8,128)(2,1)}, bf16[192,512]{1,0:T(8,128)(2,1)S(1)}, u32[]{:S(2)}, u32[]{:S(2)}) collective-permute-start(bf16[192,512]{1,0:T(8,128)(2,1)} %bitcast.73), channel_id=1, source_target_pairs={{0,2},{1,3},{2,0},{3,1},{4,6},{5,7},{6,4},{7,5},{8,10},{9,11},{10,... | collective-permute-start | bytes 589832 | tf_op jit(solution)/shard_map/ppermute | solution.py:454
  6.1 1.1 copy-done.2
  7.2 1.0 copy-done.5
  8.2 1.0 copy-done.7
  9.1 1.0 copy-done.9
  10.8 7.1 %shard_map.247 = (bf16[512,768]{1,0:T(8,128)(2,1)S(1)}, bf16[512,192]{1,0:T(8,128)(2,1)S(1)}, bf16[512,192]{1,0:T(8,128)(2,1)S(1)}, bf16[512,192]{1,0:T(8,128)(2...) custom-call(bf16[512,768]{1,0:T(8,128)(2,1)S(1)} %copy-done.2, f32[1,768]{1,0:T(1,128)S(1)} %broadcast_in_dim.38.gain, ...), custom_call_target="tpu_custom_call" | custom-call | flops 603979776 | bytes 3145728 | tf_op jit(solution)/shard_map/pallas_call | solution.py:441
  19.3 1.9 collective-permute-start.1
  21.5 1.4 collective-permute-done.21.c3
  22.9 2.5 %shard_map.249 = (bf16[512,768]{1,0:T(8,128)(2,1)S(1)}, bf16[32,768]{1,0:T(8,128)(2,1)S(1)}, bf16[32,768]{1,0:T(8,128)(2,1)S(1)}, bf16[32,768]{1,0:T(8,128)(2,1)...) custom-call(s32[2]{0:T(128)S(1)} %pad_add_fusion.1.meta, ...), custom_call_target="tpu_custom_call" | custom-call | flops 201326592 | bytes 1572864 | tf_op jit(solution)/shard_map/pallas_call | solution.py:441
  25.4 1.6 collective-permute-start.22
  27.6 3.2 %collective-permute-done.7.p2 = f32[16,192]{1,0:T(8,128)S(1)} collective-permute-done((f32[16,192]{1,0:T(8,128)S(1)}, f32[16,192]{1,0:T(8,128)S(1)}, u32[]{:S(2)}, u32[]{:S(2)}) %collective-permute-start.7) | collective-permute-done | bytes 12320 | tf_op jit(solution)/shard_map/ppermute | solution.py:454
  31.4 1.0 collective-permute-done.22
  33.1 1.0 collective-permute-done.8.p3
  34.1 1.6 collective-permute-start.23
  35.7 0.9 copy-done.23
  36.6 5.8 %shard_map.248 = (f32[512,768]{1,0:T(8,128)S(1)}, f32[512,1]{1,0:T(8,128)S(1)}, f32[512,8]{1,0:T(8,128)S(1)}, f32[16,768]{1,0:T(8,128)S(1)}, bf16[32,768]{1,0:T(...) custom-call(s32[2]{0:T(128)S(1)} %pad_add_fusion.1.meta, ...), custom_call_target="tpu_custom_call" | custom-call | flops 1207959552 | bytes 3145728 | tf_op jit(solution)/shard_map/pallas_call | solution.py:441
  42.5 1.2 copy-done
  43.7 1.5 collective-permute-start.9
  45.6 1.6 collective-permute-start.11
  47.2 2.6 %collective-permute-start.12 = (bf16[32,768]{1,0:T(8,128)(2,1)S(1)}, bf16[32,768]{1,0:T(8,128)(2,1)S(1)}, u32[]{:S(2)}, u32[]{:S(2)}) collective-permute-start(bf16[32,768]{1,0:T(8,128)(2,1)S(1)} %get-tuple-element.68), channel_id=1, source_target_pairs={{0,16},{4,20},{8,24},{12,28},{16,0},{20,4},{24,8},{28,12},{1,17},{... | collective-permute-start | bytes 147464 | tf_op jit(solution)/shard_map/ppermute | solution.py:454
  49.8 1.5 collective-permute-start.13
  51.3 2.3 collective-permute-start.14
  53.6 1.6 collective-permute-start.15
  55.2 1.5 collective-permute-done.13
  56.8 3.2 %collective-permute-start.24 = (bf16[128,768]{1,0:T(8,128)(2,1)S(1)}, bf16[128,768]{1,0:T(8,128)(2,1)S(1)}, u32[]{:S(2)}, u32[]{:S(2)}) collective-permute-start(bf16[128,768]{1,0:T(8,128)(2,1)S(1)} %pad_maximum_fusion.6), channel_id=1, source_target_pairs={{0,16},{4,20},{8,24},{12,28},{16,0},{20,4},{24,8},{28,12},{1,17},{... | collective-permute-start | bytes 589832 | tf_op jit(solution)/shard_map/ppermute | solution.py:454
  61.0 6.6 %collective-permute-done.24 = bf16[128,768]{1,0:T(8,128)(2,1)S(1)} collective-permute-done((bf16[128,768]{1,0:T(8,128)(2,1)S(1)}, bf16[128,768]{1,0:T(8,128)(2,1)S(1)}, u32[]{:S(2)}, u32[]{:S(2)}) %collective-permute-start.24) | collective-permute-done | bytes 196640 | tf_op jit(solution)/shard_map/ppermute | solution.py:454
  68.8 8.9 %collective-permute-done.26.c2 = bf16[256,768]{1,0:T(8,128)(2,1)S(1)} collective-permute-done((bf16[256,768]{1,0:T(8,128)(2,1)S(1)}, bf16[256,768]{1,0:T(8,128)(2,1)S(1)}, u32[]{:S(2)}, u32[]{:S(2)}) %collective-permute-start.26) | collective-permute-done | bytes 393248 | tf_op jit(solution)/shard_map/ppermute | solution.py:454
  77.7 1.7 collective-permute-done.27.c3
  79.4 11.0 %shard_map.250 = (bf16[1024,768]{1,0:T(8,128)(2,1)}, bf16[1024,768]{1,0:T(8,128)(2,1)}, bf16[1024,768]{1,0:T(8,128)(2,1)}, bf16[1024,768]{1,0:T(8,128)(2,1)}, bf...) custom-call(s32[2]{0:T(128)S(1)} %pad_add_fusion.1.meta, ...), custom_call_target="tpu_custom_call" | custom-call | flops 3623878656 | bytes 12582912 | tf_op jit(solution)/shard_map/pallas_call | solution.py:441
  90.4 1.4 copy-done.25
  91.8 2.9 %shard_map.251 = (bf16[2,8,64,384]{3,2,1,0:T(8,128)(2,1)S(1)}, bf16[2,8,64,384]{3,2,1,0:T(8,128)(2,1)S(1)}) custom-call(s32[2]{0:T(128)S(1)} %pad_add_fusion.1.meta, bf16[1024,768]{1,0:T(8,128)(2,1)S(1)} %copy-done.25, bf16[768,768]{1,0:T(8,128)(2,1)S(1)} %bitcast.85), custom_call_target="tpu_custom_call" | custom-call | flops 1207959552 | bytes 3145728 | tf_op jit(solution)/shard_map/pallas_call | solution.py:441
  95.3 1.8 collective-permute-done.28
  99.5 9.7 %collective-permute-done.29 = bf16[8,64,384]{2,1,0:T(8,128)(2,1)S(1)} collective-permute-done((bf16[8,64,384]{2,1,0:T(8,128)(2,1)S(1)}, bf16[8,64,384]{2,1,0:T(8,128)(2,1)S(1)}, u32[]{:S(2)}, u32[]{:S(2)}) %collective-permute-start.29) | collective-permute-done | bytes 393248 | tf_op jit(solution)/shard_map/ppermute | solution.py:454
  109.5 2.8 %collective-permute-start.30 = (bf16[256,384]{1,0:T(8,128)(2,1)S(1)}, bf16[256,384]{1,0:T(8,128)(2,1)S(1)}, u32[]{:S(2)}, u32[]{:S(2)}) collective-permute-start(bf16[256,384]{1,0:T(8,128)(2,1)S(1)} %pad_maximum_fusion.7), channel_id=1, source_target_pairs={{0,4},{4,0},{8,12},{12,8},{16,20},{20,16},{24,28},{28,24},{1,5},{5... | collective-permute-start | bytes 589832 | tf_op jit(solution)/shard_map/ppermute | solution.py:454
  112.3 7.3 %collective-permute-done.34 = bf16[1024,256]{1,0:T(8,128)(2,1)S(1)} collective-permute-done((bf16[1024,256]{1,0:T(8,128)(2,1)S(1)}, bf16[1024,256]{1,0:T(8,128)(2,1)S(1)}, u32[]{:S(2)}, u32[]{:S(2)}) %collective-permute-start.34) | collective-permute-done | bytes 524320 | tf_op jit(solution)/shard_map/ppermute | solution.py:454
  119.9 1.1 collective-permute-start.41
  121.0 5.0 %collective-permute-start.40 = (bf16[128,256]{1,0:T(8,128)(2,1)S(1)}, bf16[128,256]{1,0:T(8,128)(2,1)S(1)}, u32[]{:S(2)}, u32[]{:S(2)}) collective-permute-start(bf16[128,256]{1,0:T(8,128)(2,1)S(1)} %get-tuple-element.133), channel_id=1, source_target_pairs={{0,24},{4,28},{8,16},{12,20},{16,8},{20,12},{24,0},{28,4},{1,25},{... | collective-permute-start | bytes 196616 | tf_op jit(solution)/shard_map/ppermute | solution.py:454
  126.0 2.5 %collective-permute-start.39 = (bf16[128,256]{1,0:T(8,128)(2,1)S(1)}, bf16[128,256]{1,0:T(8,128)(2,1)S(1)}, u32[]{:S(2)}, u32[]{:S(2)}) collective-permute-start(bf16[128,256]{1,0:T(8,128)(2,1)S(1)} %get-tuple-element.134), channel_id=1, source_target_pairs={{0,20},{4,16},{8,28},{12,24},{16,4},{20,0},{24,12},{28,8},{1,21},{... | collective-permute-start | bytes 196616 | tf_op jit(solution)/shard_map/ppermute | solution.py:454
  128.5 2.9 %collective-permute-start.37 = (bf16[128,256]{1,0:T(8,128)(2,1)S(1)}, bf16[128,256]{1,0:T(8,128)(2,1)S(1)}, u32[]{:S(2)}, u32[]{:S(2)}) collective-permute-start(bf16[128,256]{1,0:T(8,128)(2,1)S(1)} %get-tuple-element.136), channel_id=1, source_target_pairs={{0,12},{4,8},{8,4},{12,0},{16,28},{20,24},{24,20},{28,16},{1,13},{... | collective-permute-start | bytes 196616 | tf_op jit(solution)/shard_map/ppermute | solution.py:454
  131.4 2.8 %collective-permute-start.36 = (bf16[128,256]{1,0:T(8,128)(2,1)S(1)}, bf16[128,256]{1,0:T(8,128)(2,1)S(1)}, u32[]{:S(2)}, u32[]{:S(2)}) collective-permute-start(bf16[128,256]{1,0:T(8,128)(2,1)S(1)} %get-tuple-element.137), channel_id=1, source_target_pairs={{0,8},{4,12},{8,0},{12,4},{16,24},{20,28},{24,16},{28,20},{1,9},{5... | collective-permute-start | bytes 196616 | tf_op jit(solution)/shard_map/ppermute | solution.py:454
  134.1 2.6 %collective-permute-done.39.rest_5_ = bf16[128,256]{1,0:T(8,128)(2,1)S(1)} collective-permute-done((bf16[128,256]{1,0:T(8,128)(2,1)S(1)}, bf16[128,256]{1,0:T(8,128)(2,1)S(1)}, u32[]{:S(2)}, u32[]{:S(2)}) %collective-permute-start.39) | collective-permute-done | bytes 65568 | tf_op jit(solution)/shard_map/ppermute | solution.py:454
  137.9 3.2 %collective-permute-done.35.rest_1_ = bf16[128,256]{1,0:T(8,128)(2,1)S(1)} collective-permute-done((bf16[128,256]{1,0:T(8,128)(2,1)S(1)}, bf16[128,256]{1,0:T(8,128)(2,1)S(1)}, u32[]{:S(2)}, u32[]{:S(2)}) %collective-permute-start.35) | collective-permute-done | bytes 65568 | tf_op jit(solution)/shard_map/ppermute | solution.py:454
  142.6 5.7 %collective-permute-done.43.r2 = bf16[512,256]{1,0:T(8,128)(2,1)S(1)} collective-permute-done((bf16[512,256]{1,0:T(8,128)(2,1)S(1)}, bf16[512,256]{1,0:T(8,128)(2,1)S(1)}, u32[]{:S(2)}, u32[]{:S(2)}) %collective-permute-start.43) | collective-permute-done | bytes 262176 | tf_op jit(solution)/shard_map/ppermute | solution.py:454
  148.2 2.8 %convolution_bitcast_fusion = f32[1,768,768]{2,1,0:T(8,128)} fusion(bf16[1024,768]{1,0:T(8,128)(2,1)S(1)} %copy-done.26, bf16[1024,768]{1,0:T(8,128)(2,1)S(1)} %copy-done.32), kind=kOutput, calls=%fused_computation | convolution fusion | flops 1207959552 | bytes 5505024 | tf_op jit(solution)/shard_map/dot_general | solution.py:35
  151.2 8.0 %shard_map.254 = (f32[512,192]{1,0:T(8,128)S(1)}, bf16[512,192]{1,0:T(8,128)(2,1)S(1)}, bf16[512,192]{1,0:T(8,128)(2,1)S(1)}, f32[8,192]{1,0:T(8,128)S(1)}, f32[...) custom-call(s32[2]{0:T(128)S(1)} %pad_add_fusion.1.meta, ...), custom_call_target="tpu_custom_call" | custom-call | flops 452984832 | bytes 4718592 | tf_op jit(solution)/shard_map/pallas_call | solution.py:441
  159.9 9.4 %shard_map.255 = (f32[24,256]{1,0:T(8,128)S(1)}, bf16[2,512,256]{2,1,0:T(8,128)(2,1)S(1)}, bf16[2,512,256]{2,1,0:T(8,128)(2,1)S(1)}, bf16[4,48,768]{2,1,0:T(8,128)(2,1)S(1)}, bf16[4,48,768]{2,1,0:T(8,128)(2,1)S(1)}) custom-call(s32[2]{0:T(128)S(1)} %pad_add_fusion.1.meta, bf16[512,768]{1,0:T(8,128)(2,1)S(1)} %copy-done.3, ...), custom_call_target="tpu_custom_call" | custom-call | flops 1207959552 | bytes 4718592 | tf_op jit(solution)/shard_map/pallas_call | solution.py:441
  170.2 3.1 %collective-permute-done.47 = f32[24,256]{1,0:T(8,128)S(1)} collective-permute-done((f32[24,256]{1,0:T(8,128)S(1)}, f32[24,256]{1,0:T(8,128)S(1)}, u32[]{:S(2)}, u32[]{:S(2)}) %collective-permute-start.47) | collective-permute-done | bytes 24608 | tf_op jit(solution)/shard_map/ppermute | solution.py:454
  173.3 2.9 %convolution_bitcast_fusion.1 = f32[1,768,768]{2,1,0:T(8,128)} fusion(bf16[1024,768]{1,0:T(8,128)(2,1)S(1)} %copy-done.30, bf16[1024,768]{1,0:T(8,128)(2,1)S(1)} %copy-done.31), kind=kOutput, calls=%fused_computation.1 | convolution fusion | flops 1207959552 | bytes 5505024 | tf_op jit(solution)/shard_map/dot_general | solution.py:35
  176.2 0.9 collective-permute-done.48
  177.1 1.8 collective-permute-start.49
  179.0 3.7 %collective-permute-done.32 = bf16[256,384]{1,0:T(8,128)(2,1)S(1)} collective-permute-done((bf16[256,384]{1,0:T(8,128)(2,1)S(1)}, bf16[256,384]{1,0:T(8,128)(2,1)S(1)}, u32[]{:S(2)}, u32[]{:S(2)}) %collective-permute-start.32) | collective-permute-done | bytes 196640 | tf_op jit(solution)/shard_map/ppermute | solution.py:454
  182.7 1.2 shard_map.252
  187.2 6.4 %collective-permute-done.52 = bf16[4,48,768]{2,1,0:T(8,128)(2,1)S(1)} collective-permute-done((bf16[4,48,768]{2,1,0:T(8,128)(2,1)}, bf16[4,48,768]{2,1,0:T(8,128)(2,1)S(1)}, u32[]{:S(2)}, u32[]{:S(2)}) %collective-permute-start.52) | collective-permute-done | bytes 294944 | tf_op jit(solution)/shard_map/ppermute | solution.py:454
  193.9 1.8 collective-permute-start.59
  195.7 6.7 %collective-permute-done.53 = bf16[2,48,768]{2,1,0:T(8,128)(2,1)S(1)} collective-permute-done((bf16[2,48,768]{2,1,0:T(8,128)(2,1)S(1)}, bf16[2,48,768]{2,1,0:T(8,128)(2,1)S(1)}, u32[]{:S(2)}, u32[]{:S(2)}) %collective-permute-start.53) | collective-permute-done | bytes 147488 | tf_op jit(solution)/shard_map/ppermute | solution.py:454
  203.3 3.6 %collective-permute-done.54 = bf16[1,48,768]{2,1,0:T(8,128)(2,1)S(1)} collective-permute-done((bf16[1,48,768]{2,1,0:T(8,128)(2,1)S(1)}, bf16[1,48,768]{2,1,0:T(8,128)(2,1)S(1)}, u32[]{:S(2)}, u32[]{:S(2)}) %collective-permute-start.54) | collective-permute-done | bytes 73760 | tf_op jit(solution)/shard_map/ppermute | solution.py:454
  208.7 2.6 %collective-permute-done.55 = bf16[1,48,768]{2,1,0:T(8,128)(2,1)S(1)} collective-permute-done((bf16[1,48,768]{2,1,0:T(8,128)(2,1)S(1)}, bf16[1,48,768]{2,1,0:T(8,128)(2,1)S(1)}, u32[]{:S(2)}, u32[]{:S(2)}) %collective-permute-start.55) | collective-permute-done | bytes 73760 | tf_op jit(solution)/shard_map/ppermute | solution.py:454
  211.7 6.4 %collective-permute-done.61 = bf16[1,48,768]{2,1,0:T(8,128)(2,1)S(1)} collective-permute-done((bf16[1,48,768]{2,1,0:T(8,128)(2,1)S(1)}, bf16[1,48,768]{2,1,0:T(8,128)(2,1)S(1)}, u32[]{:S(2)}, u32[]{:S(2)}) %collective-permute-start.61) | collective-permute-done | bytes 73760 | tf_op jit(solution)/shard_map/ppermute | solution.py:454
  218.8 2.0 collective-permute-done.56
  220.9 3.7 %collective-permute-done.62 = bf16[2,48,768]{2,1,0:T(8,128)(2,1)S(1)} collective-permute-done((bf16[2,48,768]{2,1,0:T(8,128)(2,1)S(1)}, bf16[2,48,768]{2,1,0:T(8,128)(2,1)S(1)}, u32[]{:S(2)}, u32[]{:S(2)}) %collective-permute-start.62) | collective-permute-done | bytes 147488 | tf_op jit(solution)/shard_map/ppermute | solution.py:454
  227.3 1.1 shard_map.256
  229.3 2.5 %collective-permute-done.63.other = bf16[4,48,768]{2,1,0:T(8,128)(2,1)S(1)} collective-permute-done((bf16[4,48,768]{2,1,0:T(8,128)(2,1)S(1)}, bf16[4,48,768]{2,1,0:T(8,128)(2,1)S(1)}, u32[]{:S(2)}, u32[]{:S(2)}) %collective-permute-start.63) | collective-permute-done | bytes 294944 | tf_op jit(solution)/shard_map/ppermute | solution.py:454
  231.8 1.6 shard_map.258
  233.5 1.6 shard_map.257
  (203 shorter events, 27.9 us)
Async XLA Ops:
  0.7 20.7 %collective-permute-start.20 = (bf16[192,512]{1,0:T(8,128)(2,1)}, bf16[192,512]{1,0:T(8,128)(2,1)S(1)}, u32[]{:S(2)}, u32[]{:S(2)}) collective-permute-start(bf16[192,512]{1,0:T(8,128)(2,1)} %bitcast.73), channel_id=1, source_target_pairs={{0,2},{1,3},{2,0},{3,1},{4,6},{5,7},{6,4},{7,5},{8,10},{9,11},{10,... | collective-permute-start | bytes 589832 | tf_op jit(solution)/shard_map/ppermute | solution.py:454
  3.7 17.8 %collective-permute-start.19 = (bf16[192,512]{1,0:T(8,128)(2,1)}, bf16[192,512]{1,0:T(8,128)(2,1)S(1)}, u32[]{:S(2)}, u32[]{:S(2)}) collective-permute-start(bf16[192,512]{1,0:T(8,128)(2,1)} %bitcast.74), channel_id=1, source_target_pairs={{0,1},{1,0},{2,3},{3,2},{4,5},{5,4},{6,7},{7,6},{8,9},{9,8},{10,11... | collective-permute-start | bytes 589832 | tf_op jit(solution)/shard_map/ppermute | solution.py:454
  3.7 27.6 %collective-permute-start.4 = (bf16[192,768]{1,0:T(8,128)(2,1)}, bf16[192,768]{1,0:T(8,128)(2,1)}, u32[]{:S(2)}, u32[]{:S(2)}) collective-permute-start(bf16[192,768]{1,0:T(8,128)(2,1)} %w_attn_out.1), channel_id=1, source_target_pairs={{0,2},{1,3},{2,0},{3,1},{4,6},{5,7},{6,4},{7,5},{8,10},{9,11},{10,... | collective-permute-start | bytes 884744 | tf_op jit(solution)/shard_map/ppermute | solution.py:454
  19.3 11.5 %collective-permute-start.1 = (bf16[512,192]{1,0:T(8,128)(2,1)S(1)}, bf16[512,192]{1,0:T(8,128)(2,1)S(1)}, u32[]{:S(2)}, u32[]{:S(2)}) collective-permute-start(bf16[512,192]{1,0:T(8,128)(2,1)S(1)} %get-tuple-element.63.m0.mixed), channel_id=1, source_target_pairs={{0,2},{1,3},{2,0},{3,1},{4,6},{5,7},{6,4},{7,5},{8,10},{9,11},{10,... | collective-permute-start | bytes 589832 | tf_op jit(solution)/shard_map/ppermute | solution.py:454
  21.4 1.5 collective-permute-start.21
  25.4 7.0 %collective-permute-start.22 = (bf16[128,768]{1,0:T(8,128)(2,1)S(1)}, bf16[128,768]{1,0:T(8,128)(2,1)S(1)}, u32[]{:S(2)}, u32[]{:S(2)}) collective-permute-start(bf16[128,768]{1,0:T(8,128)(2,1)S(1)} %pad_maximum_fusion.4), channel_id=1, source_target_pairs={{0,4},{4,0},{8,12},{12,8},{16,20},{20,16},{24,28},{28,24},{1,5},{5... | collective-permute-start | bytes 589832 | tf_op jit(solution)/shard_map/ppermute | solution.py:454
  27.1 3.7 %collective-permute-start.7 = (f32[16,192]{1,0:T(8,128)S(1)}, f32[16,192]{1,0:T(8,128)S(1)}, u32[]{:S(2)}, u32[]{:S(2)}) collective-permute-start(f32[16,192]{1,0:T(8,128)S(1)} %maximum_maximum_fusion.p0), channel_id=1, source_target_pairs={{0,2},{1,3},{2,0},{3,1},{4,6},{5,7},{6,4},{7,5},{8,10},{9,11},{10,... | collective-permute-start | bytes 36872 | tf_op jit(solution)/shard_map/ppermute | solution.py:454
  27.6 4.9 %collective-permute-start.6 = (f32[16,192]{1,0:T(8,128)S(1)}, f32[16,192]{1,0:T(8,128)S(1)}, u32[]{:S(2)}, u32[]{:S(2)}) collective-permute-start(f32[16,192]{1,0:T(8,128)S(1)} %maximum_maximum_fusion.p0), channel_id=1, source_target_pairs={{0,1},{1,0},{2,3},{3,2},{4,5},{5,4},{6,7},{7,6},{8,9},{9,8},{10,11... | collective-permute-start | bytes 36872 | tf_op jit(solution)/shard_map/ppermute | solution.py:454
  30.8 4.8 %collective-permute-start.3 = (bf16[192,768]{1,0:T(8,128)(2,1)S(1)}, bf16[192,768]{1,0:T(8,128)(2,1)S(1)}, u32[]{:S(2)}, u32[]{:S(2)}) collective-permute-start(bf16[192,768]{1,0:T(8,128)(2,1)S(1)} %copy-done.4), channel_id=1, source_target_pairs={{0,1},{1,0},{2,3},{3,2},{4,5},{5,4},{6,7},{7,6},{8,9},{9,8},{10,11... | collective-permute-start | bytes 884744 | tf_op jit(solution)/shard_map/ppermute | solution.py:454
  30.8 4.8 %collective-permute-start = (bf16[512,192]{1,0:T(8,128)(2,1)S(1)}, bf16[512,192]{1,0:T(8,128)(2,1)S(1)}, u32[]{:S(2)}, u32[]{:S(2)}) collective-permute-start(bf16[512,192]{1,0:T(8,128)(2,1)S(1)} %get-tuple-element.63.m0.mixed), channel_id=1, source_target_pairs={{0,1},{1,0},{2,3},{3,2},{4,5},{5,4},{6,7},{7,6},{8,9},{9,8},{10,11... | collective-permute-start | bytes 589832 | tf_op jit(solution)/shard_map/ppermute | solution.py:454
  31.3 4.3 %collective-permute-start.2 = (bf16[512,192]{1,0:T(8,128)(2,1)S(1)}, bf16[512,192]{1,0:T(8,128)(2,1)S(1)}, u32[]{:S(2)}, u32[]{:S(2)}) collective-permute-start(bf16[512,192]{1,0:T(8,128)(2,1)S(1)} %collective-permute-done.1.m2), channel_id=1, source_target_pairs={{0,1},{1,0},{2,3},{3,2},{4,5},{5,4},{6,7},{7,6},{8,9},{9,8},{10,11... | collective-permute-start | bytes 589832 | tf_op jit(solution)/shard_map/ppermute | solution.py:454
  32.5 3.2 %collective-permute-start.5 = (bf16[192,768]{1,0:T(8,128)(2,1)}, bf16[192,768]{1,0:T(8,128)(2,1)S(1)}, u32[]{:S(2)}, u32[]{:S(2)}) collective-permute-start(bf16[192,768]{1,0:T(8,128)(2,1)} %collective-permute-done.4.w2), channel_id=1, source_target_pairs={{0,1},{1,0},{2,3},{3,2},{4,5},{5,4},{6,7},{7,6},{8,9},{9,8},{10,11... | collective-permute-start | bytes 884744 | tf_op jit(solution)/shard_map/ppermute | solution.py:454
  32.5 1.6 collective-permute-start.8
  34.1 22.7 %collective-permute-start.23 = (bf16[128,768]{1,0:T(8,128)(2,1)S(1)}, bf16[128,768]{1,0:T(8,128)(2,1)S(1)}, u32[]{:S(2)}, u32[]{:S(2)}) collective-permute-start(bf16[128,768]{1,0:T(8,128)(2,1)S(1)} %pad_maximum_fusion.5), channel_id=1, source_target_pairs={{0,8},{4,12},{8,0},{12,4},{16,24},{20,28},{24,16},{28,20},{1,9},{5... | collective-permute-start | bytes 589832 | tf_op jit(solution)/shard_map/ppermute | solution.py:454
  43.7 6.1 %collective-permute-start.9 = (bf16[32,768]{1,0:T(8,128)(2,1)S(1)}, bf16[32,768]{1,0:T(8,128)(2,1)S(1)}, u32[]{:S(2)}, u32[]{:S(2)}) collective-permute-start(bf16[32,768]{1,0:T(8,128)(2,1)S(1)} %get-tuple-element.65), channel_id=1, source_target_pairs={{0,4},{4,0},{8,12},{12,8},{16,20},{20,16},{24,28},{28,24},{1,5},{5... | collective-permute-start | bytes 147464 | tf_op jit(solution)/shard_map/ppermute | solution.py:454
  45.2 6.1 %collective-permute-start.10 = (bf16[32,768]{1,0:T(8,128)(2,1)S(1)}, bf16[32,768]{1,0:T(8,128)(2,1)S(1)}, u32[]{:S(2)}, u32[]{:S(2)}) collective-permute-start(bf16[32,768]{1,0:T(8,128)(2,1)S(1)} %get-tuple-element.66), channel_id=1, source_target_pairs={{0,8},{4,12},{8,0},{12,4},{16,24},{20,28},{24,16},{28,20},{1,9},{5... | collective-permute-start | bytes 147464 | tf_op jit(solution)/shard_map/ppermute | solution.py:454
  45.6 8.0 %collective-permute-start.11 = (bf16[32,768]{1,0:T(8,128)(2,1)S(1)}, bf16[32,768]{1,0:T(8,128)(2,1)S(1)}, u32[]{:S(2)}, u32[]{:S(2)}) collective-permute-start(bf16[32,768]{1,0:T(8,128)(2,1)S(1)} %get-tuple-element.67), channel_id=1, source_target_pairs={{0,12},{4,8},{8,4},{12,0},{16,28},{20,24},{24,20},{28,16},{1,13},{... | collective-permute-start | bytes 147464 | tf_op jit(solution)/shard_map/ppermute | solution.py:454
  47.2 8.1 %collective-permute-start.12 = (bf16[32,768]{1,0:T(8,128)(2,1)S(1)}, bf16[32,768]{1,0:T(8,128)(2,1)S(1)}, u32[]{:S(2)}, u32[]{:S(2)}) collective-permute-start(bf16[32,768]{1,0:T(8,128)(2,1)S(1)} %get-tuple-element.68), channel_id=1, source_target_pairs={{0,16},{4,20},{8,24},{12,28},{16,0},{20,4},{24,8},{28,12},{1,17},{... | collective-permute-start | bytes 147464 | tf_op jit(solution)/shard_map/ppermute | solution.py:454
  49.8 7.0 %collective-permute-start.13 = (bf16[32,768]{1,0:T(8,128)(2,1)S(1)}, bf16[32,768]{1,0:T(8,128)(2,1)S(1)}, u32[]{:S(2)}, u32[]{:S(2)}) collective-permute-start(bf16[32,768]{1,0:T(8,128)(2,1)S(1)} %get-tuple-element.69), channel_id=1, source_target_pairs={{0,20},{4,16},{8,28},{12,24},{16,4},{20,0},{24,12},{28,8},{1,21},{... | collective-permute-start | bytes 147464 | tf_op jit(solution)/shard_map/ppermute | solution.py:454
  51.3 8.7 %collective-permute-start.14 = (bf16[32,768]{1,0:T(8,128)(2,1)S(1)}, bf16[32,768]{1,0:T(8,128)(2,1)S(1)}, u32[]{:S(2)}, u32[]{:S(2)}) collective-permute-start(bf16[32,768]{1,0:T(8,128)(2,1)S(1)} %get-tuple-element.70), channel_id=1, source_target_pairs={{0,24},{4,28},{8,16},{12,20},{16,8},{20,12},{24,0},{28,4},{1,25},{... | collective-permute-start | bytes 147464 | tf_op jit(solution)/shard_map/ppermute | solution.py:454
  53.6 6.9 %collective-permute-start.15 = (bf16[32,768]{1,0:T(8,128)(2,1)S(1)}, bf16[32,768]{1,0:T(8,128)(2,1)S(1)}, u32[]{:S(2)}, u32[]{:S(2)}) collective-permute-start(bf16[32,768]{1,0:T(8,128)(2,1)S(1)} %get-tuple-element.71), channel_id=1, source_target_pairs={{0,28},{4,24},{8,20},{12,16},{16,12},{20,8},{24,4},{28,0},{1,29},{... | collective-permute-start | bytes 147464 | tf_op jit(solution)/shard_map/ppermute | solution.py:454
  56.8 10.9 %collective-permute-start.24 = (bf16[128,768]{1,0:T(8,128)(2,1)S(1)}, bf16[128,768]{1,0:T(8,128)(2,1)S(1)}, u32[]{:S(2)}, u32[]{:S(2)}) collective-permute-start(bf16[128,768]{1,0:T(8,128)(2,1)S(1)} %pad_maximum_fusion.6), channel_id=1, source_target_pairs={{0,16},{4,20},{8,24},{12,28},{16,0},{20,4},{24,8},{28,12},{1,17},{... | collective-permute-start | bytes 589832 | tf_op jit(solution)/shard_map/ppermute | solution.py:454
  60.5 8.3 %collective-permute-start.17 = (bf16[256,768]{1,0:T(8,128)(2,1)S(1)}, bf16[256,768]{1,0:T(8,128)(2,1)S(1)}, u32[]{:S(2)}, u32[]{:S(2)}) collective-permute-start(bf16[256,768]{1,0:T(8,128)(2,1)S(1)} %constant_dynamic-update-slice_fusion.x0), channel_id=1, source_target_pairs={{0,2},{1,3},{2,0},{3,1},{4,6},{5,7},{6,4},{7,5},{8,10},{9,11},{10,... | collective-permute-start | bytes 1179656 | tf_op jit(solution)/shard_map/ppermute | solution.py:454
  67.7 10.0 %collective-permute-start.26 = (bf16[256,768]{1,0:T(8,128)(2,1)S(1)}, bf16[256,768]{1,0:T(8,128)(2,1)S(1)}, u32[]{:S(2)}, u32[]{:S(2)}) collective-permute-start(bf16[256,768]{1,0:T(8,128)(2,1)S(1)} %pad_maximum_fusion.c0), channel_id=1, source_target_pairs={{0,2},{1,3},{2,0},{3,1},{4,6},{5,7},{6,4},{7,5},{8,10},{9,11},{10,... | collective-permute-start | bytes 1179656 | tf_op jit(solution)/shard_map/ppermute | solution.py:454
  68.3 9.4 %collective-permute-start.16 = (bf16[256,768]{1,0:T(8,128)(2,1)S(1)}, bf16[256,768]{1,0:T(8,128)(2,1)S(1)}, u32[]{:S(2)}, u32[]{:S(2)}) collective-permute-start(bf16[256,768]{1,0:T(8,128)(2,1)S(1)} %constant_dynamic-update-slice_fusion.x0), channel_id=1, source_target_pairs={{0,1},{1,0},{2,3},{3,2},{4,5},{5,4},{6,7},{7,6},{8,9},{9,8},{10,11... | collective-permute-start | bytes 1179656 | tf_op jit(solution)/shard_map/ppermute | solution.py:454
  68.3 9.4 %collective-permute-start.25 = (bf16[256,768]{1,0:T(8,128)(2,1)S(1)}, bf16[256,768]{1,0:T(8,128)(2,1)S(1)}, u32[]{:S(2)}, u32[]{:S(2)}) collective-permute-start(bf16[256,768]{1,0:T(8,128)(2,1)S(1)} %pad_maximum_fusion.c0), channel_id=1, source_target_pairs={{0,1},{1,0},{2,3},{3,2},{4,5},{5,4},{6,7},{7,6},{8,9},{9,8},{10,11... | collective-permute-start | bytes 1179656 | tf_op jit(solution)/shard_map/ppermute | solution.py:454
  68.8 8.9 %collective-permute-start.18 = (bf16[256,768]{1,0:T(8,128)(2,1)S(1)}, bf16[256,768]{1,0:T(8,128)(2,1)S(1)}, u32[]{:S(2)}, u32[]{:S(2)}) collective-permute-start(bf16[256,768]{1,0:T(8,128)(2,1)S(1)} %collective-permute-done.17.x2), channel_id=1, source_target_pairs={{0,1},{1,0},{2,3},{3,2},{4,5},{5,4},{6,7},{7,6},{8,9},{9,8},{10,11... | collective-permute-start | bytes 1179656 | tf_op jit(solution)/shard_map/ppermute | solution.py:454
  77.7 1.7 collective-permute-start.27
  94.7 2.4 %collective-permute-start.28 = (bf16[2,8,64,384]{3,2,1,0:T(8,128)(2,1)S(1)}, bf16[2,8,64,384]{3,2,1,0:T(8,128)(2,1)S(1)}, u32[]{:S(2)}, u32[]{:S(2)}) collective-permute-start(bf16[2,8,64,384]{3,2,1,0:T(8,128)(2,1)S(1)} %get-tuple-element.83), channel_id=1, source_target_pairs={{0,1},{1,0},{2,3},{3,2},{4,5},{5,4},{6,7},{7,6},{8,9},{9,8},{10,11... | collective-permute-start | bytes 2359304 | tf_op jit(solution)/shard_map/ppermute | solution.py:454
  94.9 3.6 %collective-permute-start.33 = (bf16[2,1024,256]{2,1,0:T(8,128)(2,1)S(1)}, bf16[2,1024,256]{2,1,0:T(8,128)(2,1)S(1)}, u32[]{:S(2)}, u32[]{:S(2)}) collective-permute-start(bf16[2,1024,256]{2,1,0:T(8,128)(2,1)S(1)} %get-tuple-element.87), channel_id=1, source_target_pairs={{0,1},{1,0},{2,3},{3,2},{4,5},{5,4},{6,7},{7,6},{8,9},{9,8},{10,11... | collective-permute-start | bytes 3145736 | tf_op jit(solution)/shard_map/ppermute | solution.py:454
  97.2 12.0 %collective-permute-start.29 = (bf16[8,64,384]{2,1,0:T(8,128)(2,1)S(1)}, bf16[8,64,384]{2,1,0:T(8,128)(2,1)S(1)}, u32[]{:S(2)}, u32[]{:S(2)}) collective-permute-start(bf16[8,64,384]{2,1,0:T(8,128)(2,1)S(1)} %fusion.5), channel_id=1, source_target_pairs={{0,2},{1,3},{2,0},{3,1},{4,6},{5,7},{6,4},{7,5},{8,10},{9,11},{10,... | collective-permute-start | bytes 1179656 | tf_op jit(solution)/shard_map/ppermute | solution.py:454
  98.7 20.9 %collective-permute-start.34 = (bf16[1024,256]{1,0:T(8,128)(2,1)S(1)}, bf16[1024,256]{1,0:T(8,128)(2,1)S(1)}, u32[]{:S(2)}, u32[]{:S(2)}) collective-permute-start(bf16[1024,256]{1,0:T(8,128)(2,1)S(1)} %fusion.3), channel_id=1, source_target_pairs={{0,2},{1,3},{2,0},{3,1},{4,6},{5,7},{6,4},{7,5},{8,10},{9,11},{10,... | collective-permute-start | bytes 1572872 | tf_op jit(solution)/shard_map/ppermute | solution.py:454
  109.5 32.9 %collective-permute-start.30 = (bf16[256,384]{1,0:T(8,128)(2,1)S(1)}, bf16[256,384]{1,0:T(8,128)(2,1)S(1)}, u32[]{:S(2)}, u32[]{:S(2)}) collective-permute-start(bf16[256,384]{1,0:T(8,128)(2,1)S(1)} %pad_maximum_fusion.7), channel_id=1, source_target_pairs={{0,4},{4,0},{8,12},{12,8},{16,20},{20,16},{24,28},{28,24},{1,5},{5... | collective-permute-start | bytes 589832 | tf_op jit(solution)/shard_map/ppermute | solution.py:454
  119.9 8.6 %collective-permute-start.41 = (bf16[128,256]{1,0:T(8,128)(2,1)S(1)}, bf16[128,256]{1,0:T(8,128)(2,1)S(1)}, u32[]{:S(2)}, u32[]{:S(2)}) collective-permute-start(bf16[128,256]{1,0:T(8,128)(2,1)S(1)} %get-tuple-element.132), channel_id=1, source_target_pairs={{0,28},{4,24},{8,20},{12,16},{16,12},{20,8},{24,4},{28,0},{1,29},{... | collective-permute-start | bytes 196616 | tf_op jit(solution)/shard_map/ppermute | solution.py:454
  121.0 10.3 %collective-permute-start.40 = (bf16[128,256]{1,0:T(8,128)(2,1)S(1)}, bf16[128,256]{1,0:T(8,128)(2,1)S(1)}, u32[]{:S(2)}, u32[]{:S(2)}) collective-permute-start(bf16[128,256]{1,0:T(8,128)(2,1)S(1)} %get-tuple-element.133), channel_id=1, source_target_pairs={{0,24},{4,28},{8,16},{12,20},{16,8},{20,12},{24,0},{28,4},{1,25},{... | collective-permute-start | bytes 196616 | tf_op jit(solution)/shard_map/ppermute | solution.py:454
  126.0 10.7 %collective-permute-start.39 = (bf16[128,256]{1,0:T(8,128)(2,1)S(1)}, bf16[128,256]{1,0:T(8,128)(2,1)S(1)}, u32[]{:S(2)}, u32[]{:S(2)}) collective-permute-start(bf16[128,256]{1,0:T(8,128)(2,1)S(1)} %get-tuple-element.134), channel_id=1, source_target_pairs={{0,20},{4,16},{8,28},{12,24},{16,4},{20,0},{24,12},{28,8},{1,21},{... | collective-permute-start | bytes 196616 | tf_op jit(solution)/shard_map/ppermute | solution.py:454
  128.5 8.5 %collective-permute-start.38 = (bf16[128,256]{1,0:T(8,128)(2,1)S(1)}, bf16[128,256]{1,0:T(8,128)(2,1)S(1)}, u32[]{:S(2)}, u32[]{:S(2)}) collective-permute-start(bf16[128,256]{1,0:T(8,128)(2,1)S(1)} %get-tuple-element.135), channel_id=1, source_target_pairs={{0,16},{4,20},{8,24},{12,28},{16,0},{20,4},{24,8},{28,12},{1,17},{... | collective-permute-start | bytes 196616 | tf_op jit(solution)/shard_map/ppermute | solution.py:454
  128.5 8.5 %collective-permute-start.37 = (bf16[128,256]{1,0:T(8,128)(2,1)S(1)}, bf16[128,256]{1,0:T(8,128)(2,1)S(1)}, u32[]{:S(2)}, u32[]{:S(2)}) collective-permute-start(bf16[128,256]{1,0:T(8,128)(2,1)S(1)} %get-tuple-element.136), channel_id=1, source_target_pairs={{0,12},{4,8},{8,4},{12,0},{16,28},{20,24},{24,20},{28,16},{1,13},{... | collective-permute-start | bytes 196616 | tf_op jit(solution)/shard_map/ppermute | solution.py:454
  131.4 6.5 %collective-permute-start.36 = (bf16[128,256]{1,0:T(8,128)(2,1)S(1)}, bf16[128,256]{1,0:T(8,128)(2,1)S(1)}, u32[]{:S(2)}, u32[]{:S(2)}) collective-permute-start(bf16[128,256]{1,0:T(8,128)(2,1)S(1)} %get-tuple-element.137), channel_id=1, source_target_pairs={{0,8},{4,12},{8,0},{12,4},{16,24},{20,28},{24,16},{28,20},{1,9},{5... | collective-permute-start | bytes 196616 | tf_op jit(solution)/shard_map/ppermute | solution.py:454
  136.8 4.3 %collective-permute-start.35 = (bf16[128,256]{1,0:T(8,128)(2,1)S(1)}, bf16[128,256]{1,0:T(8,128)(2,1)S(1)}, u32[]{:S(2)}, u32[]{:S(2)}) collective-permute-start(bf16[128,256]{1,0:T(8,128)(2,1)S(1)} %get-tuple-element.138), channel_id=1, source_target_pairs={{0,4},{4,0},{8,12},{12,8},{16,20},{20,16},{24,28},{28,24},{1,5},{5... | collective-permute-start | bytes 196616 | tf_op jit(solution)/shard_map/ppermute | solution.py:454
  141.8 6.4 %collective-permute-start.43 = (bf16[512,256]{1,0:T(8,128)(2,1)S(1)}, bf16[512,256]{1,0:T(8,128)(2,1)S(1)}, u32[]{:S(2)}, u32[]{:S(2)}) collective-permute-start(bf16[512,256]{1,0:T(8,128)(2,1)S(1)} %shard_map.253.r0), channel_id=1, source_target_pairs={{0,2},{1,3},{2,0},{3,1},{4,6},{5,7},{6,4},{7,5},{8,10},{9,11},{10,... | collective-permute-start | bytes 786440 | tf_op jit(solution)/shard_map/ppermute | solution.py:454
  142.4 8.7 %collective-permute-start.31 = (bf16[256,384]{1,0:T(8,128)(2,1)S(1)}, bf16[256,384]{1,0:T(8,128)(2,1)S(1)}, u32[]{:S(2)}, u32[]{:S(2)}) collective-permute-start(bf16[256,384]{1,0:T(8,128)(2,1)S(1)} %pad_maximum_fusion.8), channel_id=1, source_target_pairs={{0,8},{4,12},{8,0},{12,4},{16,24},{20,28},{24,16},{28,20},{1,9},{5... | collective-permute-start | bytes 589832 | tf_op jit(solution)/shard_map/ppermute | solution.py:454
  142.5 8.6 %collective-permute-start.42 = (bf16[512,256]{1,0:T(8,128)(2,1)S(1)}, bf16[512,256]{1,0:T(8,128)(2,1)S(1)}, u32[]{:S(2)}, u32[]{:S(2)}) collective-permute-start(bf16[512,256]{1,0:T(8,128)(2,1)S(1)} %shard_map.253.r0), channel_id=1, source_target_pairs={{0,1},{1,0},{2,3},{3,2},{4,5},{5,4},{6,7},{7,6},{8,9},{9,8},{10,11... | collective-permute-start | bytes 786440 | tf_op jit(solution)/shard_map/ppermute | solution.py:454
  148.2 2.9 %collective-permute-start.44 = (bf16[512,256]{1,0:T(8,128)(2,1)S(1)}, bf16[512,256]{1,0:T(8,128)(2,1)S(1)}, u32[]{:S(2)}, u32[]{:S(2)}) collective-permute-start(bf16[512,256]{1,0:T(8,128)(2,1)S(1)} %collective-permute-done.43.r2), channel_id=1, source_target_pairs={{0,1},{1,0},{2,3},{3,2},{4,5},{5,4},{6,7},{7,6},{8,9},{9,8},{10,11... | collective-permute-start | bytes 786440 | tf_op jit(solution)/shard_map/ppermute | solution.py:454
  169.4 3.9 %collective-permute-start.47 = (f32[24,256]{1,0:T(8,128)S(1)}, f32[24,256]{1,0:T(8,128)S(1)}, u32[]{:S(2)}, u32[]{:S(2)}) collective-permute-start(f32[24,256]{1,0:T(8,128)S(1)} %get-tuple-element.102), channel_id=1, source_target_pairs={{0,4},{4,0},{8,12},{12,8},{16,20},{20,16},{24,28},{28,24},{1,5},{5... | collective-permute-start | bytes 73736 | tf_op jit(solution)/shard_map/ppermute | solution.py:454
  169.7 12.9 %collective-permute-start.32 = (bf16[256,384]{1,0:T(8,128)(2,1)S(1)}, bf16[256,384]{1,0:T(8,128)(2,1)S(1)}, u32[]{:S(2)}, u32[]{:S(2)}) collective-permute-start(bf16[256,384]{1,0:T(8,128)(2,1)S(1)} %pad_maximum_fusion.9), channel_id=1, source_target_pairs={{0,16},{4,20},{8,24},{12,28},{16,0},{20,4},{24,8},{28,12},{1,17},{... | collective-permute-start | bytes 589832 | tf_op jit(solution)/shard_map/ppermute | solution.py:454
  173.3 3.8 %collective-permute-start.48 = (f32[24,256]{1,0:T(8,128)S(1)}, f32[24,256]{1,0:T(8,128)S(1)}, u32[]{:S(2)}, u32[]{:S(2)}) collective-permute-start(f32[24,256]{1,0:T(8,128)S(1)} %add.107), channel_id=1, source_target_pairs={{0,8},{4,12},{8,0},{12,4},{16,24},{20,28},{24,16},{28,20},{1,9},{5... | collective-permute-start | bytes 73736 | tf_op jit(solution)/shard_map/ppermute | solution.py:454
  177.1 7.7 %collective-permute-start.49 = (f32[24,256]{1,0:T(8,128)S(1)}, f32[24,256]{1,0:T(8,128)S(1)}, u32[]{:S(2)}, u32[]{:S(2)}) collective-permute-start(f32[24,256]{1,0:T(8,128)S(1)} %add.108), channel_id=1, source_target_pairs={{0,16},{4,20},{8,24},{12,28},{16,0},{20,4},{24,8},{28,12},{1,17},{... | collective-permute-start | bytes 73736 | tf_op jit(solution)/shard_map/ppermute | solution.py:454
  184.7 8.9 %collective-permute-start.52 = (bf16[4,48,768]{2,1,0:T(8,128)(2,1)}, bf16[4,48,768]{2,1,0:T(8,128)(2,1)S(1)}, u32[]{:S(2)}, u32[]{:S(2)}) collective-permute-start(bf16[4,48,768]{2,1,0:T(8,128)(2,1)} %copy-done.21), channel_id=1, source_target_pairs={{0,8},{4,12},{8,0},{12,4},{16,24},{20,28},{24,16},{28,20},{1,9},{5... | collective-permute-start | bytes 884744 | tf_op jit(solution)/shard_map/ppermute | solution.py:454
  184.7 9.1 %collective-permute-start.58 = (bf16[4,48,768]{2,1,0:T(8,128)(2,1)}, bf16[4,48,768]{2,1,0:T(8,128)(2,1)S(1)}, u32[]{:S(2)}, u32[]{:S(2)}) collective-permute-start(bf16[4,48,768]{2,1,0:T(8,128)(2,1)} %copy-done.20), channel_id=1, source_target_pairs={{0,4},{4,0},{8,12},{12,8},{16,20},{20,16},{24,28},{28,24},{1,5},{5... | collective-permute-start | bytes 884744 | tf_op jit(solution)/shard_map/ppermute | solution.py:454
  184.8 33.4 %collective-permute-start.45 = (bf16[2,512,256]{2,1,0:T(8,128)(2,1)S(1)}, bf16[2,512,256]{2,1,0:T(8,128)(2,1)S(1)}, u32[]{:S(2)}, u32[]{:S(2)}) collective-permute-start(bf16[2,512,256]{2,1,0:T(8,128)(2,1)S(1)} %copy-done.19), channel_id=1, source_target_pairs={{0,1},{1,0},{2,3},{3,2},{4,5},{5,4},{6,7},{7,6},{8,9},{9,8},{10,11... | collective-permute-start | bytes 1572872 | tf_op jit(solution)/shard_map/ppermute | solution.py:454
  184.8 1.9 collective-permute-start.50
  186.7 39.9 %collective-permute-start.51 = (f32[8,256]{1,0:T(8,128)S(1)}, f32[8,256]{1,0:T(8,128)S(1)}, u32[]{:S(2)}, u32[]{:S(2)}) collective-permute-start(f32[8,256]{1,0:T(8,128)S(1)} %slice_add_fusion.1), channel_id=1, source_target_pairs={{0,2},{1,3},{2,0},{3,1},{4,6},{5,7},{6,4},{7,5},{8,10},{9,11},{10,... | collective-permute-start | bytes 24584 | tf_op jit(solution)/shard_map/ppermute | solution.py:454
  193.7 8.7 %collective-permute-start.53 = (bf16[2,48,768]{2,1,0:T(8,128)(2,1)S(1)}, bf16[2,48,768]{2,1,0:T(8,128)(2,1)S(1)}, u32[]{:S(2)}, u32[]{:S(2)}) collective-permute-start(bf16[2,48,768]{2,1,0:T(8,128)(2,1)S(1)} %get-tuple-element.131), channel_id=1, source_target_pairs={{0,16},{4,20},{8,24},{12,28},{16,0},{20,4},{24,8},{28,12},{1,17},{... | collective-permute-start | bytes 442376 | tf_op jit(solution)/shard_map/ppermute | solution.py:454
  193.9 9.3 %collective-permute-start.59 = (bf16[2,48,768]{2,1,0:T(8,128)(2,1)S(1)}, bf16[2,48,768]{2,1,0:T(8,128)(2,1)S(1)}, u32[]{:S(2)}, u32[]{:S(2)}) collective-permute-start(bf16[2,48,768]{2,1,0:T(8,128)(2,1)S(1)} %get-tuple-element.129), channel_id=1, source_target_pairs={{0,8},{4,12},{8,0},{12,4},{16,24},{20,28},{24,16},{28,20},{1,9},{5... | collective-permute-start | bytes 442376 | tf_op jit(solution)/shard_map/ppermute | solution.py:454
  202.4 4.4 %collective-permute-start.54 = (bf16[1,48,768]{2,1,0:T(8,128)(2,1)S(1)}, bf16[1,48,768]{2,1,0:T(8,128)(2,1)S(1)}, u32[]{:S(2)}, u32[]{:S(2)}) collective-permute-start(bf16[1,48,768]{2,1,0:T(8,128)(2,1)S(1)} %add_convert_fusion.14), channel_id=1, source_target_pairs={{0,4},{4,0},{8,12},{12,8},{16,20},{20,16},{24,28},{28,24},{1,5},{5... | collective-permute-start | bytes 221192 | tf_op jit(solution)/shard_map/ppermute | solution.py:454
  203.2 5.4 %collective-permute-start.60 = (bf16[1,48,768]{2,1,0:T(8,128)(2,1)S(1)}, bf16[1,48,768]{2,1,0:T(8,128)(2,1)S(1)}, u32[]{:S(2)}, u32[]{:S(2)}) collective-permute-start(bf16[1,48,768]{2,1,0:T(8,128)(2,1)S(1)} %add_convert_fusion.11), channel_id=1, source_target_pairs={{0,16},{4,20},{8,24},{12,28},{16,0},{20,4},{24,8},{28,12},{1,17},{... | collective-permute-start | bytes 221192 | tf_op jit(solution)/shard_map/ppermute | solution.py:454
  206.9 4.4 %collective-permute-start.55 = (bf16[1,48,768]{2,1,0:T(8,128)(2,1)S(1)}, bf16[1,48,768]{2,1,0:T(8,128)(2,1)S(1)}, u32[]{:S(2)}, u32[]{:S(2)}) collective-permute-start(bf16[1,48,768]{2,1,0:T(8,128)(2,1)S(1)} %add_convert_fusion.13), channel_id=1, source_target_pairs={{0,4},{4,0},{8,12},{12,8},{16,20},{20,16},{24,28},{28,24},{1,5},{5... | collective-permute-start | bytes 221192 | tf_op jit(solution)/shard_map/ppermute | solution.py:454
  208.6 9.5 %collective-permute-start.61 = (bf16[1,48,768]{2,1,0:T(8,128)(2,1)S(1)}, bf16[1,48,768]{2,1,0:T(8,128)(2,1)S(1)}, u32[]{:S(2)}, u32[]{:S(2)}) collective-permute-start(bf16[1,48,768]{2,1,0:T(8,128)(2,1)S(1)} %add_convert_fusion.10), channel_id=1, source_target_pairs={{0,16},{4,20},{8,24},{12,28},{16,0},{20,4},{24,8},{28,12},{1,17},{... | collective-permute-start | bytes 221192 | tf_op jit(solution)/shard_map/ppermute | solution.py:454
  211.3 9.4 %collective-permute-start.56 = (bf16[2,48,768]{2,1,0:T(8,128)(2,1)S(1)}, bf16[2,48,768]{2,1,0:T(8,128)(2,1)S(1)}, u32[]{:S(2)}, u32[]{:S(2)}) collective-permute-start(bf16[2,48,768]{2,1,0:T(8,128)(2,1)S(1)} %pad_maximum_fusion.10), channel_id=1, source_target_pairs={{0,16},{4,20},{8,24},{12,28},{16,0},{20,4},{24,8},{28,12},{1,17},{... | collective-permute-start | bytes 442376 | tf_op jit(solution)/shard_map/ppermute | solution.py:454
  218.1 6.5 %collective-permute-start.62 = (bf16[2,48,768]{2,1,0:T(8,128)(2,1)S(1)}, bf16[2,48,768]{2,1,0:T(8,128)(2,1)S(1)}, u32[]{:S(2)}, u32[]{:S(2)}) collective-permute-start(bf16[2,48,768]{2,1,0:T(8,128)(2,1)S(1)} %pad_maximum_fusion.11), channel_id=1, source_target_pairs={{0,8},{4,12},{8,0},{12,4},{16,24},{20,28},{24,16},{28,20},{1,9},{5... | collective-permute-start | bytes 442376 | tf_op jit(solution)/shard_map/ppermute | solution.py:454
  218.3 9.0 %collective-permute-start.46 = (bf16[512,256]{1,0:T(8,128)(2,1)S(1)}, bf16[512,256]{1,0:T(8,128)(2,1)S(1)}, u32[]{:S(2)}, u32[]{:S(2)}) collective-permute-start(bf16[512,256]{1,0:T(8,128)(2,1)S(1)} %get-tuple-element.126), channel_id=1, source_target_pairs={{0,2},{1,3},{2,0},{3,1},{4,6},{5,7},{6,4},{7,5},{8,10},{9,11},{10,... | collective-permute-start | bytes 786440 | tf_op jit(solution)/shard_map/ppermute | solution.py:454
  220.8 12.7 %collective-permute-start.57 = (bf16[4,48,768]{2,1,0:T(8,128)(2,1)S(1)}, bf16[4,48,768]{2,1,0:T(8,128)(2,1)S(1)}, u32[]{:S(2)}, u32[]{:S(2)}) collective-permute-start(bf16[4,48,768]{2,1,0:T(8,128)(2,1)S(1)} %pad_maximum_fusion.2.mine), channel_id=1, source_target_pairs={{0,8},{4,12},{8,0},{12,4},{16,24},{20,28},{24,16},{28,20},{1,9},{5... | collective-permute-start | bytes 884744 | tf_op jit(solution)/shard_map/ppermute | solution.py:454
  224.7 7.2 %collective-permute-start.63 = (bf16[4,48,768]{2,1,0:T(8,128)(2,1)S(1)}, bf16[4,48,768]{2,1,0:T(8,128)(2,1)S(1)}, u32[]{:S(2)}, u32[]{:S(2)}) collective-permute-start(bf16[4,48,768]{2,1,0:T(8,128)(2,1)S(1)} %pad_maximum_fusion.3.mine), channel_id=1, source_target_pairs={{0,4},{4,0},{8,12},{12,8},{16,20},{20,16},{24,28},{28,24},{1,5},{5... | collective-permute-start | bytes 884744 | tf_op jit(solution)/shard_map/ppermute | solution.py:454
  (33 other events, 312.2 us)
